TPU v7x, 512 devices: a whole 4x8x8 slice. The times are simulated.
512 devices in a mesh: replica: 16 (over y_lo, z), fsdp: 32 (over x, y_hi, core).
Axes of the slice: x: 4, y: 8 (y_hi: 4, y_lo: 2; y = y_hi * 2 + y_lo), z: 8, core: 2. Of those that a mesh axis runs over, the one named last changes fastest.
Arguments:
- acts: bfloat16 [16, 6144, 2048], P('replica', 'fsdp'), may hold values from -6 to 6
- upstream: bfloat16 [16, 6144, 2048], P('replica', 'fsdp'), may hold values from -0.076171875 to 0.076171875
- inner_params: float32 [16, 32, 256, 512], P('replica', 'fsdp'), may hold values from -6 to 6
- first_moment: float32 [16, 32, 256, 512], P('replica', 'fsdp'), may hold values from -2 to 2
- second_moment: float32 [16, 32, 256, 512], P('replica', 'fsdp'), may hold values from 0.05 to 2
- anchor: float32 [32, 256, 512], P('fsdp', 'replica'), may hold values from -6 to 6
- outer_momentum: float32 [32, 256, 512], P('fsdp', 'replica'), may hold values from -3 to 3
Outputs:
- new_params: float32 [32, 256, 512], P('fsdp')
- new_momentum: float32 [32, 256, 512], P('fsdp', 'replica')
- new_first: float32 [16, 32, 256, 512], P('replica', 'fsdp')
- new_second: float32 [16, 32, 256, 512], P('replica', 'fsdp')
All inputs are finite; a program needn't handle non-finite values.
Results may differ from a plain program's by a relative error of at most 0.0003.
Values may be sent and summed in bfloat16 or wider, within the bound.
No kernel may reach another device: no remote copies, remote signals or barrier semaphores. Data moves between devices by JAX's collectives and lax.ppermute only.
A program may use at most 64 MiB of HBM per device.

v0:
```python
import jax
import jax.numpy as jnp
from jax import lax
from jax.sharding import PartitionSpec as P

STEP = 500


beta_one = 0.9
beta_two = 0.95
adam_eps = 1e-08
decay_rate = 0.1
inner_rate = 0.02
outer_rate = 0.7
outer_mu = 0.9


def body(acts, upstream, inner_params, first_moment, second_moment, anchor, outer_momentum):
    shards = lax.axis_size("fsdp")
    members = lax.axis_size("replica")
    row_groups = shards // 4
    col_groups = 4
    tokens = acts[0]
    grads_out = upstream[0]
    count = tokens.shape[0]
    in_width = tokens.shape[1]
    out_width = grads_out.shape[1]
    block_rows = in_width // row_groups
    block_cols = out_width // col_groups
    sent_rows = jnp.broadcast_to(
        tokens.reshape(count, row_groups, 1, block_rows),
        (count, row_groups, col_groups, block_rows),
    ).reshape(count, shards * block_rows)
    sent_cols = jnp.broadcast_to(
        grads_out.reshape(count, 1, col_groups, block_cols),
        (count, row_groups, col_groups, block_cols),
    ).reshape(count, shards * block_cols)
    row_part, col_part = (
        lax.all_to_all(sent_rows, "fsdp", split_axis=1, concat_axis=0, tiled=True),
        lax.all_to_all(sent_cols, "fsdp", split_axis=1, concat_axis=0, tiled=True),
    )
    gradient = lax.dot_general(
        row_part, col_part, (((0,), (0,)), ((), ())), preferred_element_type=jnp.float32
    )
    fix_one = 1.0 - beta_one**STEP
    fix_two = 1.0 - beta_two**STEP
    params = inner_params[0, 0]
    moment_one = beta_one * first_moment[0, 0] + (1.0 - beta_one) * gradient
    moment_two = beta_two * second_moment[0, 0] + (1.0 - beta_two) * gradient * gradient
    update = (
        moment_one / fix_one / (jnp.sqrt(moment_two / fix_two) + adam_eps) + decay_rate * params
    )
    stepped = params - inner_rate * update
    slice_rows = block_rows // members
    total = lax.psum(stepped, "replica")
    anchor_block, moment_block = (
        lax.all_gather(anchor[0], "replica", axis=0, tiled=True),
        lax.all_gather(outer_momentum[0], "replica", axis=0, tiled=True),
    )
    pseudo = anchor_block - total / members
    momentum_block = outer_mu * moment_block + pseudo
    new_params = anchor_block - outer_rate * (pseudo + outer_mu * momentum_block)
    start = lax.axis_index("replica") * slice_rows
    new_momentum = lax.dynamic_slice_in_dim(momentum_block, start, slice_rows, 0)
    return (new_params[None], new_momentum[None], moment_one[None, None], moment_two[None, None])


def solution(mesh):
    in_specs = (
        P("replica", "fsdp", None),
        P("replica", "fsdp", None),
        P("replica", "fsdp", None, None),
        P("replica", "fsdp", None, None),
        P("replica", "fsdp", None, None),
        P("fsdp", "replica", None),
        P("fsdp", "replica", None),
    )
    out_specs = (
        P("fsdp", None, None),
        P("fsdp", "replica", None),
        P("replica", "fsdp", None, None),
        P("replica", "fsdp", None, None),
    )
    return jax.shard_map(body, mesh=mesh, in_specs=in_specs, out_specs=out_specs, check_vma=False)
```

profile of v0, /device:TPU:2, one launch (start us, length us, event | category | flops | bytes accessed | tf_op | source)
XLA Modules:
  0.0 398.9 jit_solution(17131471896411481602)
XLA Ops:
  7.2 1.3 copy.13
  8.5 0.2 copy.11
  8.7 2.0 broadcast_in_dim.27
  10.7 10.3 %all-to-all-start = ((bf16[192,32,256]{2,0,1:T(8,128)(2,1)}), bf16[192,32,256]{2,0,1:T(8,128)(2,1)S(1)}, u32[]{:S(2)}, u32[]{:S(2)}) async-start(bf16[192,32,256]{2,0,1:T(8,128)(2,1)} %bitcast.68), calls=%async_computation | async-start | bytes 6291456 | tf_op jit(solution)/shard_map/all_to_all | solution.py:39
  20.9 0.0 all-reduce.2.cloned.1.call-start
  21.0 3.0 broadcast_in_dim.28
  24.0 2.2 copy.12
  26.1 67.3 %all-to-all-done = bf16[192,32,256]{2,0,1:T(8,128)(2,1)S(1)} async-done(((bf16[192,32,256]{2,0,1:T(8,128)(2,1)}), bf16[192,32,256]{2,0,1:T(8,128)(2,1)S(1)}, u32[]{:S(2)}, u32[]{:S(2)}) %all-to-all-start) | async-done | bytes 3145760 | tf_op jit(solution)/shard_map/all_to_all | solution.py:39
  93.5 1.8 broadcast_in_dim.29
  95.3 0.0 copy-start
  95.3 0.0 copy-start.1
  95.3 0.0 copy-start.2
  95.3 147.1 %all_to_all.32 = bf16[192,32,512]{2,0,1:T(8,128)(2,1)S(1)} all-to-all(bf16[192,32,512]{2,0,1:T(8,128)(2,1)S(1)} %bitcast.67), channel_id=1, replica_groups=mesh['replica'=16,'fsdp'=32] {'fsdp'}, dimensions={1} | all-to-all | bytes 12582912 | tf_op jit(solution)/shard_map/all_to_all | solution.py:40
  242.4 0.0 copy-done
  242.4 0.0 copy-done.1
  242.4 0.0 copy-done.2
  242.4 0.0 copy-start.3
  242.4 0.0 copy-start.4
  242.5 3.2 fusion.13
  245.7 0.0 all-reduce.2.cloned.1.call-update
  245.7 0.0 copy-done.3
  245.7 37.1 %all-gather = f32[1,256,512]{2,1,0:T(8,128)S(1)} all-gather(f32[1,16,512]{2,1,0:T(8,128)S(1)} %copy-done.3), channel_id=2, replica_groups=mesh['replica'=16,'fsdp'=32] {'replica'}, dimensions={1}, use_global_device_ids=true | all-gather | bytes 557056 | tf_op jit(solution)/shard_map/all_gather | solution.py:57
  282.8 0.0 copy-done.4
  282.8 33.3 %all-gather.1 = f32[1,256,512]{2,1,0:T(8,128)S(1)} all-gather(f32[1,16,512]{2,1,0:T(8,128)S(1)} %copy-done.4), channel_id=3, replica_groups=mesh['replica'=16,'fsdp'=32] {'replica'}, dimensions={1}, use_global_device_ids=true | all-gather | bytes 557056 | tf_op jit(solution)/shard_map/all_gather | solution.py:58
  316.2 73.3 %all-reduce.2.cloned.1.call-done = f32[256,512]{1,0:T(8,128)} async-done(((f32[256,512]{1,0:T(8,128)}), f32[256,512]{1,0:T(8,128)}) %all-reduce.2.cloned.1.call-update) | async-done | bytes 524304 | tf_op jit(solution)/shard_map/psum | solution.py:55
  389.4 2.0 bitcast_add_fusion
  391.5 0.6 dynamic-slice_bitcast_fusion
Async XLA Ops:
  10.7 82.8 %all-to-all-start = ((bf16[192,32,256]{2,0,1:T(8,128)(2,1)}), bf16[192,32,256]{2,0,1:T(8,128)(2,1)S(1)}, u32[]{:S(2)}, u32[]{:S(2)}) async-start(bf16[192,32,256]{2,0,1:T(8,128)(2,1)} %bitcast.68), calls=%async_computation | async-start | bytes 6291456 | tf_op jit(solution)/shard_map/all_to_all | solution.py:39
  20.9 368.5 %all-reduce.2.cloned.1.call-start = ((), (), s32[]{:S(2)}) async-start(), calls=%async_computation.2 | async-start | bytes 1048576 | tf_op jit(solution)/shard_map/psum | solution.py:55
  95.3 147.1 %copy-start = (f32[1,1,256,512]{3,2,1,0:T(8,128)S(1)}, f32[1,1,256,512]{3,2,1,0:T(8,128)}, u32[]{:S(2)}) copy-start(f32[1,1,256,512]{3,2,1,0:T(8,128)} %param.11) | copy-start | bytes 1572868
  95.3 147.1 %copy-start.1 = (f32[1,1,256,512]{3,2,1,0:T(8,128)S(1)}, f32[1,1,256,512]{3,2,1,0:T(8,128)}, u32[]{:S(2)}) copy-start(f32[1,1,256,512]{3,2,1,0:T(8,128)} %param.10) | copy-start | bytes 1572868
  95.3 147.1 %copy-start.2 = (f32[1,1,256,512]{3,2,1,0:T(8,128)S(1)}, f32[1,1,256,512]{3,2,1,0:T(8,128)}, u32[]{:S(2)}) copy-start(f32[1,1,256,512]{3,2,1,0:T(8,128)} %param.9) | copy-start | bytes 1572868
  242.4 3.3 copy-start.3
  242.4 40.4 %copy-start.4 = (f32[1,16,512]{2,1,0:T(8,128)S(1)}, f32[1,16,512]{2,1,0:T(8,128)}, u32[]{:S(2)}) copy-start(f32[1,16,512]{2,1,0:T(8,128)} %param.13) | copy-start | bytes 98308
Sparse Core Ops, SparseCore 0:
  245.8 143.5 all-reduce.1
where the time goes:
time: 399 us
  blocking collectives  218 us (55%)
  waiting for transfers between devices  141 us (35%)
  between operations  14.1 us (4%)
  local copies, waits for them, and re-layouts  11.1 us (3%)
  starting transfers between devices  10.3 us (3%)
    all_to_all x1, blocking collectives, body(): lax.all_to_all(sent_cols, 'fsdp', split_axis=1, concat_axis=0, tiled=True)  147 us
    psum x1, waiting for transfers between devices, body(): total = lax.psum(stepped, 'replica')  73.3 us
    all_to_all x1, waiting for transfers between devices, body(): lax.all_to_all(sent_rows, 'fsdp', split_axis=1, concat_axis=0, tiled=True)  67.3 us
    all_gather x1, blocking collectives, body(): lax.all_gather(anchor[0], 'replica', axis=0, tiled=True)  37.1 us
    all_gather x1, blocking collectives, body(): lax.all_gather(outer_momentum[0], 'replica', axis=0, tiled=True)  33.3 us
    all_to_all x1, starting transfers between devices, body(): lax.all_to_all(sent_rows, 'fsdp', split_axis=1, concat_axis=0, tiled=True)  10.3 us
  transfers between devices with their start and end apart: 2, of which 2 were waited for; matrix products, arithmetic and copies ran while one was open for 1% of the time, Pallas kernels for 0%

commit v1 on v0

v1 whole, which is shorter than its diff:
```python
import jax
import jax.numpy as jnp
from jax import lax
from jax.sharding import PartitionSpec as P

STEP = 500


beta_one = 0.9
beta_two = 0.95
adam_eps = 1e-08
decay_rate = 0.1
inner_rate = 0.02
outer_rate = 0.7
outer_mu = 0.9

SIDE = 4
SHARDS = 32


def ring_partner(i, stage):
    return i ^ 1 if stage == 0 else i ^ 3


def place(i):
    return i // 8, i // 2 % SIDE, i % 2


def core_pairs():
    return [(i, i ^ 1) for i in range(SHARDS)]


def x_pairs(stage):
    pairs = []
    for i in range(SHARDS):
        x, y, c = place(i)
        pairs.append((i, ring_partner(x, stage ^ c) * 8 + y * 2 + c))
    return pairs


def y_pairs(stage):
    pairs = []
    for i in range(SHARDS):
        x, y, c = place(i)
        pairs.append((i, x * 8 + ring_partner(y, stage ^ c) * 2 + c))
    return pairs


def body(acts, upstream, inner_params, first_moment, second_moment, anchor, outer_momentum):
    members = lax.axis_size("replica")
    me = lax.axis_index("fsdp")
    x, y, c = me // 8, me // 2 % SIDE, me % 2
    near, far = jnp.where(c == 0, 1, 3), jnp.where(c == 0, 3, 1)
    a = acts[0]
    u = upstream[0]
    count = a.shape[0]
    rows, cols = 256, 512

    def a_for(dest):
        return lax.dynamic_slice(a, (0, dest * 2 * rows), (count, 2 * rows))

    def u_for(core):
        return jnp.concatenate(
            [lax.dynamic_slice(u, (0, (k * 2 + core) * cols), (count, cols)) for k in range(2)], 1
        )

    a_sent = jnp.concatenate([a_for(x ^ near), a_for(x ^ 2)], 0)
    a_one = lax.ppermute(a_sent, "fsdp", x_pairs(0))
    u_other = lax.ppermute(u_for(1 - c), "fsdp", core_pairs())
    u_chip = jnp.concatenate([u_for(c), u_other], 0)
    u_one = lax.ppermute(u_chip, "fsdp", x_pairs(0))
    a_two = lax.ppermute(
        jnp.concatenate([a_for(x ^ far), a_one[count:]], 0), "fsdp", x_pairs(1)
    )
    u_half = jnp.concatenate([u_chip, u_one], 0)
    u_two = lax.ppermute(u_half, "fsdp", x_pairs(1))
    a_core = jnp.concatenate([a_for(x), a_one[:count], a_two], 0)
    a_other = lax.ppermute(a_core, "fsdp", core_pairs())
    order = [a_core[i * count : (i + 1) * count] for i in range(4)]
    other = [a_other[i * count : (i + 1) * count] for i in (0, 2, 1, 3)]
    a_all = jnp.concatenate([t for pair in zip(order, other) for t in pair], 0)
    u_all = jnp.concatenate([u_half, u_two], 0)

    def part(dest):
        left = lax.dynamic_slice(a_all, (0, dest // 2 * rows), (8 * count, rows))
        right = lax.dynamic_slice(u_all, (0, dest % 2 * cols), (8 * count, cols))
        return lax.dot_general(
            left, right, (((0,), (0,)), ((), ())), preferred_element_type=jnp.float32
        )

    g_sent = jnp.stack([part(y ^ far ^ near), part(y ^ near)])
    g_one = lax.ppermute(g_sent, "fsdp", y_pairs(0))
    g_two = lax.ppermute(part(y ^ far) + g_one[0], "fsdp", y_pairs(1))
    gradient = part(y) + g_one[1] + g_two

    fix_one = 1.0 - beta_one**STEP
    fix_two = 1.0 - beta_two**STEP
    params = inner_params[0, 0]
    moment_one = beta_one * first_moment[0, 0] + (1.0 - beta_one) * gradient
    moment_two = beta_two * second_moment[0, 0] + (1.0 - beta_two) * gradient * gradient
    update = (
        moment_one / fix_one / (jnp.sqrt(moment_two / fix_two) + adam_eps) + decay_rate * params
    )
    stepped = params - inner_rate * update

    slice_rows = rows // members
    parts = lax.all_to_all(
        stepped.reshape(members, slice_rows, cols), "replica", split_axis=0, concat_axis=0, tiled=True
    )
    pseudo = anchor[0] - jnp.sum(parts, axis=0) / members
    new_momentum = outer_mu * outer_momentum[0] + pseudo
    new_params = anchor[0] - outer_rate * (pseudo + outer_mu * new_momentum)
    gathered = lax.all_to_all(
        jnp.broadcast_to(new_params[None], (members, slice_rows, cols)),
        "replica",
        split_axis=0,
        concat_axis=0,
        tiled=True,
    ).reshape(rows, cols)
    return (gathered[None], new_momentum[None], moment_one[None, None], moment_two[None, None])


def solution(mesh):
    in_specs = (
        P("replica", "fsdp", None),
        P("replica", "fsdp", None),
        P("replica", "fsdp", None, None),
        P("replica", "fsdp", None, None),
        P("replica", "fsdp", None, None),
        P("fsdp", "replica", None),
        P("fsdp", "replica", None),
    )
    out_specs = (
        P("fsdp", None, None),
        P("fsdp", "replica", None),
        P("replica", "fsdp", None, None),
        P("replica", "fsdp", None, None),
    )
    return jax.shard_map(body, mesh=mesh, in_specs=in_specs, out_specs=out_specs, check_vma=False)
```

time: 399 us -> 161 us (0.40)
  the two profiles are of different devices: /device:TPU:2 before, /device:TPU:110 now
where the time goes in v1:
time: 161 us; the launch traced here: 160 us
  waiting for transfers between devices  60.3 us (37%)
  blocking collectives  50.1 us (31%)
  starting transfers between devices  24.9 us (15%)
  local copies, waits for them, and re-layouts  9.73 us (6%)
  matrix products  7.72 us (5%)
  other arithmetic  6.3 us (4%)
    all_to_all x1, blocking collectives, body(): lax.all_to_all(stepped.reshape(members, slice_rows, cols), 'replica', spl...  29.6 us
    ppermute x1, waiting for transfers between devices, body(): g_one = lax.ppermute(g_sent, 'fsdp', y_pairs(0))  23.8 us
    all_to_all x1, blocking collectives, body(): lax.all_to_all(jnp.broadcast_to(new_params[None], (members, slice_rows, c...  20.5 us
    ppermute x1, waiting for transfers between devices, body(): u_two = lax.ppermute(u_half, 'fsdp', x_pairs(1))  13.7 us
    ppermute x1, waiting for transfers between devices, body(): g_two = lax.ppermute(part(y ^ far) + g_one[0], 'fsdp', y_pairs(1))  10.6 us
    dot_general x4, matrix products, part(): lax.dot_general(left, right, (((0,), (0,)), ((), ())), preferred_element_...  7.72 us
    unnamed x36, local copies, waits for them, and re-layouts  6.67 us
    ppermute x1, waiting for transfers between devices, body(): lax.ppermute(jnp.concatenate([a_for(x ^ far), a_one[count:]], 0), 'fsdp',...  6.27 us
  transfers between devices with their start and end apart: 8, of which 6 were waited for; matrix products, arithmetic and copies ran while one was open for 5% of the time, Pallas kernels for 0%

profile of v1, /device:TPU:110, one launch (start us, length us, event | category | flops | bytes accessed | tf_op | source)
XLA Modules:
  0.0 160.3 jit_solution(16219939521017286918)
XLA Ops:
  0.6 0.0 copy-start.10
  0.7 1.2 dynamic-slice_bitcast_fusion.4
  2.0 2.7 %collective-permute-start = (bf16[384,512]{1,0:T(8,128)(2,1)S(1)}, bf16[384,512]{1,0:T(8,128)(2,1)S(1)}, u32[]{:S(2)}, u32[]{:S(2)}) collective-permute-start(bf16[384,512]{1,0:T(8,128)(2,1)S(1)} %pad_maximum_fusion.5), channel_id=1, source_target_pairs={{0,8},{1,25},{2,10},{3,27},{4,12},{5,29},{6,14},{7,31},{8,0},{9,17... | collective-permute-start | bytes 1179656 | tf_op jit(solution)/shard_map/ppermute | solution.py:68
  4.7 0.0 copy-done.10
  4.7 0.1 dynamic-slice_bitcast_fusion.3
  4.8 0.0 copy-start
  4.8 0.0 copy-start.2
  4.9 1.9 %collective-permute-start.3 = (bf16[192,1024]{1,0:T(8,128)(2,1)S(1)}, bf16[192,1024]{1,0:T(8,128)(2,1)S(1)}, u32[]{:S(2)}, u32[]{:S(2)}) collective-permute-start(bf16[192,1024]{1,0:T(8,128)(2,1)S(1)} %pad_maximum_fusion.7), channel_id=1, source_target_pairs={{0,1},{1,0},{2,3},{3,2},{4,5},{5,4},{6,7},{7,6},{8,9},{9,8},{10,11... | collective-permute-start | bytes 1179656 | tf_op jit(solution)/shard_map/ppermute | solution.py:69
  6.8 4.8 %collective-permute-done = bf16[384,512]{1,0:T(8,128)(2,1)S(1)} collective-permute-done((bf16[384,512]{1,0:T(8,128)(2,1)S(1)}, bf16[384,512]{1,0:T(8,128)(2,1)S(1)}, u32[]{:S(2)}, u32[]{:S(2)}) %collective-permute-start) | collective-permute-done | bytes 393248 | tf_op jit(solution)/shard_map/ppermute | solution.py:68
  11.6 0.0 copy-start.8
  11.6 0.8 fusion.36
  12.4 0.8 pad_maximum_fusion.6
  13.2 2.4 %collective-permute-start.1 = (bf16[384,512]{1,0:T(8,128)(2,1)}, bf16[384,512]{1,0:T(8,128)(2,1)S(1)}, u32[]{:S(2)}, u32[]{:S(2)}) collective-permute-start(bf16[384,512]{1,0:T(8,128)(2,1)} %pad_maximum_fusion.6), channel_id=1, source_target_pairs={{0,24},{1,9},{2,26},{3,11},{4,28},{5,13},{6,30},{7,15},{8,16},{9,1... | collective-permute-start | bytes 1179656 | tf_op jit(solution)/shard_map/ppermute | solution.py:72
  15.6 0.0 copy-start.11
  15.6 0.0 collective-permute-done.3
  15.6 0.0 copy-done.8
  15.6 0.9 pad_maximum_fusion.4
  16.5 2.8 %collective-permute-start.4 = (bf16[384,1024]{1,0:T(8,128)(2,1)}, bf16[384,1024]{1,0:T(8,128)(2,1)S(1)}, u32[]{:S(2)}, u32[]{:S(2)}) collective-permute-start(bf16[384,1024]{1,0:T(8,128)(2,1)} %pad_maximum_fusion.4), channel_id=1, source_target_pairs={{0,8},{1,25},{2,10},{3,27},{4,12},{5,29},{6,14},{7,31},{8,0},{9,17... | collective-permute-start | bytes 2359304 | tf_op jit(solution)/shard_map/ppermute | solution.py:71
  19.3 1.0 constant_dynamic-update-slice_fusion.1
  20.3 6.3 %collective-permute-done.1 = bf16[384,512]{1,0:T(8,128)(2,1)S(1)} collective-permute-done((bf16[384,512]{1,0:T(8,128)(2,1)}, bf16[384,512]{1,0:T(8,128)(2,1)S(1)}, u32[]{:S(2)}, u32[]{:S(2)}) %collective-permute-start.1) | collective-permute-done | bytes 393248 | tf_op jit(solution)/shard_map/ppermute | solution.py:72
  26.6 0.0 copy-done.11
  26.6 1.0 pad_maximum_fusion.3
  27.5 1.9 %collective-permute-start.2 = (bf16[768,512]{1,0:T(8,128)(2,1)}, bf16[768,512]{1,0:T(8,128)(2,1)}, u32[]{:S(2)}, u32[]{:S(2)}) collective-permute-start(bf16[768,512]{1,0:T(8,128)(2,1)} %pad_maximum_fusion.3), channel_id=1, source_target_pairs={{0,1},{1,0},{2,3},{3,2},{4,5},{5,4},{6,7},{7,6},{8,9},{9,8},{10,11... | collective-permute-start | bytes 2359304 | tf_op jit(solution)/shard_map/ppermute | solution.py:78
  29.6 0.0 copy-start.9
  29.6 1.0 collective-permute-done.4
  30.6 0.0 copy-done
  30.6 0.0 copy-done.2
  30.6 0.0 copy-start.4
  30.6 0.1 pad_maximum_fusion.1
  30.7 0.8 copy-done.4
  31.5 0.0 copy-start.1
  31.5 0.0 copy-start.3
  31.5 4.8 %collective-permute-start.5 = (bf16[768,1024]{1,0:T(8,128)(2,1)S(1)}, bf16[768,1024]{1,0:T(8,128)(2,1)S(1)}, u32[]{:S(2)}, u32[]{:S(2)}) collective-permute-start(bf16[768,1024]{1,0:T(8,128)(2,1)S(1)} %pad_maximum_fusion.1), channel_id=1, source_target_pairs={{0,24},{1,9},{2,26},{3,11},{4,28},{5,13},{6,30},{7,15},{8,16},{9,1... | collective-permute-start | bytes 4718600 | tf_op jit(solution)/shard_map/ppermute | solution.py:76
  36.3 0.0 copy-start.5
  36.3 0.0 collective-permute-done.2
  36.3 1.0 slice_dynamic-update-slice_fusion.5
  37.3 0.0 copy-done.9
  37.4 0.9 slice_dynamic-update-slice_fusion.4
  38.3 0.9 slice_dynamic-update-slice_fusion.2
  39.3 0.9 slice_dynamic-update-slice_fusion
  40.3 0.0 copy-start.6
  40.3 1.2 copy-done.6
  41.4 13.7 %collective-permute-done.5 = bf16[768,1024]{1,0:T(8,128)(2,1)S(1)} collective-permute-done((bf16[768,1024]{1,0:T(8,128)(2,1)S(1)}, bf16[768,1024]{1,0:T(8,128)(2,1)S(1)}, u32[]{:S(2)}, u32[]{:S(2)}) %collective-permute-start.5) | collective-permute-done | bytes 1572896 | tf_op jit(solution)/shard_map/ppermute | solution.py:76
  55.1 0.0 copy-done.1
  55.2 0.0 copy-done.3
  55.2 0.0 copy-done.5
  55.2 0.0 copy-start.7
  55.2 1.7 %pad_maximum_fusion = bf16[1536,1024]{1,0:T(8,128)(2,1)S(1)} fusion(bf16[768,1024]{1,0:T(8,128)(2,1)S(1)} %collective-permute-done.5, bf16[384,1024]{1,0:T(8,128)(2,1)S(1)} %copy-done.5, bf16[192,1024]{1,0:T(8,128)(2,1)S(1)} %collective-permute-done.3, bf16[192,512]{1,0:T(8,128)(2,1)S(1)} %copy-done.3, bf16[192,512]{1,0:T(8,128)(2,1)S(1)} %copy-done.1), kind=kLoop, calls=%fused_computation | loop fusion | flops 15728640 | bytes 6291456 | tf_op jit(solution)/shard_map/concatenate | solution.py:82
  56.9 0.0 copy-done.7
  56.9 0.6 fusion.8
  57.5 0.6 fusion.11
  58.1 1.1 pad_maximum_fusion.2
  59.2 2.7 %collective-permute-start.6 = (f32[2,256,512]{2,1,0:T(8,128)}, f32[2,256,512]{2,1,0:T(8,128)}, u32[]{:S(2)}, u32[]{:S(2)}) collective-permute-start(f32[2,256,512]{2,1,0:T(8,128)} %pad_maximum_fusion.2), channel_id=1, source_target_pairs={{0,2},{1,7},{2,0},{3,5},{4,6},{5,3},{6,4},{7,1},{8,10},{9,15},{10,... | collective-permute-start | bytes 3145736 | tf_op jit(solution)/shard_map/ppermute | solution.py:92
  61.9 23.8 %collective-permute-done.6 = f32[2,256,512]{2,1,0:T(8,128)} collective-permute-done((f32[2,256,512]{2,1,0:T(8,128)}, f32[2,256,512]{2,1,0:T(8,128)}, u32[]{:S(2)}, u32[]{:S(2)}) %collective-permute-start.6) | collective-permute-done | bytes 1048608 | tf_op jit(solution)/shard_map/ppermute | solution.py:92
  85.7 2.7 %fusion.20 = f32[256,512]{1,0:T(8,128)} fusion(bf16[1536,1024]{1,0:T(8,128)(2,1)S(1)} %pad_maximum_fusion, s32[]{:T(128)S(6)} %select_n.130, bf16[1536,512]{1,0:T(8,128)(2,1)} %copy-done.6, s32[]{:T(128)S(6)} %select_n.128, f32[2,256,512]{2,1,0:T(8,128)} %collective-permute-done.6), kind=kOutput, calls=%fused_computation.14 | convolution fusion | flops 402784256 | bytes 3407880 | tf_op jit(solution)/shard_map/dot_general | solution.py:87
  88.4 5.7 %collective-permute-start.7 = (f32[256,512]{1,0:T(8,128)}, f32[256,512]{1,0:T(8,128)}, u32[]{:S(2)}, u32[]{:S(2)}) collective-permute-start(f32[256,512]{1,0:T(8,128)} %fusion.20), channel_id=1, source_target_pairs={{0,6},{1,3},{2,4},{3,1},{4,2},{5,7},{6,0},{7,5},{8,14},{9,11},{10,... | collective-permute-start | bytes 1572872 | tf_op jit(solution)/shard_map/ppermute | solution.py:93
  94.2 10.6 %collective-permute-done.7 = f32[256,512]{1,0:T(8,128)} collective-permute-done((f32[256,512]{1,0:T(8,128)}, f32[256,512]{1,0:T(8,128)}, u32[]{:S(2)}, u32[]{:S(2)}) %collective-permute-start.7) | collective-permute-done | bytes 524320 | tf_op jit(solution)/shard_map/ppermute | solution.py:93
  104.8 3.8 %fusion.31 = (f32[1,1,256,512]{3,2,1,0:T(8,128)}, f32[256,512]{1,0:T(8,128)S(1)}, f32[1,1,256,512]{3,2,1,0:T(8,128)}) fusion(f32[1,1,256,512]{3,2,1,0:T(8,128)} %param.11, f32[1,1,256,512]{3,2,1,0:T(8,128)} %param.10, f32[1,1,256,512]{3,2,1,0:T(8,128)} %param.9, f32[256,512]{1,0:T(8,128)} %collective-permute-done.7, ...), kind=kOutput, calls=%fused_computation.49 | convolution fusion | flops 404619264 | bytes 6553608 | tf_op jit(solution)/shard_map/dot_general | solution.py:87
  108.6 29.6 %all_to_all.10 = f32[16,16,512]{2,1,0:T(8,128)S(1)} all-to-all(f32[16,16,512]{2,1,0:T(8,128)S(1)} %bitcast.68), channel_id=1, replica_groups=mesh['replica'=16,'fsdp'=32] {'replica'}, dimensions={0} | all-to-all | bytes 1048576 | tf_op jit(solution)/shard_map/all_to_all | solution.py:107
  138.3 0.0 copy-done.12
  138.3 0.0 copy-done.13
  138.3 0.6 subtract_bitcast_fusion
  139.0 20.5 %all_to_all.11 = f32[16,16,512]{2,1,0:T(8,128)S(1)} all-to-all(f32[16,16,512]{2,1,0:T(8,128)S(1)} %broadcast_in_dim.16), channel_id=1, replica_groups=mesh['replica'=16,'fsdp'=32] {'replica'}, dimensions={0} | all-to-all | bytes 1048576 | tf_op jit(solution)/shard_map/all_to_all | solution.py:113
  159.5 0.8 copy.19
  (9 shorter events, 0.2 us)
Async XLA Ops:
  0.6 4.1 %copy-start.10 = (bf16[1,192,2048]{2,1,0:T(8,128)(2,1)S(1)}, bf16[1,192,2048]{2,1,0:T(8,128)(2,1)}, u32[]{:S(2)}) copy-start(bf16[1,192,2048]{2,1,0:T(8,128)(2,1)} %param.8) | copy-start | bytes 2359300
  2.0 9.7 %collective-permute-start = (bf16[384,512]{1,0:T(8,128)(2,1)S(1)}, bf16[384,512]{1,0:T(8,128)(2,1)S(1)}, u32[]{:S(2)}, u32[]{:S(2)}) collective-permute-start(bf16[384,512]{1,0:T(8,128)(2,1)S(1)} %pad_maximum_fusion.5), channel_id=1, source_target_pairs={{0,8},{1,25},{2,10},{3,27},{4,12},{5,29},{6,14},{7,31},{8,0},{9,17... | collective-permute-start | bytes 1179656 | tf_op jit(solution)/shard_map/ppermute | solution.py:68
  4.8 25.8 %copy-start = (bf16[192,512]{1,0:T(8,128)(2,1)}, bf16[192,512]{1,0:T(8,128)(2,1)S(1)}, u32[]{:S(2)}) copy-start(bf16[192,512]{1,0:T(8,128)(2,1)S(1)} %get-tuple-element.14) | copy-start | bytes 589828
  4.8 25.8 %copy-start.2 = (bf16[192,512]{1,0:T(8,128)(2,1)}, bf16[192,512]{1,0:T(8,128)(2,1)S(1)}, u32[]{:S(2)}) copy-start(bf16[192,512]{1,0:T(8,128)(2,1)S(1)} %get-tuple-element.15) | copy-start | bytes 589828
  4.9 10.7 %collective-permute-start.3 = (bf16[192,1024]{1,0:T(8,128)(2,1)S(1)}, bf16[192,1024]{1,0:T(8,128)(2,1)S(1)}, u32[]{:S(2)}, u32[]{:S(2)}) collective-permute-start(bf16[192,1024]{1,0:T(8,128)(2,1)S(1)} %pad_maximum_fusion.7), channel_id=1, source_target_pairs={{0,1},{1,0},{2,3},{3,2},{4,5},{5,4},{6,7},{7,6},{8,9},{9,8},{10,11... | collective-permute-start | bytes 1179656 | tf_op jit(solution)/shard_map/ppermute | solution.py:69
  11.6 3.9 %copy-start.8 = (bf16[384,512]{1,0:T(8,128)(2,1)}, bf16[384,512]{1,0:T(8,128)(2,1)S(1)}, u32[]{:S(2)}) copy-start(bf16[384,512]{1,0:T(8,128)(2,1)S(1)} %collective-permute-done) | copy-start | bytes 1179652
  13.2 13.4 %collective-permute-start.1 = (bf16[384,512]{1,0:T(8,128)(2,1)}, bf16[384,512]{1,0:T(8,128)(2,1)S(1)}, u32[]{:S(2)}, u32[]{:S(2)}) collective-permute-start(bf16[384,512]{1,0:T(8,128)(2,1)} %pad_maximum_fusion.6), channel_id=1, source_target_pairs={{0,24},{1,9},{2,26},{3,11},{4,28},{5,13},{6,30},{7,15},{8,16},{9,1... | collective-permute-start | bytes 1179656 | tf_op jit(solution)/shard_map/ppermute | solution.py:72
  15.6 11.0 %copy-start.11 = (bf16[192,512]{1,0:T(8,128)(2,1)S(1)}, bf16[192,512]{1,0:T(8,128)(2,1)}, u32[]{:S(2)}) copy-start(bf16[192,512]{1,0:T(8,128)(2,1)} %get-tuple-element.18) | copy-start | bytes 589828
  16.5 14.1 %collective-permute-start.4 = (bf16[384,1024]{1,0:T(8,128)(2,1)}, bf16[384,1024]{1,0:T(8,128)(2,1)S(1)}, u32[]{:S(2)}, u32[]{:S(2)}) collective-permute-start(bf16[384,1024]{1,0:T(8,128)(2,1)} %pad_maximum_fusion.4), channel_id=1, source_target_pairs={{0,8},{1,25},{2,10},{3,27},{4,12},{5,29},{6,14},{7,31},{8,0},{9,17... | collective-permute-start | bytes 2359304 | tf_op jit(solution)/shard_map/ppermute | solution.py:71
  27.5 8.8 %collective-permute-start.2 = (bf16[768,512]{1,0:T(8,128)(2,1)}, bf16[768,512]{1,0:T(8,128)(2,1)}, u32[]{:S(2)}, u32[]{:S(2)}) collective-permute-start(bf16[768,512]{1,0:T(8,128)(2,1)} %pad_maximum_fusion.3), channel_id=1, source_target_pairs={{0,1},{1,0},{2,3},{3,2},{4,5},{5,4},{6,7},{7,6},{8,9},{9,8},{10,11... | collective-permute-start | bytes 2359304 | tf_op jit(solution)/shard_map/ppermute | solution.py:78
  29.6 7.8 %copy-start.9 = (bf16[384,512]{1,0:T(8,128)(2,1)S(1)}, bf16[384,512]{1,0:T(8,128)(2,1)}, u32[]{:S(2)}) copy-start(bf16[384,512]{1,0:T(8,128)(2,1)} %copy-done.8) | copy-start | bytes 1179652
  30.6 0.9 copy-start.4
  31.5 23.6 %copy-start.1 = (bf16[192,512]{1,0:T(8,128)(2,1)S(1)}, bf16[192,512]{1,0:T(8,128)(2,1)}, u32[]{:S(2)}) copy-start(bf16[192,512]{1,0:T(8,128)(2,1)} %copy-done) | copy-start | bytes 589828
  31.5 23.6 %copy-start.3 = (bf16[192,512]{1,0:T(8,128)(2,1)S(1)}, bf16[192,512]{1,0:T(8,128)(2,1)}, u32[]{:S(2)}) copy-start(bf16[192,512]{1,0:T(8,128)(2,1)} %copy-done.2) | copy-start | bytes 589828
  31.5 23.6 %collective-permute-start.5 = (bf16[768,1024]{1,0:T(8,128)(2,1)S(1)}, bf16[768,1024]{1,0:T(8,128)(2,1)S(1)}, u32[]{:S(2)}, u32[]{:S(2)}) collective-permute-start(bf16[768,1024]{1,0:T(8,128)(2,1)S(1)} %pad_maximum_fusion.1), channel_id=1, source_target_pairs={{0,24},{1,9},{2,26},{3,11},{4,28},{5,13},{6,30},{7,15},{8,16},{9,1... | collective-permute-start | bytes 4718600 | tf_op jit(solution)/shard_map/ppermute | solution.py:76
  36.3 18.9 %copy-start.5 = (bf16[384,1024]{1,0:T(8,128)(2,1)S(1)}, bf16[384,1024]{1,0:T(8,128)(2,1)}, u32[]{:S(2)}) copy-start(bf16[384,1024]{1,0:T(8,128)(2,1)} %copy-done.4) | copy-start | bytes 2359300
  40.3 1.2 copy-start.6
  55.2 1.7 %copy-start.7 = (bf16[1536,512]{1,0:T(8,128)(2,1)S(1)}, bf16[1536,512]{1,0:T(8,128)(2,1)}, u32[]{:S(2)}) copy-start(bf16[1536,512]{1,0:T(8,128)(2,1)} %copy-done.6) | copy-start | bytes 4718596
  59.2 26.5 %collective-permute-start.6 = (f32[2,256,512]{2,1,0:T(8,128)}, f32[2,256,512]{2,1,0:T(8,128)}, u32[]{:S(2)}, u32[]{:S(2)}) collective-permute-start(f32[2,256,512]{2,1,0:T(8,128)} %pad_maximum_fusion.2), channel_id=1, source_target_pairs={{0,2},{1,7},{2,0},{3,5},{4,6},{5,3},{6,4},{7,1},{8,10},{9,15},{10,... | collective-permute-start | bytes 3145736 | tf_op jit(solution)/shard_map/ppermute | solution.py:92
  88.4 16.4 %collective-permute-start.7 = (f32[256,512]{1,0:T(8,128)}, f32[256,512]{1,0:T(8,128)}, u32[]{:S(2)}, u32[]{:S(2)}) collective-permute-start(f32[256,512]{1,0:T(8,128)} %fusion.20), channel_id=1, source_target_pairs={{0,6},{1,3},{2,4},{3,1},{4,2},{5,7},{6,0},{7,5},{8,14},{9,11},{10,... | collective-permute-start | bytes 1572872 | tf_op jit(solution)/shard_map/ppermute | solution.py:93
  108.6 29.6 %copy-start.12 = (f32[1,16,512]{2,1,0:T(8,128)S(1)}, f32[1,16,512]{2,1,0:T(8,128)}, u32[]{:S(2)}) copy-start(f32[1,16,512]{2,1,0:T(8,128)} %param.12) | copy-start | bytes 98308
  108.6 29.7 %copy-start.13 = (f32[1,16,512]{2,1,0:T(8,128)S(1)}, f32[1,16,512]{2,1,0:T(8,128)}, u32[]{:S(2)}) copy-start(f32[1,16,512]{2,1,0:T(8,128)} %param.13) | copy-start | bytes 98308

commit v2 on v1

--- a/solution.py
+++ b/solution.py
@@ -49,7 +49,7 @@
 def body(acts, upstream, inner_params, first_moment, second_moment, anchor, outer_momentum):
     members = lax.axis_size("replica")
     me = lax.axis_index("fsdp")
-    x, y, c = me // 8, me // 2 % SIDE, me % 2
+    x, y, c = me >> 3, (me >> 1) & 3, me & 1
     near, far = jnp.where(c == 0, 1, 3), jnp.where(c == 0, 3, 1)
     a = acts[0]
     u = upstream[0]
@@ -60,30 +60,32 @@
         return lax.dynamic_slice(a, (0, dest * 2 * rows), (count, 2 * rows))
 
     def u_for(core):
-        return jnp.concatenate(
-            [lax.dynamic_slice(u, (0, (k * 2 + core) * cols), (count, cols)) for k in range(2)], 1
-        )
+        return [lax.dynamic_slice(u, (0, (k * 2 + core) * cols), (count, cols)) for k in range(2)]
 
-    a_sent = jnp.concatenate([a_for(x ^ near), a_for(x ^ 2)], 0)
-    a_one = lax.ppermute(a_sent, "fsdp", x_pairs(0))
-    u_other = lax.ppermute(u_for(1 - c), "fsdp", core_pairs())
-    u_chip = jnp.concatenate([u_for(c), u_other], 0)
-    u_one = lax.ppermute(u_chip, "fsdp", x_pairs(0))
-    a_two = lax.ppermute(
-        jnp.concatenate([a_for(x ^ far), a_one[count:]], 0), "fsdp", x_pairs(1)
+    def pieces(t):
+        return [t[i * count : (i + 1) * count] for i in range(t.shape[0] // count)]
+
+    u_own = u_for(c)
+    u_swap = lax.ppermute(jnp.concatenate(u_for(1 - c), 0), "fsdp", core_pairs())
+    one = lax.ppermute(
+        jnp.concatenate([a_for(x ^ near), *u_own, a_for(x ^ 2)], 0), "fsdp", x_pairs(0)
     )
-    u_half = jnp.concatenate([u_chip, u_one], 0)
-    u_two = lax.ppermute(u_half, "fsdp", x_pairs(1))
-    a_core = jnp.concatenate([a_for(x), a_one[:count], a_two], 0)
+    two = lax.ppermute(jnp.concatenate([a_for(x ^ far), *u_own], 0), "fsdp", x_pairs(1))
+    one_swap = lax.ppermute(u_swap, "fsdp", x_pairs(0))
+    two_swap = lax.ppermute(u_swap, "fsdp", x_pairs(1))
+    three = lax.ppermute(one[count:], "fsdp", x_pairs(1))
+    three_swap = lax.ppermute(one_swap, "fsdp", x_pairs(1))
+    a_core = jnp.concatenate([a_for(x), one[:count], two[:count], three[2 * count :]], 0)
     a_other = lax.ppermute(a_core, "fsdp", core_pairs())
-    order = [a_core[i * count : (i + 1) * count] for i in range(4)]
-    other = [a_other[i * count : (i + 1) * count] for i in (0, 2, 1, 3)]
-    a_all = jnp.concatenate([t for pair in zip(order, other) for t in pair], 0)
-    u_all = jnp.concatenate([u_half, u_two], 0)
+    other = pieces(a_other)
+    a_all = jnp.concatenate([a_core, other[0], other[2], other[1], other[3]], 0)
+    u_core = [u_own, pieces(one)[1:3], pieces(two)[1:], pieces(three)[:2]]
+    u_rest = [pieces(u_swap), pieces(one_swap), pieces(two_swap), pieces(three_swap)]
+    u_all = jnp.concatenate([jnp.concatenate([p[k] for p in u_core + u_rest], 0) for k in range(2)], 1)
 
     def part(dest):
-        left = lax.dynamic_slice(a_all, (0, dest // 2 * rows), (8 * count, rows))
-        right = lax.dynamic_slice(u_all, (0, dest % 2 * cols), (8 * count, cols))
+        left = lax.dynamic_slice(a_all, (0, (dest >> 1) * rows), (8 * count, rows))
+        right = lax.dynamic_slice(u_all, (0, (dest & 1) * cols), (8 * count, cols))
         return lax.dot_general(
             left, right, (((0,), (0,)), ((), ())), preferred_element_type=jnp.float32
         )

time: 161 us -> 149 us (0.925)
  the two profiles are of different devices: /device:TPU:110 before, /device:TPU:104 now
where the time goes in v2:
time: 149 us; the launch traced here: 148 us
  waiting for transfers between devices  51.8 us (35%)
  blocking collectives  44.4 us (30%)
  starting transfers between devices  30.8 us (21%)
  local copies, waits for them, and re-layouts  9.55 us (6%)
  matrix products  9.48 us (6%)
    ppermute x1, waiting for transfers between devices, body(): g_one = lax.ppermute(g_sent, 'fsdp', y_pairs(0))  26.2 us
    all_to_all x1, blocking collectives, body(): lax.all_to_all(stepped.reshape(members, slice_rows, cols), 'replica', spl...  23.5 us
    all_to_all x1, blocking collectives, body(): lax.all_to_all(jnp.broadcast_to(new_params[None], (members, slice_rows, c...  21 us
    ppermute x1, waiting for transfers between devices, body(): g_two = lax.ppermute(part(y ^ far) + g_one[0], 'fsdp', y_pairs(1))  16.1 us
    dot_general x4, matrix products, part(): lax.dot_general(left, right, (((0,), (0,)), ((), ())), preferred_element_...  9.48 us
    unnamed x29, local copies, waits for them, and re-layouts  6.12 us
    ppermute x1, waiting for transfers between devices, body(): three = lax.ppermute(one[count:], 'fsdp', x_pairs(1))  4.63 us
    ppermute x1, starting transfers between devices, body(): lax.ppermute(jnp.concatenate([a_for(x ^ far), *u_own], 0), 'fsdp', x_pair...  4.53 us
  transfers between devices with their start and end apart: 10, of which 5 were waited for; matrix products, arithmetic and copies ran while one was open for 4% of the time, Pallas kernels for 0%

profile of v2, /device:TPU:104, one launch (start us, length us, event | category | flops | bytes accessed | tf_op | source)
XLA Modules:
  0.0 148.0 jit_solution(8893408274705950937)
XLA Ops:
  0.6 0.0 copy-start
  0.7 1.9 %constant_dynamic-update-slice_fusion.5 = (bf16[1536,512]{1,0:T(8,128)(2,1)}, bf16[192,512]{1,0:T(8,128)(2,1)S(1)}, bf16[1536,512]{1,0:T(8,128)(2,1)}, bf16[192,512]{1,0:T(8,128)(2,1)S(1)}) fusion(bf16[1,192,2048]{2,1,0:T(8,128)(2,1)} %param.8, s32[]{:T(128)S(6)} %select_n.59, s32[]{:T(128)S(6)} %select_n.58), kind=kLoop, calls=%fused_computation.72 | loop fusion | bytes 1179656
  2.6 0.0 copy-done
  2.7 0.1 pad_maximum_fusion.1
  2.7 3.4 %collective-permute-start = (bf16[768,512]{1,0:T(8,128)(2,1)S(1)}, bf16[768,512]{1,0:T(8,128)(2,1)S(1)}, u32[]{:S(2)}, u32[]{:S(2)}) collective-permute-start(bf16[768,512]{1,0:T(8,128)(2,1)S(1)} %pad_maximum_fusion.1), channel_id=1, source_target_pairs={{0,8},{1,25},{2,10},{3,27},{4,12},{5,29},{6,14},{7,31},{8,0},{9,17... | collective-permute-start | bytes 2359304 | tf_op jit(solution)/shard_map/ppermute | solution.py:70
  6.1 1.1 dynamic-slice_bitcast_fusion.1
  7.2 2.7 %collective-permute-start.4 = (bf16[384,512]{1,0:T(8,128)(2,1)S(1)}, bf16[384,512]{1,0:T(8,128)(2,1)}, u32[]{:S(2)}, u32[]{:S(2)}) collective-permute-start(bf16[384,512]{1,0:T(8,128)(2,1)S(1)} %pad_maximum_fusion.4), channel_id=1, source_target_pairs={{0,1},{1,0},{2,3},{3,2},{4,5},{5,4},{6,7},{7,6},{8,9},{9,8},{10,11... | collective-permute-start | bytes 1179656 | tf_op jit(solution)/shard_map/ppermute | solution.py:69
  10.0 1.5 collective-permute-done.4
  11.4 2.1 %collective-permute-start.5 = (bf16[384,512]{1,0:T(8,128)(2,1)}, bf16[384,512]{1,0:T(8,128)(2,1)}, u32[]{:S(2)}, u32[]{:S(2)}) collective-permute-start(bf16[384,512]{1,0:T(8,128)(2,1)} %collective-permute-done.4), channel_id=1, source_target_pairs={{0,8},{1,25},{2,10},{3,27},{4,12},{5,29},{6,14},{7,31},{8,0},{9,17... | collective-permute-start | bytes 1179656 | tf_op jit(solution)/shard_map/ppermute | solution.py:74
  13.6 4.5 %collective-permute-start.1 = (bf16[576,512]{1,0:T(8,128)(2,1)S(1)}, bf16[576,512]{1,0:T(8,128)(2,1)S(1)}, u32[]{:S(2)}, u32[]{:S(2)}) collective-permute-start(bf16[576,512]{1,0:T(8,128)(2,1)S(1)} %pad_maximum_fusion.3), channel_id=1, source_target_pairs={{0,24},{1,9},{2,26},{3,11},{4,28},{5,13},{6,30},{7,15},{8,16},{9,1... | collective-permute-start | bytes 1769480 | tf_op jit(solution)/shard_map/ppermute | solution.py:73
  18.2 0.0 copy-start.5
  18.2 0.0 collective-permute-done
  18.2 3.1 %collective-permute-start.2 = (bf16[576,512]{1,0:T(8,128)(2,1)S(1)}, bf16[576,512]{1,0:T(8,128)(2,1)S(1)}, u32[]{:S(2)}, u32[]{:S(2)}) collective-permute-start(bf16[576,512]{1,0:T(8,128)(2,1)S(1)} %slice.98), channel_id=1, source_target_pairs={{0,24},{1,9},{2,26},{3,11},{4,28},{5,13},{6,30},{7,15},{8,16},{9,1... | collective-permute-start | bytes 1769480 | tf_op jit(solution)/shard_map/ppermute | solution.py:76
  21.4 4.1 %collective-permute-start.6 = (bf16[384,512]{1,0:T(8,128)(2,1)}, bf16[384,512]{1,0:T(8,128)(2,1)S(1)}, u32[]{:S(2)}, u32[]{:S(2)}) collective-permute-start(bf16[384,512]{1,0:T(8,128)(2,1)} %collective-permute-done.4), channel_id=1, source_target_pairs={{0,24},{1,9},{2,26},{3,11},{4,28},{5,13},{6,30},{7,15},{8,16},{9,1... | collective-permute-start | bytes 1179656 | tf_op jit(solution)/shard_map/ppermute | solution.py:75
  25.5 0.0 collective-permute-done.5
  25.5 2.9 %collective-permute-start.7 = (bf16[384,512]{1,0:T(8,128)(2,1)}, bf16[384,512]{1,0:T(8,128)(2,1)S(1)}, u32[]{:S(2)}, u32[]{:S(2)}) collective-permute-start(bf16[384,512]{1,0:T(8,128)(2,1)} %collective-permute-done.5), channel_id=1, source_target_pairs={{0,24},{1,9},{2,26},{3,11},{4,28},{5,13},{6,30},{7,15},{8,16},{9,1... | collective-permute-start | bytes 1179656 | tf_op jit(solution)/shard_map/ppermute | solution.py:77
  28.4 0.0 copy-done.5
  28.5 0.7 fusion.44
  29.2 0.0 collective-permute-done.1
  29.2 0.7 fusion.45
  29.9 4.6 %collective-permute-done.2 = bf16[576,512]{1,0:T(8,128)(2,1)S(1)} collective-permute-done((bf16[576,512]{1,0:T(8,128)(2,1)S(1)}, bf16[576,512]{1,0:T(8,128)(2,1)S(1)}, u32[]{:S(2)}, u32[]{:S(2)}) %collective-permute-start.2) | collective-permute-done | bytes 589856 | tf_op jit(solution)/shard_map/ppermute | solution.py:76
  34.5 0.7 fusion.46
  35.3 0.0 copy-start.8
  35.3 0.1 pad_maximum_fusion.2
  35.3 2.1 %collective-permute-start.3 = (bf16[768,512]{1,0:T(8,128)(2,1)S(1)}, bf16[768,512]{1,0:T(8,128)(2,1)S(1)}, u32[]{:S(2)}, u32[]{:S(2)}) collective-permute-start(bf16[768,512]{1,0:T(8,128)(2,1)S(1)} %pad_maximum_fusion.2), channel_id=1, source_target_pairs={{0,1},{1,0},{2,3},{3,2},{4,5},{5,4},{6,7},{7,6},{8,9},{9,8},{10,11... | collective-permute-start | bytes 2359304 | tf_op jit(solution)/shard_map/ppermute | solution.py:79
  37.4 0.0 copy-done.8
  37.4 1.1 slice_dynamic-update-slice_fusion.3
  38.5 1.1 slice_dynamic-update-slice_fusion.2
  39.5 0.0 collective-permute-done.6
  39.6 3.4 %collective-permute-done.7 = bf16[384,512]{1,0:T(8,128)(2,1)S(1)} collective-permute-done((bf16[384,512]{1,0:T(8,128)(2,1)}, bf16[384,512]{1,0:T(8,128)(2,1)S(1)}, u32[]{:S(2)}, u32[]{:S(2)}) %collective-permute-start.7) | collective-permute-done | bytes 393248 | tf_op jit(solution)/shard_map/ppermute | solution.py:77
  43.0 0.0 copy-start.6
  43.0 0.0 copy-start.9
  43.0 0.0 collective-permute-done.3
  43.1 0.0 copy-start.3
  43.1 0.9 fusion.15
  44.0 0.1 copy-done.6
  44.1 0.5 copy-done.9
  44.7 0.5 copy-done.3
  45.2 0.9 fusion.12
  46.1 0.0 copy-start.4
  46.1 0.1 pad_maximum_fusion
  46.2 2.8 %collective-permute-start.8 = (f32[2,256,512]{2,1,0:T(8,128)S(1)}, f32[2,256,512]{2,1,0:T(8,128)}, u32[]{:S(2)}, u32[]{:S(2)}) collective-permute-start(f32[2,256,512]{2,1,0:T(8,128)S(1)} %pad_maximum_fusion), channel_id=1, source_target_pairs={{0,2},{1,7},{2,0},{3,5},{4,6},{5,3},{6,4},{7,1},{8,10},{9,15},{10,... | collective-permute-start | bytes 3145736 | tf_op jit(solution)/shard_map/ppermute | solution.py:94
  49.1 26.2 %collective-permute-done.8 = f32[2,256,512]{2,1,0:T(8,128)} collective-permute-done((f32[2,256,512]{2,1,0:T(8,128)S(1)}, f32[2,256,512]{2,1,0:T(8,128)}, u32[]{:S(2)}, u32[]{:S(2)}) %collective-permute-start.8) | collective-permute-done | bytes 1048608 | tf_op jit(solution)/shard_map/ppermute | solution.py:94
  75.3 0.0 copy-done.4
  75.3 0.0 copy-start.7
  75.3 3.3 %fusion.21 = f32[256,512]{1,0:T(8,128)} fusion(s32[]{:T(128)S(6)} %select_n.72, bf16[1536,512]{1,0:T(8,128)(2,1)} %copy-done.9, bf16[1536,512]{1,0:T(8,128)(2,1)} %copy-done.6, bf16[1536,512]{1,0:T(8,128)(2,1)S(1)} %copy-done.4, s32[]{:T(128)S(6)} %select_n.71, f32[2,256,512]{2,1,0:T(8,128)} %collective-permute-done.8), kind=kOutput, calls=%fused_computation.19 | convolution fusion | flops 405929984 | bytes 4980744 | tf_op jit(solution)/shard_map/dot_general | solution.py:89
  78.6 3.0 %collective-permute-start.9 = (f32[256,512]{1,0:T(8,128)}, f32[256,512]{1,0:T(8,128)}, u32[]{:S(2)}, u32[]{:S(2)}) collective-permute-start(f32[256,512]{1,0:T(8,128)} %fusion.21), channel_id=1, source_target_pairs={{0,6},{1,3},{2,4},{3,1},{4,2},{5,7},{6,0},{7,5},{8,14},{9,11},{10,... | collective-permute-start | bytes 1572872 | tf_op jit(solution)/shard_map/ppermute | solution.py:95
  81.7 16.1 %collective-permute-done.9 = f32[256,512]{1,0:T(8,128)} collective-permute-done((f32[256,512]{1,0:T(8,128)}, f32[256,512]{1,0:T(8,128)}, u32[]{:S(2)}, u32[]{:S(2)}) %collective-permute-start.9) | collective-permute-done | bytes 524320 | tf_op jit(solution)/shard_map/ppermute | solution.py:95
  97.7 0.0 copy-done.7
  97.7 4.3 %fusion.35 = (f32[1,1,256,512]{3,2,1,0:T(8,128)}, f32[256,512]{1,0:T(8,128)S(1)}, f32[1,1,256,512]{3,2,1,0:T(8,128)}) fusion(f32[1,1,256,512]{3,2,1,0:T(8,128)} %param.11, f32[1,1,256,512]{3,2,1,0:T(8,128)} %param.10, f32[1,1,256,512]{3,2,1,0:T(8,128)} %param.9, f32[256,512]{1,0:T(8,128)} %collective-permute-done.9, ...), kind=kOutput, calls=%fused_computation.66 | convolution fusion | flops 407764992 | bytes 8126472 | tf_op jit(solution)/shard_map/dot_general | solution.py:89
  102.0 0.0 copy-start.1
  102.0 0.0 copy-start.2
  102.0 23.5 %all_to_all.10 = f32[16,16,512]{2,1,0:T(8,128)S(1)} all-to-all(f32[16,16,512]{2,1,0:T(8,128)S(1)} %bitcast.70), channel_id=1, replica_groups=mesh['replica'=16,'fsdp'=32] {'replica'}, dimensions={0} | all-to-all | bytes 1048576 | tf_op jit(solution)/shard_map/all_to_all | solution.py:109
  125.5 0.0 copy-done.1
  125.6 0.0 copy-done.2
  125.6 0.6 subtract_bitcast_fusion
  126.3 21.0 %all_to_all.11 = f32[16,16,512]{2,1,0:T(8,128)S(1)} all-to-all(f32[16,16,512]{2,1,0:T(8,128)S(1)} %broadcast_in_dim.16), channel_id=1, replica_groups=mesh['replica'=16,'fsdp'=32] {'replica'}, dimensions={0} | all-to-all | bytes 1048576 | tf_op jit(solution)/shard_map/all_to_all | solution.py:115
  147.2 0.8 copy.33
  (13 shorter events, 0.4 us)
Async XLA Ops:
  0.6 2.0 %copy-start = (bf16[1,192,2048]{2,1,0:T(8,128)(2,1)S(1)}, bf16[1,192,2048]{2,1,0:T(8,128)(2,1)}, u32[]{:S(2)}) copy-start(bf16[1,192,2048]{2,1,0:T(8,128)(2,1)} %param.7) | copy-start | bytes 2359300
  2.7 15.5 %collective-permute-start = (bf16[768,512]{1,0:T(8,128)(2,1)S(1)}, bf16[768,512]{1,0:T(8,128)(2,1)S(1)}, u32[]{:S(2)}, u32[]{:S(2)}) collective-permute-start(bf16[768,512]{1,0:T(8,128)(2,1)S(1)} %pad_maximum_fusion.1), channel_id=1, source_target_pairs={{0,8},{1,25},{2,10},{3,27},{4,12},{5,29},{6,14},{7,31},{8,0},{9,17... | collective-permute-start | bytes 2359304 | tf_op jit(solution)/shard_map/ppermute | solution.py:70
  7.2 4.2 %collective-permute-start.4 = (bf16[384,512]{1,0:T(8,128)(2,1)S(1)}, bf16[384,512]{1,0:T(8,128)(2,1)}, u32[]{:S(2)}, u32[]{:S(2)}) collective-permute-start(bf16[384,512]{1,0:T(8,128)(2,1)S(1)} %pad_maximum_fusion.4), channel_id=1, source_target_pairs={{0,1},{1,0},{2,3},{3,2},{4,5},{5,4},{6,7},{7,6},{8,9},{9,8},{10,11... | collective-permute-start | bytes 1179656 | tf_op jit(solution)/shard_map/ppermute | solution.py:69
  11.4 14.1 %collective-permute-start.5 = (bf16[384,512]{1,0:T(8,128)(2,1)}, bf16[384,512]{1,0:T(8,128)(2,1)}, u32[]{:S(2)}, u32[]{:S(2)}) collective-permute-start(bf16[384,512]{1,0:T(8,128)(2,1)} %collective-permute-done.4), channel_id=1, source_target_pairs={{0,8},{1,25},{2,10},{3,27},{4,12},{5,29},{6,14},{7,31},{8,0},{9,17... | collective-permute-start | bytes 1179656 | tf_op jit(solution)/shard_map/ppermute | solution.py:74
  13.6 15.6 %collective-permute-start.1 = (bf16[576,512]{1,0:T(8,128)(2,1)S(1)}, bf16[576,512]{1,0:T(8,128)(2,1)S(1)}, u32[]{:S(2)}, u32[]{:S(2)}) collective-permute-start(bf16[576,512]{1,0:T(8,128)(2,1)S(1)} %pad_maximum_fusion.3), channel_id=1, source_target_pairs={{0,24},{1,9},{2,26},{3,11},{4,28},{5,13},{6,30},{7,15},{8,16},{9,1... | collective-permute-start | bytes 1769480 | tf_op jit(solution)/shard_map/ppermute | solution.py:73
  18.2 10.3 %copy-start.5 = (bf16[1536,512]{1,0:T(8,128)(2,1)S(1)}, bf16[1536,512]{1,0:T(8,128)(2,1)}, u32[]{:S(2)}) copy-start(bf16[1536,512]{1,0:T(8,128)(2,1)} %get-tuple-element.8) | copy-start | bytes 4718596
  18.2 16.3 %collective-permute-start.2 = (bf16[576,512]{1,0:T(8,128)(2,1)S(1)}, bf16[576,512]{1,0:T(8,128)(2,1)S(1)}, u32[]{:S(2)}, u32[]{:S(2)}) collective-permute-start(bf16[576,512]{1,0:T(8,128)(2,1)S(1)} %slice.98), channel_id=1, source_target_pairs={{0,24},{1,9},{2,26},{3,11},{4,28},{5,13},{6,30},{7,15},{8,16},{9,1... | collective-permute-start | bytes 1769480 | tf_op jit(solution)/shard_map/ppermute | solution.py:76
  21.4 18.2 %collective-permute-start.6 = (bf16[384,512]{1,0:T(8,128)(2,1)}, bf16[384,512]{1,0:T(8,128)(2,1)S(1)}, u32[]{:S(2)}, u32[]{:S(2)}) collective-permute-start(bf16[384,512]{1,0:T(8,128)(2,1)} %collective-permute-done.4), channel_id=1, source_target_pairs={{0,24},{1,9},{2,26},{3,11},{4,28},{5,13},{6,30},{7,15},{8,16},{9,1... | collective-permute-start | bytes 1179656 | tf_op jit(solution)/shard_map/ppermute | solution.py:75
  25.5 17.5 %collective-permute-start.7 = (bf16[384,512]{1,0:T(8,128)(2,1)}, bf16[384,512]{1,0:T(8,128)(2,1)S(1)}, u32[]{:S(2)}, u32[]{:S(2)}) collective-permute-start(bf16[384,512]{1,0:T(8,128)(2,1)} %collective-permute-done.5), channel_id=1, source_target_pairs={{0,24},{1,9},{2,26},{3,11},{4,28},{5,13},{6,30},{7,15},{8,16},{9,1... | collective-permute-start | bytes 1179656 | tf_op jit(solution)/shard_map/ppermute | solution.py:77
  35.3 2.1 %copy-start.8 = (bf16[1536,512]{1,0:T(8,128)(2,1)S(1)}, bf16[1536,512]{1,0:T(8,128)(2,1)}, u32[]{:S(2)}) copy-start(bf16[1536,512]{1,0:T(8,128)(2,1)} %get-tuple-element.33) | copy-start | bytes 4718596
  35.3 7.7 %collective-permute-start.3 = (bf16[768,512]{1,0:T(8,128)(2,1)S(1)}, bf16[768,512]{1,0:T(8,128)(2,1)S(1)}, u32[]{:S(2)}, u32[]{:S(2)}) collective-permute-start(bf16[768,512]{1,0:T(8,128)(2,1)S(1)} %pad_maximum_fusion.2), channel_id=1, source_target_pairs={{0,1},{1,0},{2,3},{3,2},{4,5},{5,4},{6,7},{7,6},{8,9},{9,8},{10,11... | collective-permute-start | bytes 2359304 | tf_op jit(solution)/shard_map/ppermute | solution.py:79
  43.0 1.1 copy-start.6
  43.0 1.7 %copy-start.9 = (bf16[1536,512]{1,0:T(8,128)(2,1)}, bf16[1536,512]{1,0:T(8,128)(2,1)S(1)}, u32[]{:S(2)}) copy-start(bf16[1536,512]{1,0:T(8,128)(2,1)S(1)} %get-tuple-element.35) | copy-start | bytes 4718596
  43.1 2.1 %copy-start.3 = (bf16[1536,512]{1,0:T(8,128)(2,1)}, bf16[1536,512]{1,0:T(8,128)(2,1)S(1)}, u32[]{:S(2)}) copy-start(bf16[1536,512]{1,0:T(8,128)(2,1)S(1)} %slice_dynamic-update-slice_fusion.14) | copy-start | bytes 4718596
  46.1 29.1 %copy-start.4 = (bf16[1536,512]{1,0:T(8,128)(2,1)S(1)}, bf16[1536,512]{1,0:T(8,128)(2,1)}, u32[]{:S(2)}) copy-start(bf16[1536,512]{1,0:T(8,128)(2,1)} %copy-done.3) | copy-start | bytes 4718596
  46.2 29.1 %collective-permute-start.8 = (f32[2,256,512]{2,1,0:T(8,128)S(1)}, f32[2,256,512]{2,1,0:T(8,128)}, u32[]{:S(2)}, u32[]{:S(2)}) collective-permute-start(f32[2,256,512]{2,1,0:T(8,128)S(1)} %pad_maximum_fusion), channel_id=1, source_target_pairs={{0,2},{1,7},{2,0},{3,5},{4,6},{5,3},{6,4},{7,1},{8,10},{9,15},{10,... | collective-permute-start | bytes 3145736 | tf_op jit(solution)/shard_map/ppermute | solution.py:94
  75.3 22.4 %copy-start.7 = (bf16[1536,512]{1,0:T(8,128)(2,1)S(1)}, bf16[1536,512]{1,0:T(8,128)(2,1)}, u32[]{:S(2)}) copy-start(bf16[1536,512]{1,0:T(8,128)(2,1)} %copy-done.6) | copy-start | bytes 4718596
  78.6 19.1 %collective-permute-start.9 = (f32[256,512]{1,0:T(8,128)}, f32[256,512]{1,0:T(8,128)}, u32[]{:S(2)}, u32[]{:S(2)}) collective-permute-start(f32[256,512]{1,0:T(8,128)} %fusion.21), channel_id=1, source_target_pairs={{0,6},{1,3},{2,4},{3,1},{4,2},{5,7},{6,0},{7,5},{8,14},{9,11},{10,... | collective-permute-start | bytes 1572872 | tf_op jit(solution)/shard_map/ppermute | solution.py:95
  102.0 23.5 %copy-start.1 = (f32[1,16,512]{2,1,0:T(8,128)S(1)}, f32[1,16,512]{2,1,0:T(8,128)}, u32[]{:S(2)}) copy-start(f32[1,16,512]{2,1,0:T(8,128)} %param.12) | copy-start | bytes 98308
  102.0 23.5 %copy-start.2 = (f32[1,16,512]{2,1,0:T(8,128)S(1)}, f32[1,16,512]{2,1,0:T(8,128)}, u32[]{:S(2)}) copy-start(f32[1,16,512]{2,1,0:T(8,128)} %param.13) | copy-start | bytes 98308

commit v3 on v1

v3 whole, which is shorter than its diff:
```python
import jax
import jax.numpy as jnp
from jax import lax
from jax.experimental import pallas as pl
from jax.sharding import PartitionSpec as P

STEP = 500


beta_one = 0.9
beta_two = 0.95
adam_eps = 1e-08
decay_rate = 0.1
inner_rate = 0.02
outer_rate = 0.7
outer_mu = 0.9

SIDE = 4
SHARDS = 32


def ring_partner(i, stage):
    return i ^ 1 if stage == 0 else i ^ 3


def place(i):
    return i // 8, i // 2 % SIDE, i % 2


def core_pairs():
    return [(i, i ^ 1) for i in range(SHARDS)]


def x_pairs(stage):
    pairs = []
    for i in range(SHARDS):
        x, y, c = place(i)
        pairs.append((i, ring_partner(x, stage ^ c) * 8 + y * 2 + c))
    return pairs


def y_pairs(stage):
    pairs = []
    for i in range(SHARDS):
        x, y, c = place(i)
        pairs.append((i, x * 8 + ring_partner(y, stage ^ c) * 2 + c))
    return pairs


def after(value, *others):
    others = [lax.slice(t, (0, 0), (16, 128)) for t in others]
    return pl.pallas_call(
        lambda *refs: None,
        out_shape=jax.ShapeDtypeStruct(value.shape, value.dtype),
        in_specs=[pl.BlockSpec(memory_space=pl.ANY)] * (1 + len(others)),
        out_specs=pl.BlockSpec(memory_space=pl.ANY),
        input_output_aliases={0: 0},
    )(value, *others)


def body(acts, upstream, inner_params, first_moment, second_moment, anchor, outer_momentum):
    members = lax.axis_size("replica")
    me = lax.axis_index("fsdp")
    x, y, c = me >> 3, (me >> 1) & 3, me & 1
    near, far = jnp.where(c == 0, 1, 3), jnp.where(c == 0, 3, 1)
    a = acts[0]
    u = upstream[0]
    count = a.shape[0]
    rows, cols = 256, 512

    halves = 2
    width = cols // halves

    def a_for(dest):
        return lax.dynamic_slice(a, (0, dest * 2 * rows), (count, 2 * rows))

    def u_for(core, j):
        return jnp.concatenate(
            [
                lax.dynamic_slice(u, (0, (k * 2 + core) * cols + j * width), (count, width))
                for k in range(2)
            ],
            1,
        )

    def pieces(t):
        return [t[i * count : (i + 1) * count] for i in range(t.shape[0] // count)]

    def gather_x(mine):
        one = lax.ppermute(mine, "fsdp", x_pairs(0))
        two = lax.ppermute(mine, "fsdp", x_pairs(1))
        return mine, one, two, lax.ppermute(one, "fsdp", x_pairs(1))

    swap = lax.ppermute(
        jnp.concatenate([u_for(1 - c, j) for j in range(halves)], 0), "fsdp", core_pairs()
    )
    a_one = lax.ppermute(jnp.concatenate([a_for(x ^ near), a_for(x ^ 2)], 0), "fsdp", x_pairs(0))
    a_one = after(a_one, swap)
    a_two = lax.ppermute(
        jnp.concatenate([a_for(x ^ far), a_one[count:]], 0), "fsdp", x_pairs(1)
    )
    mine = [
        jnp.concatenate([u_for(c, j), swap[j * count : (j + 1) * count]], 0) for j in range(halves)
    ]
    first = gather_x(mine[0])
    a_two = after(a_two, first[1])
    a_core = jnp.concatenate([a_for(x), a_one[:count], a_two], 0)
    a_other = lax.ppermute(a_core, "fsdp", core_pairs())
    own, other = pieces(a_core), pieces(a_other)
    a_chips = [jnp.concatenate([own[i], other[j]], 0) for i, j in enumerate((0, 2, 1, 3))]

    def chunk_sum(gathered):
        return sum(
            lax.dot_general(
                left, right, (((0,), (0,)), ((), ())), preferred_element_type=jnp.float32
            )
            for left, right in zip(a_chips, gathered)
        )

    def reduce_y(whole):
        def part(dest):
            return lax.dynamic_slice(
                whole, ((dest >> 1) * rows, (dest & 1) * width), (rows, width)
            )

        g_one = lax.ppermute(jnp.stack([part(y ^ 2), part(y ^ near)]), "fsdp", y_pairs(0))
        passed_on = part(y ^ far) + g_one[0]
        g_two = lax.ppermute(passed_on, "fsdp", y_pairs(1))
        return part(y) + g_one[1] + g_two, passed_on

    fix_one = 1.0 - beta_one**STEP
    fix_two = 1.0 - beta_two**STEP
    slice_rows = rows // members

    second = gather_x(after(mine[1], first[2], a_other))
    near_done, token = reduce_y(chunk_sum(first))
    far_done, _ = reduce_y(chunk_sum((*second[:3], after(second[3], token))))
    gradient = jnp.concatenate([near_done, far_done], 1)

    params = inner_params[0, 0]
    moment_one = beta_one * first_moment[0, 0] + (1.0 - beta_one) * gradient
    moment_two = beta_two * second_moment[0, 0] + (1.0 - beta_two) * gradient * gradient
    update = (
        moment_one / fix_one / (jnp.sqrt(moment_two / fix_two) + adam_eps) + decay_rate * params
    )
    stepped = params - inner_rate * update
    parts = lax.all_to_all(
        stepped.reshape(members, slice_rows, cols),
        "replica",
        split_axis=0,
        concat_axis=0,
        tiled=True,
    )
    total = jnp.sum(parts, axis=0)
    pseudo = anchor[0] - total / members
    new_momentum = outer_mu * outer_momentum[0] + pseudo
    new_params = anchor[0] - outer_rate * (pseudo + outer_mu * new_momentum)
    gathered = lax.all_to_all(
        jnp.broadcast_to(new_params[None], (members, slice_rows, cols)),
        "replica",
        split_axis=0,
        concat_axis=0,
        tiled=True,
    ).reshape(rows, cols)
    return (gathered[None], new_momentum[None], moment_one[None, None], moment_two[None, None])


def solution(mesh):
    in_specs = (
        P("replica", "fsdp", None),
        P("replica", "fsdp", None),
        P("replica", "fsdp", None, None),
        P("replica", "fsdp", None, None),
        P("replica", "fsdp", None, None),
        P("fsdp", "replica", None),
        P("fsdp", "replica", None),
    )
    out_specs = (
        P("fsdp", None, None),
        P("fsdp", "replica", None),
        P("replica", "fsdp", None, None),
        P("replica", "fsdp", None, None),
    )
    return jax.shard_map(body, mesh=mesh, in_specs=in_specs, out_specs=out_specs, check_vma=False)
```

time: 161 us -> 162 us (level)
  the two profiles are of different devices: /device:TPU:110 before, /device:TPU:24 now
where the time goes in v3:
time: 162 us; the launch traced here: 161 us
  waiting for transfers between devices  46.9 us (29%)
  starting transfers between devices  44.9 us (28%)
  blocking collectives  44.4 us (27%)
  local copies, waits for them, and re-layouts  9.49 us (6%)
  other arithmetic  8.04 us (5%)
  matrix products  5.69 us (4%)
    all_to_all x1, blocking collectives, body(): lax.all_to_all(stepped.reshape(members, slice_rows, cols), 'replica', spl...  24.5 us
    ppermute x2, waiting for transfers between devices, reduce_y(): lax.ppermute(jnp.stack([part(y ^ 2), part(y ^ near)]), 'fsdp', y_pairs(0))  23.8 us
    all_to_all x1, blocking collectives, body(): lax.all_to_all(jnp.broadcast_to(new_params[None], (members, slice_rows, c...  19.9 us
    ppermute x2, starting transfers between devices, reduce_y(): g_two = lax.ppermute(passed_on, 'fsdp', y_pairs(1))  9.99 us
    ppermute x2, starting transfers between devices, gather_x(): two = lax.ppermute(mine, 'fsdp', x_pairs(1))  9.34 us
    ppermute x1, waiting for transfers between devices, body(): lax.ppermute(jnp.concatenate([a_for(x ^ near), a_for(x ^ 2)], 0), 'fsdp',...  5.76 us
    ppermute x2, waiting for transfers between devices, reduce_y(): g_two = lax.ppermute(passed_on, 'fsdp', y_pairs(1))  5.73 us
    dot_general x8, matrix products, chunk_sum(): lax.dot_general(left, right, (((0,), (0,)), ((), ())), preferred_element_...  5.69 us
  transfers between devices with their start and end apart: 14, of which 8 were waited for; matrix products, arithmetic and copies ran while one was open for 7% of the time, Pallas kernels for 0%

profile of v3, /device:TPU:24, one launch (start us, length us, event | category | flops | bytes accessed | tf_op | source)
XLA Modules:
  0.0 160.7 jit_solution(16569745834042352295)
XLA Ops:
  0.7 1.4 dynamic-slice_bitcast_fusion.11
  2.0 1.9 %collective-permute-start.1 = (bf16[384,512]{1,0:T(8,128)(2,1)S(1)}, bf16[384,512]{1,0:T(8,128)(2,1)S(1)}, u32[]{:S(2)}, u32[]{:S(2)}) collective-permute-start(bf16[384,512]{1,0:T(8,128)(2,1)S(1)} %maximum_maximum_fusion), channel_id=1, source_target_pairs={{0,1},{1,0},{2,3},{3,2},{4,5},{5,4},{6,7},{7,6},{8,9},{9,8},{10,11... | collective-permute-start | bytes 1179656 | tf_op jit(solution)/shard_map/ppermute | solution.py:94
  4.0 0.1 dynamic-slice_bitcast_fusion.7
  4.1 3.4 %collective-permute-start = (bf16[384,512]{1,0:T(8,128)(2,1)S(1)}, bf16[384,512]{1,0:T(8,128)(2,1)}, u32[]{:S(2)}, u32[]{:S(2)}) collective-permute-start(bf16[384,512]{1,0:T(8,128)(2,1)S(1)} %pad_maximum_fusion.5), channel_id=1, source_target_pairs={{0,8},{1,25},{2,10},{3,27},{4,12},{5,29},{6,14},{7,31},{8,0},{9,17... | collective-permute-start | bytes 1179656 | tf_op jit(solution)/shard_map/ppermute | solution.py:97
  7.6 0.6 slice.76.refs_1_
  8.2 5.8 %collective-permute-done.refs_0_ = bf16[384,512]{1,0:T(8,128)(2,1)} collective-permute-done((bf16[384,512]{1,0:T(8,128)(2,1)S(1)}, bf16[384,512]{1,0:T(8,128)(2,1)}, u32[]{:S(2)}, u32[]{:S(2)}) %collective-permute-start) | collective-permute-done | bytes 393248 | tf_op jit(solution)/shard_map/ppermute | solution.py:97
  13.9 1.0 fusion.30
  15.0 3.4 %collective-permute-start.3 = (bf16[384,512]{1,0:T(8,128)(2,1)S(1)}, bf16[384,512]{1,0:T(8,128)(2,1)}, u32[]{:S(2)}, u32[]{:S(2)}) collective-permute-start(bf16[384,512]{1,0:T(8,128)(2,1)S(1)} %pad_maximum_fusion.7), channel_id=1, source_target_pairs={{0,8},{1,25},{2,10},{3,27},{4,12},{5,29},{6,14},{7,31},{8,0},{9,17... | collective-permute-start | bytes 1179656 | tf_op jit(solution)/shard_map/ppermute | solution.py:90
  18.5 4.0 %collective-permute-start.2 = (bf16[384,512]{1,0:T(8,128)(2,1)S(1)}, bf16[384,512]{1,0:T(8,128)(2,1)S(1)}, u32[]{:S(2)}, u32[]{:S(2)}) collective-permute-start(bf16[384,512]{1,0:T(8,128)(2,1)S(1)} %pad_maximum_fusion.6), channel_id=1, source_target_pairs={{0,24},{1,9},{2,26},{3,11},{4,28},{5,13},{6,30},{7,15},{8,16},{9,1... | collective-permute-start | bytes 1179656 | tf_op jit(solution)/shard_map/ppermute | solution.py:99
  22.5 2.5 %collective-permute-done.3 = bf16[384,512]{1,0:T(8,128)(2,1)} collective-permute-done((bf16[384,512]{1,0:T(8,128)(2,1)S(1)}, bf16[384,512]{1,0:T(8,128)(2,1)}, u32[]{:S(2)}, u32[]{:S(2)}) %collective-permute-start.3) | collective-permute-done | bytes 393248 | tf_op jit(solution)/shard_map/ppermute | solution.py:90
  25.0 1.3 slice.80.refs_1_
  26.3 3.4 %collective-permute-done.2.refs_0_ = bf16[384,512]{1,0:T(8,128)(2,1)S(1)} collective-permute-done((bf16[384,512]{1,0:T(8,128)(2,1)S(1)}, bf16[384,512]{1,0:T(8,128)(2,1)S(1)}, u32[]{:S(2)}, u32[]{:S(2)}) %collective-permute-start.2) | collective-permute-done | bytes 393248 | tf_op jit(solution)/shard_map/ppermute | solution.py:99
  29.7 0.7 copy-done
  30.5 2.0 %pad_maximum_fusion = bf16[768,512]{1,0:T(8,128)(2,1)} fusion(bf16[384,512]{1,0:T(8,128)(2,1)} %shard_map.103, bf16[192,512]{1,0:T(8,128)(2,1)S(1)} %get-tuple-element.32, bf16[192,512]{1,0:T(8,128)(2,1)S(1)} %get-tuple-element.14), kind=kLoop, calls=%fused_computation.6 | loop fusion | flops 2359296 | bytes 1572864 | tf_op jit(solution)/shard_map/concatenate | solution.py:107
  32.5 1.9 %collective-permute-start.4 = (bf16[768,512]{1,0:T(8,128)(2,1)}, bf16[768,512]{1,0:T(8,128)(2,1)S(1)}, u32[]{:S(2)}, u32[]{:S(2)}) collective-permute-start(bf16[768,512]{1,0:T(8,128)(2,1)} %pad_maximum_fusion), channel_id=1, source_target_pairs={{0,1},{1,0},{2,3},{3,2},{4,5},{5,4},{6,7},{7,6},{8,9},{9,8},{10,11... | collective-permute-start | bytes 2359304 | tf_op jit(solution)/shard_map/ppermute | solution.py:108
  34.4 4.7 %collective-permute-start.5 = (bf16[384,512]{1,0:T(8,128)(2,1)S(1)}, bf16[384,512]{1,0:T(8,128)(2,1)S(1)}, u32[]{:S(2)}, u32[]{:S(2)}) collective-permute-start(bf16[384,512]{1,0:T(8,128)(2,1)S(1)} %pad_maximum_fusion.7), channel_id=1, source_target_pairs={{0,24},{1,9},{2,26},{3,11},{4,28},{5,13},{6,30},{7,15},{8,16},{9,1... | collective-permute-start | bytes 1179656 | tf_op jit(solution)/shard_map/ppermute | solution.py:91
  39.1 0.8 pad_maximum_fusion.12.refs_0_
  39.9 2.4 %collective-permute-start.6 = (bf16[384,512]{1,0:T(8,128)(2,1)}, bf16[384,512]{1,0:T(8,128)(2,1)S(1)}, u32[]{:S(2)}, u32[]{:S(2)}) collective-permute-start(bf16[384,512]{1,0:T(8,128)(2,1)} %collective-permute-done.3), channel_id=1, source_target_pairs={{0,24},{1,9},{2,26},{3,11},{4,28},{5,13},{6,30},{7,15},{8,16},{9,1... | collective-permute-start | bytes 1179656 | tf_op jit(solution)/shard_map/ppermute | solution.py:92
  42.3 3.0 %collective-permute-done.5 = bf16[384,512]{1,0:T(8,128)(2,1)S(1)} collective-permute-done((bf16[384,512]{1,0:T(8,128)(2,1)S(1)}, bf16[384,512]{1,0:T(8,128)(2,1)S(1)}, u32[]{:S(2)}, u32[]{:S(2)}) %collective-permute-start.5) | collective-permute-done | bytes 393248 | tf_op jit(solution)/shard_map/ppermute | solution.py:91
  45.3 0.6 slice.90.refs_1_
  46.0 0.7 slice.91.refs_2_
  46.6 4.7 %collective-permute-start.10 = (bf16[384,512]{1,0:T(8,128)(2,1)}, bf16[384,512]{1,0:T(8,128)(2,1)S(1)}, u32[]{:S(2)}, u32[]{:S(2)}) collective-permute-start(bf16[384,512]{1,0:T(8,128)(2,1)} %shard_map.104), channel_id=1, source_target_pairs={{0,24},{1,9},{2,26},{3,11},{4,28},{5,13},{6,30},{7,15},{8,16},{9,1... | collective-permute-start | bytes 1179656 | tf_op jit(solution)/shard_map/ppermute | solution.py:91
  51.3 1.9 %collective-permute-start.9 = (bf16[384,512]{1,0:T(8,128)(2,1)}, bf16[384,512]{1,0:T(8,128)(2,1)S(1)}, u32[]{:S(2)}, u32[]{:S(2)}) collective-permute-start(bf16[384,512]{1,0:T(8,128)(2,1)} %shard_map.104), channel_id=1, source_target_pairs={{0,8},{1,25},{2,10},{3,27},{4,12},{5,29},{6,14},{7,31},{8,0},{9,17... | collective-permute-start | bytes 1179656 | tf_op jit(solution)/shard_map/ppermute | solution.py:90
  53.2 0.1 fusion.28
  53.3 0.0 copy-start.12
  53.3 1.5 fusion.19
  54.8 0.5 fusion.17
  55.3 0.5 fusion.1
  55.8 0.5 convolution_add_fusion.2
  56.3 2.2 %collective-permute-start.7 = (f32[2,256,256]{2,1,0:T(8,128)S(1)}, f32[2,256,256]{2,1,0:T(8,128)S(1)}, u32[]{:S(2)}, u32[]{:S(2)}) collective-permute-start(f32[2,256,256]{2,1,0:T(8,128)S(1)} %pad_maximum_fusion.1), channel_id=1, source_target_pairs={{0,2},{1,7},{2,0},{3,5},{4,6},{5,3},{6,4},{7,1},{8,10},{9,15},{10,... | collective-permute-start | bytes 1572872 | tf_op jit(solution)/shard_map/ppermute | solution.py:126
  58.6 2.6 %collective-permute-done.9 = bf16[384,512]{1,0:T(8,128)(2,1)S(1)} collective-permute-done((bf16[384,512]{1,0:T(8,128)(2,1)}, bf16[384,512]{1,0:T(8,128)(2,1)S(1)}, u32[]{:S(2)}, u32[]{:S(2)}) %collective-permute-start.9) | collective-permute-done | bytes 393248 | tf_op jit(solution)/shard_map/ppermute | solution.py:90
  61.2 2.4 %collective-permute-start.11 = (bf16[384,512]{1,0:T(8,128)(2,1)S(1)}, bf16[384,512]{1,0:T(8,128)(2,1)}, u32[]{:S(2)}, u32[]{:S(2)}) collective-permute-start(bf16[384,512]{1,0:T(8,128)(2,1)S(1)} %collective-permute-done.9), channel_id=1, source_target_pairs={{0,24},{1,9},{2,26},{3,11},{4,28},{5,13},{6,30},{7,15},{8,16},{9,1... | collective-permute-start | bytes 1179656 | tf_op jit(solution)/shard_map/ppermute | solution.py:92
  63.6 0.5 fusion.18
  64.0 0.0 copy-start.2
  64.0 0.5 fusion.16
  64.5 0.5 copy-done.2
  65.0 0.5 fusion
  65.5 8.5 %collective-permute-done.7 = f32[2,256,256]{2,1,0:T(8,128)S(1)} collective-permute-done((f32[2,256,256]{2,1,0:T(8,128)S(1)}, f32[2,256,256]{2,1,0:T(8,128)S(1)}, u32[]{:S(2)}, u32[]{:S(2)}) %collective-permute-start.7) | collective-permute-done | bytes 524320 | tf_op jit(solution)/shard_map/ppermute | solution.py:126
  74.0 0.8 copy-done.9
  74.8 0.0 copy-start.13
  74.8 0.7 slice.92.refs_1_
  75.5 0.0 copy-done.13
  75.5 1.5 convolution_add_fusion
  77.0 0.0 copy-start.14
  77.0 0.0 copy-start.10
  77.1 2.1 %collective-permute-start.12 = (f32[2,256,256]{2,1,0:T(8,128)S(1)}, f32[2,256,256]{2,1,0:T(8,128)S(1)}, u32[]{:S(2)}, u32[]{:S(2)}) collective-permute-start(f32[2,256,256]{2,1,0:T(8,128)S(1)} %pad_maximum_fusion.2), channel_id=1, source_target_pairs={{0,2},{1,7},{2,0},{3,5},{4,6},{5,3},{6,4},{7,1},{8,10},{9,15},{10,... | collective-permute-start | bytes 1572872 | tf_op jit(solution)/shard_map/ppermute | solution.py:126
  79.2 5.5 %collective-permute-start.8 = (f32[256,256]{1,0:T(8,128)S(1)}, f32[256,256]{1,0:T(8,128)}, u32[]{:S(2)}, u32[]{:S(2)}) collective-permute-start(f32[256,256]{1,0:T(8,128)S(1)} %copy-done.14), channel_id=1, source_target_pairs={{0,6},{1,3},{2,4},{3,1},{4,2},{5,7},{6,0},{7,5},{8,14},{9,11},{10,... | collective-permute-start | bytes 786440 | tf_op jit(solution)/shard_map/ppermute | solution.py:128
  84.7 15.4 %collective-permute-done.12 = f32[2,256,256]{2,1,0:T(8,128)S(1)} collective-permute-done((f32[2,256,256]{2,1,0:T(8,128)S(1)}, f32[2,256,256]{2,1,0:T(8,128)S(1)}, u32[]{:S(2)}, u32[]{:S(2)}) %collective-permute-start.12) | collective-permute-done | bytes 524320 | tf_op jit(solution)/shard_map/ppermute | solution.py:126
  100.1 0.7 fusion.10
  100.8 4.4 %collective-permute-start.13 = (f32[256,256]{1,0:T(8,128)}, f32[256,256]{1,0:T(8,128)}, u32[]{:S(2)}, u32[]{:S(2)}) collective-permute-start(f32[256,256]{1,0:T(8,128)} %fusion.10), channel_id=1, source_target_pairs={{0,6},{1,3},{2,4},{3,1},{4,2},{5,7},{6,0},{7,5},{8,14},{9,11},{10,... | collective-permute-start | bytes 786440 | tf_op jit(solution)/shard_map/ppermute | solution.py:128
  105.3 0.0 copy-start.6
  105.3 0.0 copy-start.7
  105.3 1.1 fusion.15
  106.4 5.7 %collective-permute-done.13 = f32[256,256]{1,0:T(8,128)} collective-permute-done((f32[256,256]{1,0:T(8,128)}, f32[256,256]{1,0:T(8,128)}, u32[]{:S(2)}, u32[]{:S(2)}) %collective-permute-start.13) | collective-permute-done | bytes 262176 | tf_op jit(solution)/shard_map/ppermute | solution.py:128
  112.2 1.0 fusion.12
  113.2 0.0 copy-start.8
  113.2 1.2 fusion.9
  114.4 0.3 fusion.8
  114.7 0.0 copy-start.15
  114.7 0.0 copy-start.16
  114.8 24.5 %all_to_all.10 = f32[16,16,512]{2,1,0:T(8,128)S(1)} all-to-all(f32[16,16,512]{2,1,0:T(8,128)S(1)} %fusion.8), channel_id=1, replica_groups=mesh['replica'=16,'fsdp'=32] {'replica'}, dimensions={0} | all-to-all | bytes 1048576 | tf_op jit(solution)/shard_map/all_to_all | solution.py:147
  139.3 0.6 subtract_bitcast_fusion
  140.0 19.9 %all_to_all.11 = f32[16,16,512]{2,1,0:T(8,128)S(1)} all-to-all(f32[16,16,512]{2,1,0:T(8,128)S(1)} %broadcast_in_dim.5), channel_id=1, replica_groups=mesh['replica'=16,'fsdp'=32] {'replica'}, dimensions={0} | all-to-all | bytes 1048576 | tf_op jit(solution)/shard_map/all_to_all | solution.py:158
  159.9 0.8 copy.20
  (43 shorter events, 0.5 us)
Async XLA Ops:
  0.6 3.4 %copy-start.5 = (bf16[1,192,2048]{2,1,0:T(8,128)(2,1)S(1)}, bf16[1,192,2048]{2,1,0:T(8,128)(2,1)}, u32[]{:S(2)}) copy-start(bf16[1,192,2048]{2,1,0:T(8,128)(2,1)} %param.7) | copy-start | bytes 2359300
  2.0 5.5 %collective-permute-start.1 = (bf16[384,512]{1,0:T(8,128)(2,1)S(1)}, bf16[384,512]{1,0:T(8,128)(2,1)S(1)}, u32[]{:S(2)}, u32[]{:S(2)}) collective-permute-start(bf16[384,512]{1,0:T(8,128)(2,1)S(1)} %maximum_maximum_fusion), channel_id=1, source_target_pairs={{0,1},{1,0},{2,3},{3,2},{4,5},{5,4},{6,7},{7,6},{8,9},{9,8},{10,11... | collective-permute-start | bytes 1179656 | tf_op jit(solution)/shard_map/ppermute | solution.py:94
  4.1 9.8 %collective-permute-start = (bf16[384,512]{1,0:T(8,128)(2,1)S(1)}, bf16[384,512]{1,0:T(8,128)(2,1)}, u32[]{:S(2)}, u32[]{:S(2)}) collective-permute-start(bf16[384,512]{1,0:T(8,128)(2,1)S(1)} %pad_maximum_fusion.5), channel_id=1, source_target_pairs={{0,8},{1,25},{2,10},{3,27},{4,12},{5,29},{6,14},{7,31},{8,0},{9,17... | collective-permute-start | bytes 1179656 | tf_op jit(solution)/shard_map/ppermute | solution.py:97
  15.0 10.0 %collective-permute-start.3 = (bf16[384,512]{1,0:T(8,128)(2,1)S(1)}, bf16[384,512]{1,0:T(8,128)(2,1)}, u32[]{:S(2)}, u32[]{:S(2)}) collective-permute-start(bf16[384,512]{1,0:T(8,128)(2,1)S(1)} %pad_maximum_fusion.7), channel_id=1, source_target_pairs={{0,8},{1,25},{2,10},{3,27},{4,12},{5,29},{6,14},{7,31},{8,0},{9,17... | collective-permute-start | bytes 1179656 | tf_op jit(solution)/shard_map/ppermute | solution.py:90
  18.5 11.2 %collective-permute-start.2 = (bf16[384,512]{1,0:T(8,128)(2,1)S(1)}, bf16[384,512]{1,0:T(8,128)(2,1)S(1)}, u32[]{:S(2)}, u32[]{:S(2)}) collective-permute-start(bf16[384,512]{1,0:T(8,128)(2,1)S(1)} %pad_maximum_fusion.6), channel_id=1, source_target_pairs={{0,24},{1,9},{2,26},{3,11},{4,28},{5,13},{6,30},{7,15},{8,16},{9,1... | collective-permute-start | bytes 1179656 | tf_op jit(solution)/shard_map/ppermute | solution.py:99
  29.7 0.7 copy-start
  30.5 15.4 %copy-start.1 = (bf16[384,512]{1,0:T(8,128)(2,1)S(1)}, bf16[384,512]{1,0:T(8,128)(2,1)}, u32[]{:S(2)}) copy-start(bf16[384,512]{1,0:T(8,128)(2,1)} %shard_map.103) | copy-start | bytes 1179652
  32.5 13.5 %collective-permute-start.4 = (bf16[768,512]{1,0:T(8,128)(2,1)}, bf16[768,512]{1,0:T(8,128)(2,1)S(1)}, u32[]{:S(2)}, u32[]{:S(2)}) collective-permute-start(bf16[768,512]{1,0:T(8,128)(2,1)} %pad_maximum_fusion), channel_id=1, source_target_pairs={{0,1},{1,0},{2,3},{3,2},{4,5},{5,4},{6,7},{7,6},{8,9},{9,8},{10,11... | collective-permute-start | bytes 2359304 | tf_op jit(solution)/shard_map/ppermute | solution.py:108
  34.4 10.9 %collective-permute-start.5 = (bf16[384,512]{1,0:T(8,128)(2,1)S(1)}, bf16[384,512]{1,0:T(8,128)(2,1)S(1)}, u32[]{:S(2)}, u32[]{:S(2)}) collective-permute-start(bf16[384,512]{1,0:T(8,128)(2,1)S(1)} %pad_maximum_fusion.7), channel_id=1, source_target_pairs={{0,24},{1,9},{2,26},{3,11},{4,28},{5,13},{6,30},{7,15},{8,16},{9,1... | collective-permute-start | bytes 1179656 | tf_op jit(solution)/shard_map/ppermute | solution.py:91
  39.9 15.9 %collective-permute-start.6 = (bf16[384,512]{1,0:T(8,128)(2,1)}, bf16[384,512]{1,0:T(8,128)(2,1)S(1)}, u32[]{:S(2)}, u32[]{:S(2)}) collective-permute-start(bf16[384,512]{1,0:T(8,128)(2,1)} %collective-permute-done.3), channel_id=1, source_target_pairs={{0,24},{1,9},{2,26},{3,11},{4,28},{5,13},{6,30},{7,15},{8,16},{9,1... | collective-permute-start | bytes 1179656 | tf_op jit(solution)/shard_map/ppermute | solution.py:92
  45.3 6.0 %copy-start.11 = (bf16[384,512]{1,0:T(8,128)(2,1)}, bf16[384,512]{1,0:T(8,128)(2,1)S(1)}, u32[]{:S(2)}) copy-start(bf16[384,512]{1,0:T(8,128)(2,1)S(1)} %collective-permute-done.5) | copy-start | bytes 1179652
  45.9 9.8 %copy-start.3 = (bf16[192,512]{1,0:T(8,128)(2,1)}, bf16[192,512]{1,0:T(8,128)(2,1)S(1)}, u32[]{:S(2)}) copy-start(bf16[192,512]{1,0:T(8,128)(2,1)S(1)} %get-tuple-element.30) | copy-start | bytes 589828
  46.6 17.4 %collective-permute-start.10 = (bf16[384,512]{1,0:T(8,128)(2,1)}, bf16[384,512]{1,0:T(8,128)(2,1)S(1)}, u32[]{:S(2)}, u32[]{:S(2)}) collective-permute-start(bf16[384,512]{1,0:T(8,128)(2,1)} %shard_map.104), channel_id=1, source_target_pairs={{0,24},{1,9},{2,26},{3,11},{4,28},{5,13},{6,30},{7,15},{8,16},{9,1... | collective-permute-start | bytes 1179656 | tf_op jit(solution)/shard_map/ppermute | solution.py:91
  51.3 9.9 %collective-permute-start.9 = (bf16[384,512]{1,0:T(8,128)(2,1)}, bf16[384,512]{1,0:T(8,128)(2,1)S(1)}, u32[]{:S(2)}, u32[]{:S(2)}) collective-permute-start(bf16[384,512]{1,0:T(8,128)(2,1)} %shard_map.104), channel_id=1, source_target_pairs={{0,8},{1,25},{2,10},{3,27},{4,12},{5,29},{6,14},{7,31},{8,0},{9,17... | collective-permute-start | bytes 1179656 | tf_op jit(solution)/shard_map/ppermute | solution.py:90
  53.3 1.5 copy-start.12
  56.3 17.6 %collective-permute-start.7 = (f32[2,256,256]{2,1,0:T(8,128)S(1)}, f32[2,256,256]{2,1,0:T(8,128)S(1)}, u32[]{:S(2)}, u32[]{:S(2)}) collective-permute-start(f32[2,256,256]{2,1,0:T(8,128)S(1)} %pad_maximum_fusion.1), channel_id=1, source_target_pairs={{0,2},{1,7},{2,0},{3,5},{4,6},{5,3},{6,4},{7,1},{8,10},{9,15},{10,... | collective-permute-start | bytes 1572872 | tf_op jit(solution)/shard_map/ppermute | solution.py:126
  61.2 14.3 %collective-permute-start.11 = (bf16[384,512]{1,0:T(8,128)(2,1)S(1)}, bf16[384,512]{1,0:T(8,128)(2,1)}, u32[]{:S(2)}, u32[]{:S(2)}) collective-permute-start(bf16[384,512]{1,0:T(8,128)(2,1)S(1)} %collective-permute-done.9), channel_id=1, source_target_pairs={{0,24},{1,9},{2,26},{3,11},{4,28},{5,13},{6,30},{7,15},{8,16},{9,1... | collective-permute-start | bytes 1179656 | tf_op jit(solution)/shard_map/ppermute | solution.py:92
  64.0 1.0 copy-start.2
  65.5 10.0 %copy-start.4 = (bf16[192,512]{1,0:T(8,128)(2,1)S(1)}, bf16[192,512]{1,0:T(8,128)(2,1)}, u32[]{:S(2)}) copy-start(bf16[192,512]{1,0:T(8,128)(2,1)} %copy-done.3) | copy-start | bytes 589828
  74.0 0.8 copy-start.9
  74.8 0.7 copy-start.13
  77.0 2.2 %copy-start.14 = (f32[256,256]{1,0:T(8,128)S(1)}, f32[256,256]{1,0:T(8,128)}, u32[]{:S(2)}) copy-start(f32[256,256]{1,0:T(8,128)} %copy-done.13) | copy-start | bytes 786436
  77.0 28.3 %copy-start.10 = (f32[2,256,256]{2,1,0:T(8,128)S(1)}, f32[2,256,256]{2,1,0:T(8,128)}, u32[]{:S(2)}) copy-start(f32[2,256,256]{2,1,0:T(8,128)} %copy-done.9) | copy-start | bytes 1572868
  77.1 23.0 %collective-permute-start.12 = (f32[2,256,256]{2,1,0:T(8,128)S(1)}, f32[2,256,256]{2,1,0:T(8,128)S(1)}, u32[]{:S(2)}, u32[]{:S(2)}) collective-permute-start(f32[2,256,256]{2,1,0:T(8,128)S(1)} %pad_maximum_fusion.2), channel_id=1, source_target_pairs={{0,2},{1,7},{2,0},{3,5},{4,6},{5,3},{6,4},{7,1},{8,10},{9,15},{10,... | collective-permute-start | bytes 1572872 | tf_op jit(solution)/shard_map/ppermute | solution.py:126
  79.2 26.1 %collective-permute-start.8 = (f32[256,256]{1,0:T(8,128)S(1)}, f32[256,256]{1,0:T(8,128)}, u32[]{:S(2)}, u32[]{:S(2)}) collective-permute-start(f32[256,256]{1,0:T(8,128)S(1)} %copy-done.14), channel_id=1, source_target_pairs={{0,6},{1,3},{2,4},{3,1},{4,2},{5,7},{6,0},{7,5},{8,14},{9,11},{10,... | collective-permute-start | bytes 786440 | tf_op jit(solution)/shard_map/ppermute | solution.py:128
  100.8 11.3 %collective-permute-start.13 = (f32[256,256]{1,0:T(8,128)}, f32[256,256]{1,0:T(8,128)}, u32[]{:S(2)}, u32[]{:S(2)}) collective-permute-start(f32[256,256]{1,0:T(8,128)} %fusion.10), channel_id=1, source_target_pairs={{0,6},{1,3},{2,4},{3,1},{4,2},{5,7},{6,0},{7,5},{8,14},{9,11},{10,... | collective-permute-start | bytes 786440 | tf_op jit(solution)/shard_map/ppermute | solution.py:128
  105.3 7.9 %copy-start.6 = (f32[1,1,256,512]{3,2,1,0:T(8,128)S(1)}, f32[1,1,256,512]{3,2,1,0:T(8,128)}, u32[]{:S(2)}) copy-start(f32[1,1,256,512]{3,2,1,0:T(8,128)} %param.11) | copy-start | bytes 1572868
  105.3 7.9 %copy-start.7 = (f32[1,1,256,512]{3,2,1,0:T(8,128)S(1)}, f32[1,1,256,512]{3,2,1,0:T(8,128)}, u32[]{:S(2)}) copy-start(f32[1,1,256,512]{3,2,1,0:T(8,128)} %param.10) | copy-start | bytes 1572868
  113.2 1.2 copy-start.8
  114.7 24.6 %copy-start.15 = (f32[1,16,512]{2,1,0:T(8,128)S(1)}, f32[1,16,512]{2,1,0:T(8,128)}, u32[]{:S(2)}) copy-start(f32[1,16,512]{2,1,0:T(8,128)} %param.12) | copy-start | bytes 98308
  114.7 24.6 %copy-start.16 = (f32[1,16,512]{2,1,0:T(8,128)S(1)}, f32[1,16,512]{2,1,0:T(8,128)}, u32[]{:S(2)}) copy-start(f32[1,16,512]{2,1,0:T(8,128)} %param.13) | copy-start | bytes 98308

commit v4 on v3

--- a/solution.py
+++ b/solution.py
@@ -2,6 +2,7 @@
 import jax.numpy as jnp
 from jax import lax
 from jax.experimental import pallas as pl
+from jax.experimental.pallas import tpu as pltpu
 from jax.sharding import PartitionSpec as P
 
 STEP = 500
@@ -47,15 +48,15 @@
     return pairs
 
 
-def after(value, *others):
-    others = [lax.slice(t, (0, 0), (16, 128)) for t in others]
+def after(value, other):
     return pl.pallas_call(
         lambda *refs: None,
         out_shape=jax.ShapeDtypeStruct(value.shape, value.dtype),
-        in_specs=[pl.BlockSpec(memory_space=pl.ANY)] * (1 + len(others)),
+        in_specs=[pl.BlockSpec(memory_space=pl.ANY), pl.BlockSpec(memory_space=pltpu.VMEM)],
         out_specs=pl.BlockSpec(memory_space=pl.ANY),
         input_output_aliases={0: 0},
-    )(value, *others)
+        cost_estimate=pl.CostEstimate(flops=1 << 36, bytes_accessed=0, transcendentals=0),
+    )(value, other)
 
 
 def body(acts, upstream, inner_params, first_moment, second_moment, anchor, outer_momentum):
@@ -74,48 +75,44 @@
     def a_for(dest):
         return lax.dynamic_slice(a, (0, dest * 2 * rows), (count, 2 * rows))
 
-    def u_for(core, j):
+    def u_for(j):
+        at = [(k * 2 + core) * cols + j * width for core in range(2) for k in range(2)]
+        parts = [u[:, i : i + width] for i in at]
         return jnp.concatenate(
-            [
-                lax.dynamic_slice(u, (0, (k * 2 + core) * cols + j * width), (count, width))
-                for k in range(2)
-            ],
-            1,
+            [jnp.concatenate(parts[:2], 1), jnp.concatenate(parts[2:], 1)], 0
         )
 
     def pieces(t):
         return [t[i * count : (i + 1) * count] for i in range(t.shape[0] // count)]
 
-    def gather_x(mine):
-        one = lax.ppermute(mine, "fsdp", x_pairs(0))
-        two = lax.ppermute(mine, "fsdp", x_pairs(1))
-        return mine, one, two, lax.ppermute(one, "fsdp", x_pairs(1))
+    u_zero = u_for(0)
+    one = lax.ppermute(
+        jnp.concatenate([a_for(x ^ near), u_zero, a_for(x ^ 2)], 0), "fsdp", x_pairs(0)
+    )
+    two = lax.ppermute(jnp.concatenate([u_zero, a_for(x ^ far)], 0), "fsdp", x_pairs(1))
+    three = lax.ppermute(one[count:], "fsdp", x_pairs(1))
+    a_chips = [a_for(x), one[:count], two[2 * count :], three[2 * count :]]
+    zero = [u_zero, one[count : 3 * count], two[: 2 * count], three[: 2 * count]]
 
-    swap = lax.ppermute(
-        jnp.concatenate([u_for(1 - c, j) for j in range(halves)], 0), "fsdp", core_pairs()
-    )
-    a_one = lax.ppermute(jnp.concatenate([a_for(x ^ near), a_for(x ^ 2)], 0), "fsdp", x_pairs(0))
-    a_one = after(a_one, swap)
-    a_two = lax.ppermute(
-        jnp.concatenate([a_for(x ^ far), a_one[count:]], 0), "fsdp", x_pairs(1)
-    )
-    mine = [
-        jnp.concatenate([u_for(c, j), swap[j * count : (j + 1) * count]], 0) for j in range(halves)
-    ]
-    first = gather_x(mine[0])
-    a_two = after(a_two, first[1])
-    a_core = jnp.concatenate([a_for(x), a_one[:count], a_two], 0)
-    a_other = lax.ppermute(a_core, "fsdp", core_pairs())
-    own, other = pieces(a_core), pieces(a_other)
-    a_chips = [jnp.concatenate([own[i], other[j]], 0) for i, j in enumerate((0, 2, 1, 3))]
+    u_one = after(u_for(1), one)
+    next_one = lax.ppermute(u_one, "fsdp", x_pairs(0))
+    next_two = lax.ppermute(after(u_one, three), "fsdp", x_pairs(1))
+    next_three = lax.ppermute(after(next_one, three), "fsdp", x_pairs(1))
 
-    def chunk_sum(gathered):
-        return sum(
-            lax.dot_general(
-                left, right, (((0,), (0,)), ((), ())), preferred_element_type=jnp.float32
+    def chunk_sum(gathered, behind=None):
+        def half(core):
+            return sum(
+                lax.dot_general(
+                    left,
+                    lax.dynamic_slice(right, (core * count, 0), (count, cols)),
+                    (((0,), (0,)), ((), ())),
+                    preferred_element_type=jnp.float32,
+                )
+                for left, right in zip(a_chips, gathered)
             )
-            for left, right in zip(a_chips, gathered)
-        )
+
+        arrived = lax.ppermute(half(1 - c), "fsdp", core_pairs())
+        return half(c) + (arrived if behind is None else after(arrived, behind))
 
     def reduce_y(whole):
         def part(dest):
@@ -124,18 +121,18 @@
             )
 
         g_one = lax.ppermute(jnp.stack([part(y ^ 2), part(y ^ near)]), "fsdp", y_pairs(0))
-        passed_on = part(y ^ far) + g_one[0]
-        g_two = lax.ppermute(passed_on, "fsdp", y_pairs(1))
-        return part(y) + g_one[1] + g_two, passed_on
+        g_two = lax.ppermute(part(y ^ far) + g_one[0], "fsdp", y_pairs(1))
+        return part(y) + g_one[1] + g_two, g_one
 
     fix_one = 1.0 - beta_one**STEP
     fix_two = 1.0 - beta_two**STEP
     slice_rows = rows // members
 
-    second = gather_x(after(mine[1], first[2], a_other))
-    near_done, token = reduce_y(chunk_sum(first))
-    far_done, _ = reduce_y(chunk_sum((*second[:3], after(second[3], token))))
-    gradient = jnp.concatenate([near_done, far_done], 1)
+    sum_zero = chunk_sum(zero)
+    done_zero, g_zero = reduce_y(sum_zero)
+    next_three = after(next_three, sum_zero)
+    done_one, _ = reduce_y(chunk_sum([u_one, next_one, next_two, next_three], g_zero))
+    gradient = jnp.concatenate([done_zero, done_one], 1)
 
     params = inner_params[0, 0]
     moment_one = beta_one * first_moment[0, 0] + (1.0 - beta_one) * gradient

time: 162 us -> 184 us (1.14)
  the two profiles are of different devices: /device:TPU:24 before, /device:TPU:72 now
where the time goes in v4:
time: 184 us; the launch traced here: 183 us
  blocking collectives  48.5 us (26%)
  starting transfers between devices  45.3 us (25%)
  waiting for transfers between devices  40.4 us (22%)
  matrix products  24.9 us (14%)
  local copies, waits for them, and re-layouts  8.85 us (5%)
  other arithmetic  7.8 us (4%)
  Pallas kernels  5.54 us (3%)
    all_to_all x1, blocking collectives, body(): lax.all_to_all(stepped.reshape(members, slice_rows, cols), 'replica', spl...  27.7 us
    dot_general x16, matrix products, half(): lax.dot_general(left, lax.dynamic_slice(right, (core * count, 0), (count,...  24.9 us
    all_to_all x1, blocking collectives, body(): lax.all_to_all(jnp.broadcast_to(new_params[None], (members, slice_rows, c...  20.9 us
    ppermute x2, waiting for transfers between devices, reduce_y(): lax.ppermute(jnp.stack([part(y ^ 2), part(y ^ near)]), 'fsdp', y_pairs(0))  18.6 us
    ppermute x2, starting transfers between devices, reduce_y(): lax.ppermute(jnp.stack([part(y ^ 2), part(y ^ near)]), 'fsdp', y_pairs(0))  9.94 us
    ppermute x1, waiting for transfers between devices, body(): lax.ppermute(jnp.concatenate([u_zero, a_for(x ^ far)], 0), 'fsdp', x_pair...  9.87 us
    ppermute x2, starting transfers between devices, reduce_y(): g_two = lax.ppermute(part(y ^ far) + g_one[0], 'fsdp', y_pairs(1))  9.08 us
    pallas_call x5, Pallas kernels, after(): pl.pallas_call(lambda *refs: None, out_shape=jax.ShapeDtypeStruct(value.s...  5.54 us
  transfers between devices with their start and end apart: 12, of which 7 were waited for; matrix products, arithmetic and copies ran while one was open for 12% of the time, Pallas kernels for 2%

profile of v4, /device:TPU:72, one launch (start us, length us, event | category | flops | bytes accessed | tf_op | source)
XLA Modules:
  0.0 182.5 jit_solution(7686482670282825933)
XLA Ops:
  0.6 0.0 copy-start.7
  0.7 1.3 fusion.84
  2.0 0.1 copy-done.7
  2.2 1.0 pad_maximum_fusion
  3.1 3.4 %collective-permute-start = (bf16[768,512]{1,0:T(8,128)(2,1)}, bf16[768,512]{1,0:T(8,128)(2,1)S(1)}, u32[]{:S(2)}, u32[]{:S(2)}) collective-permute-start(bf16[768,512]{1,0:T(8,128)(2,1)} %pad_maximum_fusion), channel_id=1, source_target_pairs={{0,8},{1,25},{2,10},{3,27},{4,12},{5,29},{6,14},{7,31},{8,0},{9,17... | collective-permute-start | bytes 2359304 | tf_op jit(solution)/shard_map/ppermute | solution.py:89
  6.5 0.9 pad_maximum_fusion.1
  7.4 4.0 %collective-permute-start.1 = (bf16[576,512]{1,0:T(8,128)(2,1)}, bf16[576,512]{1,0:T(8,128)(2,1)}, u32[]{:S(2)}, u32[]{:S(2)}) collective-permute-start(bf16[576,512]{1,0:T(8,128)(2,1)} %pad_maximum_fusion.1), channel_id=1, source_target_pairs={{0,24},{1,9},{2,26},{3,11},{4,28},{5,13},{6,30},{7,15},{8,16},{9,1... | collective-permute-start | bytes 1769480 | tf_op jit(solution)/shard_map/ppermute | solution.py:92
  11.5 0.8 maximum_maximum_fusion.1.refs_0_
  12.2 0.3 fusion.24
  12.6 1.3 fusion.26
  13.8 9.9 %collective-permute-done.1 = bf16[576,512]{1,0:T(8,128)(2,1)} collective-permute-done((bf16[576,512]{1,0:T(8,128)(2,1)}, bf16[576,512]{1,0:T(8,128)(2,1)}, u32[]{:S(2)}, u32[]{:S(2)}) %collective-permute-start.1) | collective-permute-done | bytes 589856 | tf_op jit(solution)/shard_map/ppermute | solution.py:92
  23.7 1.0 slice.83
  24.8 0.9 slice.84
  25.7 4.7 %collective-permute-start.2 = (bf16[576,512]{1,0:T(8,128)(2,1)}, bf16[576,512]{1,0:T(8,128)(2,1)}, u32[]{:S(2)}, u32[]{:S(2)}) collective-permute-start(bf16[576,512]{1,0:T(8,128)(2,1)} %slice.84), channel_id=1, source_target_pairs={{0,24},{1,9},{2,26},{3,11},{4,28},{5,13},{6,30},{7,15},{8,16},{9,1... | collective-permute-start | bytes 1769480 | tf_op jit(solution)/shard_map/ppermute | solution.py:93
  30.3 1.1 shard_map.102
  31.5 1.9 %collective-permute-start.6 = (bf16[384,512]{1,0:T(8,128)(2,1)}, bf16[384,512]{1,0:T(8,128)(2,1)S(1)}, u32[]{:S(2)}, u32[]{:S(2)}) collective-permute-start(bf16[384,512]{1,0:T(8,128)(2,1)} %shard_map.102), channel_id=1, source_target_pairs={{0,8},{1,25},{2,10},{3,27},{4,12},{5,29},{6,14},{7,31},{8,0},{9,17... | collective-permute-start | bytes 1179656 | tf_op jit(solution)/shard_map/ppermute | solution.py:98
  33.4 1.0 slice.81
  34.4 1.3 convolution_add_fusion.3
  35.8 0.3 convolution_add_fusion.5
  36.1 0.6 copy-done.5
  36.8 0.7 copy.19.refs_0_
  37.5 3.8 %collective-permute-done.6.refs_0_ = bf16[384,512]{1,0:T(8,128)(2,1)S(1)} collective-permute-done((bf16[384,512]{1,0:T(8,128)(2,1)}, bf16[384,512]{1,0:T(8,128)(2,1)S(1)}, u32[]{:S(2)}, u32[]{:S(2)}) %collective-permute-start.6) | collective-permute-done | bytes 393248 | tf_op jit(solution)/shard_map/ppermute | solution.py:98
  41.4 1.3 fusion.32
  42.7 1.3 fusion.39
  44.0 1.0 slice.86
  45.0 1.3 fusion.42
  46.3 2.2 %fusion.5 = f32[512,512]{1,0:T(8,128)} fusion(f32[512,512]{1,0:T(8,128)S(1)} %fusion.42, f32[512,512]{1,0:T(8,128)S(1)} %convolution_add_fusion.3, bf16[384,512]{1,0:T(8,128)(2,1)S(1)} %slice.83, s32[]{:T(128)S(6)} %select_n.78, bf16[576,512]{1,0:T(8,128)(2,1)} %collective-permute-done.1), kind=kOutput, calls=%fused_computation.8 | convolution fusion | flops 101187584 | bytes 3538948 | tf_op jit(solution)/shard_map/dot_general | solution.py:105
  48.5 3.4 %collective-permute-start.3 = (f32[512,512]{1,0:T(8,128)}, f32[512,512]{1,0:T(8,128)S(1)}, u32[]{:S(2)}, u32[]{:S(2)}) collective-permute-start(f32[512,512]{1,0:T(8,128)} %fusion.5), channel_id=1, source_target_pairs={{0,1},{1,0},{2,3},{3,2},{4,5},{5,4},{6,7},{7,6},{8,9},{9,8},{10,11... | collective-permute-start | bytes 3145736 | tf_op jit(solution)/shard_map/ppermute | solution.py:114
  52.0 1.1 shard_map.103
  53.0 4.7 %collective-permute-start.7 = (bf16[384,512]{1,0:T(8,128)(2,1)}, bf16[384,512]{1,0:T(8,128)(2,1)}, u32[]{:S(2)}, u32[]{:S(2)}) collective-permute-start(bf16[384,512]{1,0:T(8,128)(2,1)} %shard_map.103), channel_id=1, source_target_pairs={{0,24},{1,9},{2,26},{3,11},{4,28},{5,13},{6,30},{7,15},{8,16},{9,1... | collective-permute-start | bytes 1179656 | tf_op jit(solution)/shard_map/ppermute | solution.py:99
  57.7 1.1 shard_map.104
  58.8 2.4 %collective-permute-start.8 = (bf16[384,512]{1,0:T(8,128)(2,1)}, bf16[384,512]{1,0:T(8,128)(2,1)}, u32[]{:S(2)}, u32[]{:S(2)}) collective-permute-start(bf16[384,512]{1,0:T(8,128)(2,1)} %shard_map.104), channel_id=1, source_target_pairs={{0,24},{1,9},{2,26},{3,11},{4,28},{5,13},{6,30},{7,15},{8,16},{9,1... | collective-permute-start | bytes 1179656 | tf_op jit(solution)/shard_map/ppermute | solution.py:100
  61.2 1.3 fusion.47
  62.4 1.8 collective-permute-done.7
  64.2 1.4 fusion.30
  65.6 2.2 %fusion.7.refs_1_ = f32[512,512]{1,0:T(8,128)} fusion(f32[512,512]{1,0:T(8,128)S(1)} %collective-permute-done.3, f32[512,512]{1,0:T(8,128)S(1)} %fusion.47, f32[512,512]{1,0:T(8,128)S(1)} %convolution_add_fusion.5, bf16[384,512]{1,0:T(8,128)(2,1)S(1)} %slice.83, s32[]{:T(128)S(6)} %select_n.36, bf16[576,512]{1,0:T(8,128)(2,1)} %collective-permute-done.1), kind=kOutput, calls=%fused_computation.12 | convolution fusion | flops 101449728 | bytes 4587524 | tf_op jit(solution)/shard_map/dot_general | solution.py:105
  67.8 2.1 %collective-permute-done.8.refs_0_ = bf16[384,512]{1,0:T(8,128)(2,1)} collective-permute-done((bf16[384,512]{1,0:T(8,128)(2,1)}, bf16[384,512]{1,0:T(8,128)(2,1)}, u32[]{:S(2)}, u32[]{:S(2)}) %collective-permute-start.8) | collective-permute-done | bytes 393248 | tf_op jit(solution)/shard_map/ppermute | solution.py:100
  70.0 1.2 shard_map.105
  71.2 1.5 fusion.28
  72.7 0.0 copy-done.6
  72.7 2.3 %fusion.1 = f32[512,512]{1,0:T(8,128)} fusion(f32[512,512]{1,0:T(8,128)S(1)} %fusion.28, f32[512,512]{1,0:T(8,128)S(1)} %fusion.30, f32[512,512]{1,0:T(8,128)S(1)} %copy-done.1, bf16[384,512]{1,0:T(8,128)(2,1)S(1)} %copy-done.6, s32[]{:T(128)S(6)} %select_n.78, bf16[1,192,2048]{2,1,0:T(8,128)(2,1)} %param.7, s32[]{:T(128)S(6)} %select_n.35), kind=kOutput, calls=%fused_computation.2 | convolution fusion | flops 101449728 | bytes 4587528 | tf_op jit(solution)/shard_map/dot_general | solution.py:105
  75.0 1.9 %collective-permute-start.9 = (f32[512,512]{1,0:T(8,128)}, f32[512,512]{1,0:T(8,128)S(1)}, u32[]{:S(2)}, u32[]{:S(2)}) collective-permute-start(f32[512,512]{1,0:T(8,128)} %fusion.1), channel_id=1, source_target_pairs={{0,1},{1,0},{2,3},{3,2},{4,5},{5,4},{6,7},{7,6},{8,9},{9,8},{10,11... | collective-permute-start | bytes 3145736 | tf_op jit(solution)/shard_map/ppermute | solution.py:114
  77.1 4.5 %collective-permute-start.4 = (f32[2,256,256]{2,1,0:T(8,128)S(1)}, f32[2,256,256]{2,1,0:T(8,128)}, u32[]{:S(2)}, u32[]{:S(2)}) collective-permute-start(f32[2,256,256]{2,1,0:T(8,128)S(1)} %pad_maximum_fusion.2), channel_id=1, source_target_pairs={{0,2},{1,7},{2,0},{3,5},{4,6},{5,3},{6,4},{7,1},{8,10},{9,15},{10,... | collective-permute-start | bytes 1572872 | tf_op jit(solution)/shard_map/ppermute | solution.py:123
  81.6 2.3 %fusion.37 = f32[512,512]{1,0:T(8,128)} fusion(bf16[384,512]{1,0:T(8,128)(2,1)} %collective-permute-done.7, s32[]{:T(128)S(6)} %select_n.36, bf16[576,512]{1,0:T(8,128)(2,1)} %collective-permute-done.1), kind=kOutput, calls=%fused_computation.64 | convolution fusion | flops 100663296 | bytes 1441796 | tf_op jit(solution)/shard_map/dot_general | solution.py:105
  83.9 2.3 %fusion.35 = f32[512,512]{1,0:T(8,128)} fusion(bf16[384,512]{1,0:T(8,128)(2,1)} %shard_map.105, s32[]{:T(128)S(6)} %select_n.36, bf16[576,512]{1,0:T(8,128)(2,1)} %collective-permute-done.2.refs_1_), kind=kOutput, calls=%fused_computation.62 | convolution fusion | flops 100663296 | bytes 1441796 | tf_op jit(solution)/shard_map/dot_general | solution.py:105
  86.2 7.6 %collective-permute-done.4.refs_1_ = f32[2,256,256]{2,1,0:T(8,128)} collective-permute-done((f32[2,256,256]{2,1,0:T(8,128)S(1)}, f32[2,256,256]{2,1,0:T(8,128)}, u32[]{:S(2)}, u32[]{:S(2)}) %collective-permute-start.4) | collective-permute-done | bytes 524320 | tf_op jit(solution)/shard_map/ppermute | solution.py:123
  93.8 1.0 copy-done.8
  94.8 1.0 shard_map.106
  95.9 2.3 %fusion.4 = f32[512,512]{1,0:T(8,128)S(1)} fusion(f32[512,512]{1,0:T(8,128)} %shard_map.106, f32[512,512]{1,0:T(8,128)} %fusion.35, f32[512,512]{1,0:T(8,128)} %fusion.37, f32[512,512]{1,0:T(8,128)S(1)} %copy-done.2, bf16[384,512]{1,0:T(8,128)(2,1)S(1)} %copy-done.6, s32[]{:T(128)S(6)} %select_n.36, bf16[1,192,2048]{2,1,0:T(8,128)(2,1)} %param.7, ...), kind=kOutput, calls=%fused_computation.6 | convolution fusion | flops 101711872 | bytes 5636104 | tf_op jit(solution)/shard_map/dot_general | solution.py:105
  98.2 0.1 dynamic-slice_bitcast_fusion.1
  98.3 5.4 %collective-permute-start.10 = (f32[2,256,256]{2,1,0:T(8,128)S(1)}, f32[2,256,256]{2,1,0:T(8,128)S(1)}, u32[]{:S(2)}, u32[]{:S(2)}) collective-permute-start(f32[2,256,256]{2,1,0:T(8,128)S(1)} %pad_maximum_fusion.3), channel_id=1, source_target_pairs={{0,2},{1,7},{2,0},{3,5},{4,6},{5,3},{6,4},{7,1},{8,10},{9,15},{10,... | collective-permute-start | bytes 1572872 | tf_op jit(solution)/shard_map/ppermute | solution.py:123
  103.7 1.7 fusion.19
  105.4 2.7 %collective-permute-start.5 = (f32[256,256]{1,0:T(8,128)}, f32[256,256]{1,0:T(8,128)S(1)}, u32[]{:S(2)}, u32[]{:S(2)}) collective-permute-start(f32[256,256]{1,0:T(8,128)} %fusion.19), channel_id=1, source_target_pairs={{0,6},{1,3},{2,4},{3,1},{4,2},{5,7},{6,0},{7,5},{8,14},{9,11},{10,... | collective-permute-start | bytes 786440 | tf_op jit(solution)/shard_map/ppermute | solution.py:124
  108.1 11.0 %collective-permute-done.10 = f32[2,256,256]{2,1,0:T(8,128)S(1)} collective-permute-done((f32[2,256,256]{2,1,0:T(8,128)S(1)}, f32[2,256,256]{2,1,0:T(8,128)S(1)}, u32[]{:S(2)}, u32[]{:S(2)}) %collective-permute-start.10) | collective-permute-done | bytes 524320 | tf_op jit(solution)/shard_map/ppermute | solution.py:123
  119.1 6.4 %collective-permute-start.11 = (f32[256,256]{1,0:T(8,128)S(1)}, f32[256,256]{1,0:T(8,128)S(1)}, u32[]{:S(2)}, u32[]{:S(2)}) collective-permute-start(f32[256,256]{1,0:T(8,128)S(1)} %fusion.16), channel_id=1, source_target_pairs={{0,6},{1,3},{2,4},{3,1},{4,2},{5,7},{6,0},{7,5},{8,14},{9,11},{10,... | collective-permute-start | bytes 786440 | tf_op jit(solution)/shard_map/ppermute | solution.py:124
  125.6 1.1 fusion.21
  126.7 4.1 %collective-permute-done.11 = f32[256,256]{1,0:T(8,128)S(1)} collective-permute-done((f32[256,256]{1,0:T(8,128)S(1)}, f32[256,256]{1,0:T(8,128)S(1)}, u32[]{:S(2)}, u32[]{:S(2)}) %collective-permute-start.11) | collective-permute-done | bytes 262176 | tf_op jit(solution)/shard_map/ppermute | solution.py:124
  130.8 0.1 fusion.18
  130.9 1.2 fusion.15
  132.1 0.3 fusion.14
  132.5 27.7 %all_to_all.10 = f32[16,16,512]{2,1,0:T(8,128)S(1)} all-to-all(f32[16,16,512]{2,1,0:T(8,128)S(1)} %fusion.14), channel_id=1, replica_groups=mesh['replica'=16,'fsdp'=32] {'replica'}, dimensions={0} | all-to-all | bytes 1048576 | tf_op jit(solution)/shard_map/all_to_all | solution.py:144
  160.2 0.6 subtract_bitcast_fusion
  160.9 20.9 %all_to_all.11 = f32[16,16,512]{2,1,0:T(8,128)S(1)} all-to-all(f32[16,16,512]{2,1,0:T(8,128)S(1)} %broadcast_in_dim.5), channel_id=1, replica_groups=mesh['replica'=16,'fsdp'=32] {'replica'}, dimensions={0} | all-to-all | bytes 1048576 | tf_op jit(solution)/shard_map/all_to_all | solution.py:155
  181.7 0.8 copy.22
  (38 shorter events, 0.4 us)
Async XLA Ops:
  0.6 1.5 copy-start.7
  3.1 21.6 %collective-permute-start = (bf16[768,512]{1,0:T(8,128)(2,1)}, bf16[768,512]{1,0:T(8,128)(2,1)S(1)}, u32[]{:S(2)}, u32[]{:S(2)}) collective-permute-start(bf16[768,512]{1,0:T(8,128)(2,1)} %pad_maximum_fusion), channel_id=1, source_target_pairs={{0,8},{1,25},{2,10},{3,27},{4,12},{5,29},{6,14},{7,31},{8,0},{9,17... | collective-permute-start | bytes 2359304 | tf_op jit(solution)/shard_map/ppermute | solution.py:89
  7.4 16.3 %collective-permute-start.1 = (bf16[576,512]{1,0:T(8,128)(2,1)}, bf16[576,512]{1,0:T(8,128)(2,1)}, u32[]{:S(2)}, u32[]{:S(2)}) collective-permute-start(bf16[576,512]{1,0:T(8,128)(2,1)} %pad_maximum_fusion.1), channel_id=1, source_target_pairs={{0,24},{1,9},{2,26},{3,11},{4,28},{5,13},{6,30},{7,15},{8,16},{9,1... | collective-permute-start | bytes 1769480 | tf_op jit(solution)/shard_map/ppermute | solution.py:92
  24.7 5.6 %copy-start.3 = (bf16[768,512]{1,0:T(8,128)(2,1)}, bf16[768,512]{1,0:T(8,128)(2,1)S(1)}, u32[]{:S(2)}) copy-start(bf16[768,512]{1,0:T(8,128)(2,1)S(1)} %collective-permute-done.refs_1_) | copy-start | bytes 2359300
  25.7 18.3 %collective-permute-start.2 = (bf16[576,512]{1,0:T(8,128)(2,1)}, bf16[576,512]{1,0:T(8,128)(2,1)}, u32[]{:S(2)}, u32[]{:S(2)}) collective-permute-start(bf16[576,512]{1,0:T(8,128)(2,1)} %slice.84), channel_id=1, source_target_pairs={{0,24},{1,9},{2,26},{3,11},{4,28},{5,13},{6,30},{7,15},{8,16},{9,1... | collective-permute-start | bytes 1769480 | tf_op jit(solution)/shard_map/ppermute | solution.py:93
  31.5 9.9 %collective-permute-start.6 = (bf16[384,512]{1,0:T(8,128)(2,1)}, bf16[384,512]{1,0:T(8,128)(2,1)S(1)}, u32[]{:S(2)}, u32[]{:S(2)}) collective-permute-start(bf16[384,512]{1,0:T(8,128)(2,1)} %shard_map.102), channel_id=1, source_target_pairs={{0,8},{1,25},{2,10},{3,27},{4,12},{5,29},{6,14},{7,31},{8,0},{9,17... | collective-permute-start | bytes 1179656 | tf_op jit(solution)/shard_map/ppermute | solution.py:98
  34.4 1.4 copy-start.4
  35.8 1.0 copy-start.5
  41.4 2.6 %copy-start.12 = (bf16[384,512]{1,0:T(8,128)(2,1)}, bf16[384,512]{1,0:T(8,128)(2,1)S(1)}, u32[]{:S(2)}) copy-start(bf16[384,512]{1,0:T(8,128)(2,1)S(1)} %collective-permute-done.6.refs_0_) | copy-start | bytes 1179652
  48.5 17.1 %collective-permute-start.3 = (f32[512,512]{1,0:T(8,128)}, f32[512,512]{1,0:T(8,128)S(1)}, u32[]{:S(2)}, u32[]{:S(2)}) collective-permute-start(f32[512,512]{1,0:T(8,128)} %fusion.5), channel_id=1, source_target_pairs={{0,1},{1,0},{2,3},{3,2},{4,5},{5,4},{6,7},{7,6},{8,9},{9,8},{10,11... | collective-permute-start | bytes 3145736 | tf_op jit(solution)/shard_map/ppermute | solution.py:114
  53.0 11.2 %collective-permute-start.7 = (bf16[384,512]{1,0:T(8,128)(2,1)}, bf16[384,512]{1,0:T(8,128)(2,1)}, u32[]{:S(2)}, u32[]{:S(2)}) collective-permute-start(bf16[384,512]{1,0:T(8,128)(2,1)} %shard_map.103), channel_id=1, source_target_pairs={{0,24},{1,9},{2,26},{3,11},{4,28},{5,13},{6,30},{7,15},{8,16},{9,1... | collective-permute-start | bytes 1179656 | tf_op jit(solution)/shard_map/ppermute | solution.py:99
  58.8 11.2 %collective-permute-start.8 = (bf16[384,512]{1,0:T(8,128)(2,1)}, bf16[384,512]{1,0:T(8,128)(2,1)}, u32[]{:S(2)}, u32[]{:S(2)}) collective-permute-start(bf16[384,512]{1,0:T(8,128)(2,1)} %shard_map.104), channel_id=1, source_target_pairs={{0,24},{1,9},{2,26},{3,11},{4,28},{5,13},{6,30},{7,15},{8,16},{9,1... | collective-permute-start | bytes 1179656 | tf_op jit(solution)/shard_map/ppermute | solution.py:100
  71.2 1.5 copy-start.1
  71.2 1.5 copy-start.6
  72.7 4.3 %copy-start = (f32[512,512]{1,0:T(8,128)S(1)}, f32[512,512]{1,0:T(8,128)}, u32[]{:S(2)}) copy-start(f32[512,512]{1,0:T(8,128)} %fusion.7.refs_1_) | copy-start | bytes 3145732
  75.0 18.8 %collective-permute-start.9 = (f32[512,512]{1,0:T(8,128)}, f32[512,512]{1,0:T(8,128)S(1)}, u32[]{:S(2)}, u32[]{:S(2)}) collective-permute-start(f32[512,512]{1,0:T(8,128)} %fusion.1), channel_id=1, source_target_pairs={{0,1},{1,0},{2,3},{3,2},{4,5},{5,4},{6,7},{7,6},{8,9},{9,8},{10,11... | collective-permute-start | bytes 3145736 | tf_op jit(solution)/shard_map/ppermute | solution.py:114
  77.1 16.8 %collective-permute-start.4 = (f32[2,256,256]{2,1,0:T(8,128)S(1)}, f32[2,256,256]{2,1,0:T(8,128)}, u32[]{:S(2)}, u32[]{:S(2)}) collective-permute-start(f32[2,256,256]{2,1,0:T(8,128)S(1)} %pad_maximum_fusion.2), channel_id=1, source_target_pairs={{0,2},{1,7},{2,0},{3,5},{4,6},{5,3},{6,4},{7,1},{8,10},{9,15},{10,... | collective-permute-start | bytes 1572872 | tf_op jit(solution)/shard_map/ppermute | solution.py:123
  86.2 9.7 %copy-start.2 = (f32[512,512]{1,0:T(8,128)S(1)}, f32[512,512]{1,0:T(8,128)}, u32[]{:S(2)}) copy-start(f32[512,512]{1,0:T(8,128)} %fusion.39) | copy-start | bytes 3145732
  93.8 1.0 copy-start.8
  98.3 20.8 %collective-permute-start.10 = (f32[2,256,256]{2,1,0:T(8,128)S(1)}, f32[2,256,256]{2,1,0:T(8,128)S(1)}, u32[]{:S(2)}, u32[]{:S(2)}) collective-permute-start(f32[2,256,256]{2,1,0:T(8,128)S(1)} %pad_maximum_fusion.3), channel_id=1, source_target_pairs={{0,2},{1,7},{2,0},{3,5},{4,6},{5,3},{6,4},{7,1},{8,10},{9,15},{10,... | collective-permute-start | bytes 1572872 | tf_op jit(solution)/shard_map/ppermute | solution.py:123
  105.4 20.2 %collective-permute-start.5 = (f32[256,256]{1,0:T(8,128)}, f32[256,256]{1,0:T(8,128)S(1)}, u32[]{:S(2)}, u32[]{:S(2)}) collective-permute-start(f32[256,256]{1,0:T(8,128)} %fusion.19), channel_id=1, source_target_pairs={{0,6},{1,3},{2,4},{3,1},{4,2},{5,7},{6,0},{7,5},{8,14},{9,11},{10,... | collective-permute-start | bytes 786440 | tf_op jit(solution)/shard_map/ppermute | solution.py:124
  119.1 11.7 %collective-permute-start.11 = (f32[256,256]{1,0:T(8,128)S(1)}, f32[256,256]{1,0:T(8,128)S(1)}, u32[]{:S(2)}, u32[]{:S(2)}) collective-permute-start(f32[256,256]{1,0:T(8,128)S(1)} %fusion.16), channel_id=1, source_target_pairs={{0,6},{1,3},{2,4},{3,1},{4,2},{5,7},{6,0},{7,5},{8,14},{9,11},{10,... | collective-permute-start | bytes 786440 | tf_op jit(solution)/shard_map/ppermute | solution.py:124
  125.6 5.3 %copy-start.9 = (f32[1,1,256,512]{3,2,1,0:T(8,128)S(1)}, f32[1,1,256,512]{3,2,1,0:T(8,128)}, u32[]{:S(2)}) copy-start(f32[1,1,256,512]{3,2,1,0:T(8,128)} %param.11) | copy-start | bytes 1572868
  125.6 5.3 %copy-start.10 = (f32[1,1,256,512]{3,2,1,0:T(8,128)S(1)}, f32[1,1,256,512]{3,2,1,0:T(8,128)}, u32[]{:S(2)}) copy-start(f32[1,1,256,512]{3,2,1,0:T(8,128)} %param.10) | copy-start | bytes 1572868
  130.9 1.2 copy-start.11
  132.4 27.7 %copy-start.13 = (f32[1,16,512]{2,1,0:T(8,128)S(1)}, f32[1,16,512]{2,1,0:T(8,128)}, u32[]{:S(2)}) copy-start(f32[1,16,512]{2,1,0:T(8,128)} %param.12) | copy-start | bytes 98308
  132.4 27.7 %copy-start.14 = (f32[1,16,512]{2,1,0:T(8,128)S(1)}, f32[1,16,512]{2,1,0:T(8,128)}, u32[]{:S(2)}) copy-start(f32[1,16,512]{2,1,0:T(8,128)} %param.13) | copy-start | bytes 98308

commit v5 on v2

--- a/solution.py
+++ b/solution.py
@@ -90,10 +90,11 @@
             left, right, (((0,), (0,)), ((), ())), preferred_element_type=jnp.float32
         )
 
-    g_sent = jnp.stack([part(y ^ far ^ near), part(y ^ near)])
-    g_one = lax.ppermute(g_sent, "fsdp", y_pairs(0))
-    g_two = lax.ppermute(part(y ^ far) + g_one[0], "fsdp", y_pairs(1))
-    gradient = part(y) + g_one[1] + g_two
+    g_far = lax.ppermute(part(y ^ 2), "fsdp", y_pairs(0))
+    g_near = lax.ppermute(part(y ^ near), "fsdp", y_pairs(0))
+    kept_far, kept = lax.optimization_barrier((part(y ^ far), part(y)))
+    g_two = lax.ppermute(kept_far + g_far, "fsdp", y_pairs(1))
+    gradient = kept + g_near + g_two
 
     fix_one = 1.0 - beta_one**STEP
     fix_two = 1.0 - beta_two**STEP

time: 149 us -> 137 us (0.919)
  the two profiles are of different devices: /device:TPU:104 before, /device:TPU:72 now
where the time goes in v5:
time: 137 us
  blocking collectives  49.7 us (36%)
  starting transfers between devices  36.2 us (26%)
  waiting for transfers between devices  31.7 us (23%)
  local copies, waits for them, and re-layouts  9.47 us (7%)
  matrix products  5.46 us (4%)
  other arithmetic  3.1 us (2%)
    all_to_all x1, blocking collectives, body(): lax.all_to_all(stepped.reshape(members, slice_rows, cols), 'replica', spl...  28.8 us
    all_to_all x1, blocking collectives, body(): lax.all_to_all(jnp.broadcast_to(new_params[None], (members, slice_rows, c...  20.9 us
    ppermute x1, waiting for transfers between devices, body(): g_near = lax.ppermute(part(y ^ near), 'fsdp', y_pairs(0))  9.25 us
    ppermute x1, waiting for transfers between devices, body(): g_far = lax.ppermute(part(y ^ 2), 'fsdp', y_pairs(0))  8.03 us
    unnamed x37, local copies, waits for them, and re-layouts  6.06 us
    dot_general x4, matrix products, part(): lax.dot_general(left, right, (((0,), (0,)), ((), ())), preferred_element_...  5.46 us
    ppermute x1, waiting for transfers between devices, body(): g_two = lax.ppermute(kept_far + g_far, 'fsdp', y_pairs(1))  4.88 us
    ppermute x1, waiting for transfers between devices, body(): three = lax.ppermute(one[count:], 'fsdp', x_pairs(1))  4.64 us
  transfers between devices with their start and end apart: 11, of which 6 were waited for; matrix products, arithmetic and copies ran while one was open for 7% of the time, Pallas kernels for 0%

profile of v5, /device:TPU:72, one launch (start us, length us, event | category | flops | bytes accessed | tf_op | source)
XLA Modules:
  0.0 136.7 jit_solution(6252553126370734316)
XLA Ops:
  0.6 0.0 copy-start.1
  0.7 1.9 %constant_dynamic-update-slice_fusion.5 = (bf16[1536,512]{1,0:T(8,128)(2,1)}, bf16[192,512]{1,0:T(8,128)(2,1)S(1)}, bf16[1536,512]{1,0:T(8,128)(2,1)}, bf16[192,512]{1,0:T(8,128)(2,1)S(1)}) fusion(bf16[1,192,2048]{2,1,0:T(8,128)(2,1)} %param.8, s32[]{:T(128)S(6)} %select_n.59, s32[]{:T(128)S(6)} %select_n.58), kind=kLoop, calls=%fused_computation.65 | loop fusion | bytes 1179656
  2.6 0.0 copy-done.1
  2.6 0.1 pad_maximum_fusion
  2.7 3.4 %collective-permute-start = (bf16[768,512]{1,0:T(8,128)(2,1)S(1)}, bf16[768,512]{1,0:T(8,128)(2,1)S(1)}, u32[]{:S(2)}, u32[]{:S(2)}) collective-permute-start(bf16[768,512]{1,0:T(8,128)(2,1)S(1)} %pad_maximum_fusion), channel_id=1, source_target_pairs={{0,8},{1,25},{2,10},{3,27},{4,12},{5,29},{6,14},{7,31},{8,0},{9,17... | collective-permute-start | bytes 2359304 | tf_op jit(solution)/shard_map/ppermute | solution.py:70
  6.1 1.1 dynamic-slice_bitcast_fusion.1
  7.2 2.7 %collective-permute-start.4 = (bf16[384,512]{1,0:T(8,128)(2,1)S(1)}, bf16[384,512]{1,0:T(8,128)(2,1)}, u32[]{:S(2)}, u32[]{:S(2)}) collective-permute-start(bf16[384,512]{1,0:T(8,128)(2,1)S(1)} %pad_maximum_fusion.3), channel_id=1, source_target_pairs={{0,1},{1,0},{2,3},{3,2},{4,5},{5,4},{6,7},{7,6},{8,9},{9,8},{10,11... | collective-permute-start | bytes 1179656 | tf_op jit(solution)/shard_map/ppermute | solution.py:69
  9.9 1.5 %collective-permute-done.4 = bf16[384,512]{1,0:T(8,128)(2,1)} collective-permute-done((bf16[384,512]{1,0:T(8,128)(2,1)S(1)}, bf16[384,512]{1,0:T(8,128)(2,1)}, u32[]{:S(2)}, u32[]{:S(2)}) %collective-permute-start.4) | collective-permute-done | bytes 393248 | tf_op jit(solution)/shard_map/ppermute | solution.py:69
  11.4 2.1 %collective-permute-start.5 = (bf16[384,512]{1,0:T(8,128)(2,1)}, bf16[384,512]{1,0:T(8,128)(2,1)}, u32[]{:S(2)}, u32[]{:S(2)}) collective-permute-start(bf16[384,512]{1,0:T(8,128)(2,1)} %collective-permute-done.4), channel_id=1, source_target_pairs={{0,8},{1,25},{2,10},{3,27},{4,12},{5,29},{6,14},{7,31},{8,0},{9,17... | collective-permute-start | bytes 1179656 | tf_op jit(solution)/shard_map/ppermute | solution.py:74
  13.6 4.5 %collective-permute-start.1 = (bf16[576,512]{1,0:T(8,128)(2,1)S(1)}, bf16[576,512]{1,0:T(8,128)(2,1)S(1)}, u32[]{:S(2)}, u32[]{:S(2)}) collective-permute-start(bf16[576,512]{1,0:T(8,128)(2,1)S(1)} %pad_maximum_fusion.2), channel_id=1, source_target_pairs={{0,24},{1,9},{2,26},{3,11},{4,28},{5,13},{6,30},{7,15},{8,16},{9,1... | collective-permute-start | bytes 1769480 | tf_op jit(solution)/shard_map/ppermute | solution.py:73
  18.1 0.0 copy-start.8
  18.1 0.0 collective-permute-done
  18.2 3.1 %collective-permute-start.2 = (bf16[576,512]{1,0:T(8,128)(2,1)S(1)}, bf16[576,512]{1,0:T(8,128)(2,1)S(1)}, u32[]{:S(2)}, u32[]{:S(2)}) collective-permute-start(bf16[576,512]{1,0:T(8,128)(2,1)S(1)} %slice.90), channel_id=1, source_target_pairs={{0,24},{1,9},{2,26},{3,11},{4,28},{5,13},{6,30},{7,15},{8,16},{9,1... | collective-permute-start | bytes 1769480 | tf_op jit(solution)/shard_map/ppermute | solution.py:76
  21.3 4.1 %collective-permute-start.6 = (bf16[384,512]{1,0:T(8,128)(2,1)}, bf16[384,512]{1,0:T(8,128)(2,1)S(1)}, u32[]{:S(2)}, u32[]{:S(2)}) collective-permute-start(bf16[384,512]{1,0:T(8,128)(2,1)} %collective-permute-done.4), channel_id=1, source_target_pairs={{0,24},{1,9},{2,26},{3,11},{4,28},{5,13},{6,30},{7,15},{8,16},{9,1... | collective-permute-start | bytes 1179656 | tf_op jit(solution)/shard_map/ppermute | solution.py:75
  25.4 0.0 collective-permute-done.5
  25.5 3.0 %collective-permute-start.7 = (bf16[384,512]{1,0:T(8,128)(2,1)}, bf16[384,512]{1,0:T(8,128)(2,1)S(1)}, u32[]{:S(2)}, u32[]{:S(2)}) collective-permute-start(bf16[384,512]{1,0:T(8,128)(2,1)} %collective-permute-done.5), channel_id=1, source_target_pairs={{0,24},{1,9},{2,26},{3,11},{4,28},{5,13},{6,30},{7,15},{8,16},{9,1... | collective-permute-start | bytes 1179656 | tf_op jit(solution)/shard_map/ppermute | solution.py:77
  28.4 0.0 copy-done.8
  28.4 0.7 fusion.29
  29.2 0.0 collective-permute-done.1
  29.2 0.7 fusion.30
  29.9 4.6 %collective-permute-done.2 = bf16[576,512]{1,0:T(8,128)(2,1)S(1)} collective-permute-done((bf16[576,512]{1,0:T(8,128)(2,1)S(1)}, bf16[576,512]{1,0:T(8,128)(2,1)S(1)}, u32[]{:S(2)}, u32[]{:S(2)}) %collective-permute-start.2) | collective-permute-done | bytes 589856 | tf_op jit(solution)/shard_map/ppermute | solution.py:76
  34.5 0.7 fusion.31
  35.3 0.1 pad_maximum_fusion.1
  35.3 2.1 %collective-permute-start.3 = (bf16[768,512]{1,0:T(8,128)(2,1)S(1)}, bf16[768,512]{1,0:T(8,128)(2,1)S(1)}, u32[]{:S(2)}, u32[]{:S(2)}) collective-permute-start(bf16[768,512]{1,0:T(8,128)(2,1)S(1)} %pad_maximum_fusion.1), channel_id=1, source_target_pairs={{0,1},{1,0},{2,3},{3,2},{4,5},{5,4},{6,7},{7,6},{8,9},{9,8},{10,11... | collective-permute-start | bytes 2359304 | tf_op jit(solution)/shard_map/ppermute | solution.py:79
  37.4 0.0 copy-done.11
  37.4 1.1 slice_dynamic-update-slice_fusion.3
  38.4 1.1 slice_dynamic-update-slice_fusion.2
  39.5 0.0 collective-permute-done.6
  39.5 3.4 %collective-permute-done.7 = bf16[384,512]{1,0:T(8,128)(2,1)S(1)} collective-permute-done((bf16[384,512]{1,0:T(8,128)(2,1)}, bf16[384,512]{1,0:T(8,128)(2,1)S(1)}, u32[]{:S(2)}, u32[]{:S(2)}) %collective-permute-start.7) | collective-permute-done | bytes 393248 | tf_op jit(solution)/shard_map/ppermute | solution.py:77
  43.0 0.0 copy-start.9
  43.0 0.0 copy-start.12
  43.0 0.0 collective-permute-done.3
  43.1 0.0 copy-start.6
  43.1 0.9 fusion.1
  44.1 0.1 copy-done.9
  44.1 0.5 copy-done.12
  44.6 0.5 copy-done.6
  45.1 4.5 %collective-permute-start.9 = (f32[256,512]{1,0:T(8,128)S(1)}, f32[256,512]{1,0:T(8,128)S(1)}, u32[]{:S(2)}, u32[]{:S(2)}) collective-permute-start(f32[256,512]{1,0:T(8,128)S(1)} %fusion.1), channel_id=1, source_target_pairs={{0,2},{1,7},{2,0},{3,5},{4,6},{5,3},{6,4},{7,1},{8,10},{9,15},{10,... | collective-permute-start | bytes 1572872 | tf_op jit(solution)/shard_map/ppermute | solution.py:93
  49.7 0.0 copy-start.7
  49.7 0.0 copy-start.10
  49.7 0.0 copy-start.13
  49.7 2.7 %fusion.10 = f32[256,512]{1,0:T(8,128)S(1)} fusion(s32[]{:T(128)S(6)} %select_n.70, bf16[1536,512]{1,0:T(8,128)(2,1)} %copy-done.12, bf16[1536,512]{1,0:T(8,128)(2,1)} %copy-done.9, bf16[1536,512]{1,0:T(8,128)(2,1)} %copy-done.6, s32[]{:T(128)S(6)} %select_n.69), kind=kOutput, calls=%fused_computation.15 | convolution fusion | flops 405798912 | bytes 4456456 | tf_op jit(solution)/shard_map/dot_general | solution.py:89
  52.4 2.2 %collective-permute-start.8 = (f32[256,512]{1,0:T(8,128)S(1)}, f32[256,512]{1,0:T(8,128)S(1)}, u32[]{:S(2)}, u32[]{:S(2)}) collective-permute-start(f32[256,512]{1,0:T(8,128)S(1)} %fusion.10), channel_id=1, source_target_pairs={{0,2},{1,7},{2,0},{3,5},{4,6},{5,3},{6,4},{7,1},{8,10},{9,15},{10,... | collective-permute-start | bytes 1572872 | tf_op jit(solution)/shard_map/ppermute | solution.py:94
  54.6 0.0 copy-done.7
  54.7 0.0 copy-done.10
  54.7 0.0 copy-done.13
  54.7 0.9 fusion.7
  55.6 0.9 fusion.4
  56.5 0.0 copy-start
  56.5 8.0 %collective-permute-done.9 = f32[256,512]{1,0:T(8,128)S(1)} collective-permute-done((f32[256,512]{1,0:T(8,128)S(1)}, f32[256,512]{1,0:T(8,128)S(1)}, u32[]{:S(2)}, u32[]{:S(2)}) %collective-permute-start.9) | collective-permute-done | bytes 524320 | tf_op jit(solution)/shard_map/ppermute | solution.py:93
  64.6 0.1 add.107
  64.7 0.0 copy-start.2
  64.7 0.0 copy-start.3
  64.7 4.5 %collective-permute-start.10 = (f32[256,512]{1,0:T(8,128)S(1)}, f32[256,512]{1,0:T(8,128)S(1)}, u32[]{:S(2)}, u32[]{:S(2)}) collective-permute-start(f32[256,512]{1,0:T(8,128)S(1)} %add.107), channel_id=1, source_target_pairs={{0,6},{1,3},{2,4},{3,1},{4,2},{5,7},{6,0},{7,5},{8,14},{9,11},{10,... | collective-permute-start | bytes 1572872 | tf_op jit(solution)/shard_map/ppermute | solution.py:96
  69.2 9.2 %collective-permute-done.8 = f32[256,512]{1,0:T(8,128)S(1)} collective-permute-done((f32[256,512]{1,0:T(8,128)S(1)}, f32[256,512]{1,0:T(8,128)S(1)}, u32[]{:S(2)}, u32[]{:S(2)}) %collective-permute-start.8) | collective-permute-done | bytes 524320 | tf_op jit(solution)/shard_map/ppermute | solution.py:94
  78.4 4.9 %collective-permute-done.10 = f32[256,512]{1,0:T(8,128)S(1)} collective-permute-done((f32[256,512]{1,0:T(8,128)S(1)}, f32[256,512]{1,0:T(8,128)S(1)}, u32[]{:S(2)}, u32[]{:S(2)}) %collective-permute-start.10) | collective-permute-done | bytes 524320 | tf_op jit(solution)/shard_map/ppermute | solution.py:96
  83.3 0.0 copy-done
  83.3 1.0 fusion.20
  84.3 0.0 copy-done.2
  84.3 1.1 fusion.19
  85.5 28.8 %all_to_all.10 = f32[16,16,512]{2,1,0:T(8,128)S(1)} all-to-all(f32[16,16,512]{2,1,0:T(8,128)S(1)} %bitcast.56), channel_id=1, replica_groups=mesh['replica'=16,'fsdp'=32] {'replica'}, dimensions={0} | all-to-all | bytes 1048576 | tf_op jit(solution)/shard_map/all_to_all | solution.py:110
  114.4 0.6 subtract_bitcast_fusion
  115.0 20.9 %all_to_all.11 = f32[16,16,512]{2,1,0:T(8,128)S(1)} all-to-all(f32[16,16,512]{2,1,0:T(8,128)S(1)} %broadcast_in_dim.16), channel_id=1, replica_groups=mesh['replica'=16,'fsdp'=32] {'replica'}, dimensions={0} | all-to-all | bytes 1048576 | tf_op jit(solution)/shard_map/all_to_all | solution.py:116
  135.9 0.8 copy.33
  (19 shorter events, 0.4 us)
Async XLA Ops:
  0.6 2.0 %copy-start.1 = (bf16[1,192,2048]{2,1,0:T(8,128)(2,1)S(1)}, bf16[1,192,2048]{2,1,0:T(8,128)(2,1)}, u32[]{:S(2)}) copy-start(bf16[1,192,2048]{2,1,0:T(8,128)(2,1)} %param.7) | copy-start | bytes 2359300
  2.7 15.4 %collective-permute-start = (bf16[768,512]{1,0:T(8,128)(2,1)S(1)}, bf16[768,512]{1,0:T(8,128)(2,1)S(1)}, u32[]{:S(2)}, u32[]{:S(2)}) collective-permute-start(bf16[768,512]{1,0:T(8,128)(2,1)S(1)} %pad_maximum_fusion), channel_id=1, source_target_pairs={{0,8},{1,25},{2,10},{3,27},{4,12},{5,29},{6,14},{7,31},{8,0},{9,17... | collective-permute-start | bytes 2359304 | tf_op jit(solution)/shard_map/ppermute | solution.py:70
  7.2 4.2 %collective-permute-start.4 = (bf16[384,512]{1,0:T(8,128)(2,1)S(1)}, bf16[384,512]{1,0:T(8,128)(2,1)}, u32[]{:S(2)}, u32[]{:S(2)}) collective-permute-start(bf16[384,512]{1,0:T(8,128)(2,1)S(1)} %pad_maximum_fusion.3), channel_id=1, source_target_pairs={{0,1},{1,0},{2,3},{3,2},{4,5},{5,4},{6,7},{7,6},{8,9},{9,8},{10,11... | collective-permute-start | bytes 1179656 | tf_op jit(solution)/shard_map/ppermute | solution.py:69
  11.4 14.0 %collective-permute-start.5 = (bf16[384,512]{1,0:T(8,128)(2,1)}, bf16[384,512]{1,0:T(8,128)(2,1)}, u32[]{:S(2)}, u32[]{:S(2)}) collective-permute-start(bf16[384,512]{1,0:T(8,128)(2,1)} %collective-permute-done.4), channel_id=1, source_target_pairs={{0,8},{1,25},{2,10},{3,27},{4,12},{5,29},{6,14},{7,31},{8,0},{9,17... | collective-permute-start | bytes 1179656 | tf_op jit(solution)/shard_map/ppermute | solution.py:74
  13.6 15.6 %collective-permute-start.1 = (bf16[576,512]{1,0:T(8,128)(2,1)S(1)}, bf16[576,512]{1,0:T(8,128)(2,1)S(1)}, u32[]{:S(2)}, u32[]{:S(2)}) collective-permute-start(bf16[576,512]{1,0:T(8,128)(2,1)S(1)} %pad_maximum_fusion.2), channel_id=1, source_target_pairs={{0,24},{1,9},{2,26},{3,11},{4,28},{5,13},{6,30},{7,15},{8,16},{9,1... | collective-permute-start | bytes 1769480 | tf_op jit(solution)/shard_map/ppermute | solution.py:73
  18.1 10.3 %copy-start.8 = (bf16[1536,512]{1,0:T(8,128)(2,1)S(1)}, bf16[1536,512]{1,0:T(8,128)(2,1)}, u32[]{:S(2)}) copy-start(bf16[1536,512]{1,0:T(8,128)(2,1)} %get-tuple-element.14) | copy-start | bytes 4718596
  18.2 16.3 %collective-permute-start.2 = (bf16[576,512]{1,0:T(8,128)(2,1)S(1)}, bf16[576,512]{1,0:T(8,128)(2,1)S(1)}, u32[]{:S(2)}, u32[]{:S(2)}) collective-permute-start(bf16[576,512]{1,0:T(8,128)(2,1)S(1)} %slice.90), channel_id=1, source_target_pairs={{0,24},{1,9},{2,26},{3,11},{4,28},{5,13},{6,30},{7,15},{8,16},{9,1... | collective-permute-start | bytes 1769480 | tf_op jit(solution)/shard_map/ppermute | solution.py:76
  21.3 18.2 %collective-permute-start.6 = (bf16[384,512]{1,0:T(8,128)(2,1)}, bf16[384,512]{1,0:T(8,128)(2,1)S(1)}, u32[]{:S(2)}, u32[]{:S(2)}) collective-permute-start(bf16[384,512]{1,0:T(8,128)(2,1)} %collective-permute-done.4), channel_id=1, source_target_pairs={{0,24},{1,9},{2,26},{3,11},{4,28},{5,13},{6,30},{7,15},{8,16},{9,1... | collective-permute-start | bytes 1179656 | tf_op jit(solution)/shard_map/ppermute | solution.py:75
  25.5 17.5 %collective-permute-start.7 = (bf16[384,512]{1,0:T(8,128)(2,1)}, bf16[384,512]{1,0:T(8,128)(2,1)S(1)}, u32[]{:S(2)}, u32[]{:S(2)}) collective-permute-start(bf16[384,512]{1,0:T(8,128)(2,1)} %collective-permute-done.5), channel_id=1, source_target_pairs={{0,24},{1,9},{2,26},{3,11},{4,28},{5,13},{6,30},{7,15},{8,16},{9,1... | collective-permute-start | bytes 1179656 | tf_op jit(solution)/shard_map/ppermute | solution.py:77
  35.3 2.1 %copy-start.11 = (bf16[1536,512]{1,0:T(8,128)(2,1)S(1)}, bf16[1536,512]{1,0:T(8,128)(2,1)}, u32[]{:S(2)}) copy-start(bf16[1536,512]{1,0:T(8,128)(2,1)} %get-tuple-element.38) | copy-start | bytes 4718596
  35.3 7.7 %collective-permute-start.3 = (bf16[768,512]{1,0:T(8,128)(2,1)S(1)}, bf16[768,512]{1,0:T(8,128)(2,1)S(1)}, u32[]{:S(2)}, u32[]{:S(2)}) collective-permute-start(bf16[768,512]{1,0:T(8,128)(2,1)S(1)} %pad_maximum_fusion.1), channel_id=1, source_target_pairs={{0,1},{1,0},{2,3},{3,2},{4,5},{5,4},{6,7},{7,6},{8,9},{9,8},{10,11... | collective-permute-start | bytes 2359304 | tf_op jit(solution)/shard_map/ppermute | solution.py:79
  43.0 1.1 copy-start.9
  43.0 1.6 %copy-start.12 = (bf16[1536,512]{1,0:T(8,128)(2,1)}, bf16[1536,512]{1,0:T(8,128)(2,1)S(1)}, u32[]{:S(2)}) copy-start(bf16[1536,512]{1,0:T(8,128)(2,1)S(1)} %get-tuple-element.40) | copy-start | bytes 4718596
  43.1 2.0 %copy-start.6 = (bf16[1536,512]{1,0:T(8,128)(2,1)}, bf16[1536,512]{1,0:T(8,128)(2,1)S(1)}, u32[]{:S(2)}) copy-start(bf16[1536,512]{1,0:T(8,128)(2,1)S(1)} %slice_dynamic-update-slice_fusion.14) | copy-start | bytes 4718596
  45.1 19.4 %collective-permute-start.9 = (f32[256,512]{1,0:T(8,128)S(1)}, f32[256,512]{1,0:T(8,128)S(1)}, u32[]{:S(2)}, u32[]{:S(2)}) collective-permute-start(f32[256,512]{1,0:T(8,128)S(1)} %fusion.1), channel_id=1, source_target_pairs={{0,2},{1,7},{2,0},{3,5},{4,6},{5,3},{6,4},{7,1},{8,10},{9,15},{10,... | collective-permute-start | bytes 1572872 | tf_op jit(solution)/shard_map/ppermute | solution.py:93
  49.7 5.0 %copy-start.7 = (bf16[1536,512]{1,0:T(8,128)(2,1)S(1)}, bf16[1536,512]{1,0:T(8,128)(2,1)}, u32[]{:S(2)}) copy-start(bf16[1536,512]{1,0:T(8,128)(2,1)} %copy-done.6) | copy-start | bytes 4718596
  49.7 5.0 %copy-start.10 = (bf16[1536,512]{1,0:T(8,128)(2,1)S(1)}, bf16[1536,512]{1,0:T(8,128)(2,1)}, u32[]{:S(2)}) copy-start(bf16[1536,512]{1,0:T(8,128)(2,1)} %copy-done.9) | copy-start | bytes 4718596
  49.7 5.0 %copy-start.13 = (bf16[1536,512]{1,0:T(8,128)(2,1)S(1)}, bf16[1536,512]{1,0:T(8,128)(2,1)}, u32[]{:S(2)}) copy-start(bf16[1536,512]{1,0:T(8,128)(2,1)} %copy-done.12) | copy-start | bytes 4718596
  52.4 26.0 %collective-permute-start.8 = (f32[256,512]{1,0:T(8,128)S(1)}, f32[256,512]{1,0:T(8,128)S(1)}, u32[]{:S(2)}, u32[]{:S(2)}) collective-permute-start(f32[256,512]{1,0:T(8,128)S(1)} %fusion.10), channel_id=1, source_target_pairs={{0,2},{1,7},{2,0},{3,5},{4,6},{5,3},{6,4},{7,1},{8,10},{9,15},{10,... | collective-permute-start | bytes 1572872 | tf_op jit(solution)/shard_map/ppermute | solution.py:94
  56.5 26.8 %copy-start = (f32[1,1,256,512]{3,2,1,0:T(8,128)S(1)}, f32[1,1,256,512]{3,2,1,0:T(8,128)}, u32[]{:S(2)}) copy-start(f32[1,1,256,512]{3,2,1,0:T(8,128)} %param.11) | copy-start | bytes 1572868
  64.7 19.7 %copy-start.2 = (f32[1,1,256,512]{3,2,1,0:T(8,128)S(1)}, f32[1,1,256,512]{3,2,1,0:T(8,128)}, u32[]{:S(2)}) copy-start(f32[1,1,256,512]{3,2,1,0:T(8,128)} %param.10) | copy-start | bytes 1572868
  64.7 19.7 %copy-start.3 = (f32[1,1,256,512]{3,2,1,0:T(8,128)S(1)}, f32[1,1,256,512]{3,2,1,0:T(8,128)}, u32[]{:S(2)}) copy-start(f32[1,1,256,512]{3,2,1,0:T(8,128)} %param.9) | copy-start | bytes 1572868
  64.7 18.6 %collective-permute-start.10 = (f32[256,512]{1,0:T(8,128)S(1)}, f32[256,512]{1,0:T(8,128)S(1)}, u32[]{:S(2)}, u32[]{:S(2)}) collective-permute-start(f32[256,512]{1,0:T(8,128)S(1)} %add.107), channel_id=1, source_target_pairs={{0,6},{1,3},{2,4},{3,1},{4,2},{5,7},{6,0},{7,5},{8,14},{9,11},{10,... | collective-permute-start | bytes 1572872 | tf_op jit(solution)/shard_map/ppermute | solution.py:96
  85.5 28.8 %copy-start.4 = (f32[1,16,512]{2,1,0:T(8,128)S(1)}, f32[1,16,512]{2,1,0:T(8,128)}, u32[]{:S(2)}) copy-start(f32[1,16,512]{2,1,0:T(8,128)} %param.12) | copy-start | bytes 98308
  85.5 28.9 %copy-start.5 = (f32[1,16,512]{2,1,0:T(8,128)S(1)}, f32[1,16,512]{2,1,0:T(8,128)}, u32[]{:S(2)}) copy-start(f32[1,16,512]{2,1,0:T(8,128)} %param.13) | copy-start | bytes 98308

commit v6 on v5

--- a/solution.py
+++ b/solution.py
@@ -65,7 +65,7 @@
     def pieces(t):
         return [t[i * count : (i + 1) * count] for i in range(t.shape[0] // count)]
 
-    u_own = u_for(c)
+    u_own = lax.optimization_barrier(u_for(c))
     u_swap = lax.ppermute(jnp.concatenate(u_for(1 - c), 0), "fsdp", core_pairs())
     one = lax.ppermute(
         jnp.concatenate([a_for(x ^ near), *u_own, a_for(x ^ 2)], 0), "fsdp", x_pairs(0)
@@ -99,10 +99,19 @@
     fix_one = 1.0 - beta_one**STEP
     fix_two = 1.0 - beta_two**STEP
     params = inner_params[0, 0]
-    moment_one = beta_one * first_moment[0, 0] + (1.0 - beta_one) * gradient
-    moment_two = beta_two * second_moment[0, 0] + (1.0 - beta_two) * gradient * gradient
+
+    def moments(g, first, second):
+        return (
+            beta_one * first + (1.0 - beta_one) * g,
+            beta_two * second + (1.0 - beta_two) * g * g,
+        )
+
+    moment_one, moment_two = moments(gradient, first_moment[0, 0], second_moment[0, 0])
     update = (
         moment_one / fix_one / (jnp.sqrt(moment_two / fix_two) + adam_eps) + decay_rate * params
+    )
+    moment_one, moment_two = moments(
+        *lax.optimization_barrier((gradient, first_moment[0, 0], second_moment[0, 0]))
     )
     stepped = params - inner_rate * update
 
@@ -110,9 +119,14 @@
     parts = lax.all_to_all(
         stepped.reshape(members, slice_rows, cols), "replica", split_axis=0, concat_axis=0, tiled=True
     )
-    pseudo = anchor[0] - jnp.sum(parts, axis=0) / members
-    new_momentum = outer_mu * outer_momentum[0] + pseudo
-    new_params = anchor[0] - outer_rate * (pseudo + outer_mu * new_momentum)
+    def outer(mean, anchor, momentum):
+        pseudo = anchor - mean
+        momentum = outer_mu * momentum + pseudo
+        return momentum, anchor - outer_rate * (pseudo + outer_mu * momentum)
+
+    mean = jnp.sum(parts, axis=0) / members
+    _, new_params = outer(mean, anchor[0], outer_momentum[0])
+    new_momentum, _ = outer(*lax.optimization_barrier((mean, anchor[0], outer_momentum[0])))
     gathered = lax.all_to_all(
         jnp.broadcast_to(new_params[None], (members, slice_rows, cols)),
         "replica",

time: 137 us -> 135 us (0.985)
  the two profiles are of different devices: /device:TPU:72 before, /device:TPU:14 now
where the time goes in v6:
time: 135 us; the launch traced here: 134 us
  waiting for transfers between devices  49.8 us (37%)
  starting transfers between devices  37.6 us (28%)
  blocking collectives  29.7 us (22%)
  local copies, waits for them, and re-layouts  7.83 us (6%)
  matrix products  5.46 us (4%)
  other arithmetic  2.52 us (2%)
    all_to_all x1, blocking collectives, body(): lax.all_to_all(stepped.reshape(members, slice_rows, cols), 'replica', spl...  29.7 us
    all_to_all x1, waiting for transfers between devices, body(): lax.all_to_all(jnp.broadcast_to(new_params[None], (members, slice_rows, c...  13.2 us
    ppermute x1, waiting for transfers between devices, body(): g_far = lax.ppermute(part(y ^ 2), 'fsdp', y_pairs(0))  8.73 us
    ppermute x1, waiting for transfers between devices, body(): g_near = lax.ppermute(part(y ^ near), 'fsdp', y_pairs(0))  7.14 us
    ppermute x1, waiting for transfers between devices, body(): g_two = lax.ppermute(kept_far + g_far, 'fsdp', y_pairs(1))  6.94 us
    dot_general x4, matrix products, part(): lax.dot_general(left, right, (((0,), (0,)), ((), ())), preferred_element_...  5.46 us
    ppermute x1, waiting for transfers between devices, body(): three = lax.ppermute(one[count:], 'fsdp', x_pairs(1))  5.04 us
    ppermute x1, starting transfers between devices, body(): g_two = lax.ppermute(kept_far + g_far, 'fsdp', y_pairs(1))  4.59 us
  transfers between devices with their start and end apart: 12, of which 10 were waited for; matrix products, arithmetic and copies ran while one was open for 8% of the time, Pallas kernels for 0%

profile of v6, /device:TPU:14, one launch (start us, length us, event | category | flops | bytes accessed | tf_op | source)
XLA Modules:
  0.0 134.0 jit_solution(4512649945674657843)
XLA Ops:
  0.6 0.0 copy-start.2
  0.7 1.3 dynamic-slice_bitcast_fusion.1
  2.0 0.1 copy-done.2
  2.2 0.1 pad_maximum_fusion
  2.2 2.7 %collective-permute-start = (bf16[768,512]{1,0:T(8,128)(2,1)S(1)}, bf16[768,512]{1,0:T(8,128)(2,1)S(1)}, u32[]{:S(2)}, u32[]{:S(2)}) collective-permute-start(bf16[768,512]{1,0:T(8,128)(2,1)S(1)} %pad_maximum_fusion), channel_id=1, source_target_pairs={{0,8},{1,25},{2,10},{3,27},{4,12},{5,29},{6,14},{7,31},{8,0},{9,17... | collective-permute-start | bytes 2359304 | tf_op jit(solution)/shard_map/ppermute | solution.py:70
  5.0 1.9 %collective-permute-start.4 = (bf16[384,512]{1,0:T(8,128)(2,1)S(1)}, bf16[384,512]{1,0:T(8,128)(2,1)}, u32[]{:S(2)}, u32[]{:S(2)}) collective-permute-start(bf16[384,512]{1,0:T(8,128)(2,1)S(1)} %pad_maximum_fusion.3), channel_id=1, source_target_pairs={{0,1},{1,0},{2,3},{3,2},{4,5},{5,4},{6,7},{7,6},{8,9},{9,8},{10,11... | collective-permute-start | bytes 1179656 | tf_op jit(solution)/shard_map/ppermute | solution.py:69
  6.9 1.8 %collective-permute-done.4 = bf16[384,512]{1,0:T(8,128)(2,1)} collective-permute-done((bf16[384,512]{1,0:T(8,128)(2,1)S(1)}, bf16[384,512]{1,0:T(8,128)(2,1)}, u32[]{:S(2)}, u32[]{:S(2)}) %collective-permute-start.4) | collective-permute-done | bytes 393248 | tf_op jit(solution)/shard_map/ppermute | solution.py:69
  8.8 3.1 %collective-permute-start.5 = (bf16[384,512]{1,0:T(8,128)(2,1)}, bf16[384,512]{1,0:T(8,128)(2,1)}, u32[]{:S(2)}, u32[]{:S(2)}) collective-permute-start(bf16[384,512]{1,0:T(8,128)(2,1)} %collective-permute-done.4), channel_id=1, source_target_pairs={{0,8},{1,25},{2,10},{3,27},{4,12},{5,29},{6,14},{7,31},{8,0},{9,17... | collective-permute-start | bytes 1179656 | tf_op jit(solution)/shard_map/ppermute | solution.py:74
  11.9 2.5 %collective-permute-start.1 = (bf16[576,512]{1,0:T(8,128)(2,1)S(1)}, bf16[576,512]{1,0:T(8,128)(2,1)}, u32[]{:S(2)}, u32[]{:S(2)}) collective-permute-start(bf16[576,512]{1,0:T(8,128)(2,1)S(1)} %pad_maximum_fusion.2), channel_id=1, source_target_pairs={{0,24},{1,9},{2,26},{3,11},{4,28},{5,13},{6,30},{7,15},{8,16},{9,1... | collective-permute-start | bytes 1769480 | tf_op jit(solution)/shard_map/ppermute | solution.py:73
  14.5 1.6 %collective-permute-done = bf16[768,512]{1,0:T(8,128)(2,1)S(1)} collective-permute-done((bf16[768,512]{1,0:T(8,128)(2,1)S(1)}, bf16[768,512]{1,0:T(8,128)(2,1)S(1)}, u32[]{:S(2)}, u32[]{:S(2)}) %collective-permute-start) | collective-permute-done | bytes 786464 | tf_op jit(solution)/shard_map/ppermute | solution.py:70
  16.1 2.9 %collective-permute-start.2 = (bf16[576,512]{1,0:T(8,128)(2,1)S(1)}, bf16[576,512]{1,0:T(8,128)(2,1)S(1)}, u32[]{:S(2)}, u32[]{:S(2)}) collective-permute-start(bf16[576,512]{1,0:T(8,128)(2,1)S(1)} %slice.90), channel_id=1, source_target_pairs={{0,24},{1,9},{2,26},{3,11},{4,28},{5,13},{6,30},{7,15},{8,16},{9,1... | collective-permute-start | bytes 1769480 | tf_op jit(solution)/shard_map/ppermute | solution.py:76
  19.1 4.1 %collective-permute-start.6 = (bf16[384,512]{1,0:T(8,128)(2,1)}, bf16[384,512]{1,0:T(8,128)(2,1)S(1)}, u32[]{:S(2)}, u32[]{:S(2)}) collective-permute-start(bf16[384,512]{1,0:T(8,128)(2,1)} %collective-permute-done.4), channel_id=1, source_target_pairs={{0,24},{1,9},{2,26},{3,11},{4,28},{5,13},{6,30},{7,15},{8,16},{9,1... | collective-permute-start | bytes 1179656 | tf_op jit(solution)/shard_map/ppermute | solution.py:75
  23.3 0.5 collective-permute-done.5
  23.8 2.4 %collective-permute-start.7 = (bf16[384,512]{1,0:T(8,128)(2,1)}, bf16[384,512]{1,0:T(8,128)(2,1)S(1)}, u32[]{:S(2)}, u32[]{:S(2)}) collective-permute-start(bf16[384,512]{1,0:T(8,128)(2,1)} %collective-permute-done.5), channel_id=1, source_target_pairs={{0,24},{1,9},{2,26},{3,11},{4,28},{5,13},{6,30},{7,15},{8,16},{9,1... | collective-permute-start | bytes 1179656 | tf_op jit(solution)/shard_map/ppermute | solution.py:77
  26.2 0.1 fusion.33
  26.3 0.6 collective-permute-done.1
  26.8 1.2 fusion.34
  28.0 5.0 %collective-permute-done.2 = bf16[576,512]{1,0:T(8,128)(2,1)S(1)} collective-permute-done((bf16[576,512]{1,0:T(8,128)(2,1)S(1)}, bf16[576,512]{1,0:T(8,128)(2,1)S(1)}, u32[]{:S(2)}, u32[]{:S(2)}) %collective-permute-start.2) | collective-permute-done | bytes 589856 | tf_op jit(solution)/shard_map/ppermute | solution.py:76
  33.0 0.1 fusion.35
  33.1 0.1 pad_maximum_fusion.1
  33.2 1.9 %collective-permute-start.3 = (bf16[768,512]{1,0:T(8,128)(2,1)S(1)}, bf16[768,512]{1,0:T(8,128)(2,1)S(1)}, u32[]{:S(2)}, u32[]{:S(2)}) collective-permute-start(bf16[768,512]{1,0:T(8,128)(2,1)S(1)} %pad_maximum_fusion.1), channel_id=1, source_target_pairs={{0,1},{1,0},{2,3},{3,2},{4,5},{5,4},{6,7},{7,6},{8,9},{9,8},{10,11... | collective-permute-start | bytes 2359304 | tf_op jit(solution)/shard_map/ppermute | solution.py:79
  35.1 1.1 slice_dynamic-update-slice_fusion.3
  36.2 1.1 slice_dynamic-update-slice_fusion.2
  37.2 0.0 collective-permute-done.6
  37.3 4.2 %collective-permute-done.7 = bf16[384,512]{1,0:T(8,128)(2,1)S(1)} collective-permute-done((bf16[384,512]{1,0:T(8,128)(2,1)}, bf16[384,512]{1,0:T(8,128)(2,1)S(1)}, u32[]{:S(2)}, u32[]{:S(2)}) %collective-permute-start.7) | collective-permute-done | bytes 393248 | tf_op jit(solution)/shard_map/ppermute | solution.py:77
  41.5 0.0 copy-start.6
  41.5 0.0 copy-start.8
  41.5 0.0 collective-permute-done.3
  41.6 0.0 copy-start.10
  41.6 0.9 fusion.1
  42.6 0.1 copy-done.6
  42.7 0.5 copy-done.8
  43.1 0.5 copy-done.10
  43.6 4.5 %collective-permute-start.9 = (f32[256,512]{1,0:T(8,128)S(1)}, f32[256,512]{1,0:T(8,128)S(1)}, u32[]{:S(2)}, u32[]{:S(2)}) collective-permute-start(f32[256,512]{1,0:T(8,128)S(1)} %fusion.1), channel_id=1, source_target_pairs={{0,2},{1,7},{2,0},{3,5},{4,6},{5,3},{6,4},{7,1},{8,10},{9,15},{10,... | collective-permute-start | bytes 1572872 | tf_op jit(solution)/shard_map/ppermute | solution.py:93
  48.1 0.0 copy-start.7
  48.2 0.0 copy-start.9
  48.2 0.0 copy-start.11
  48.2 2.7 %fusion.10 = f32[256,512]{1,0:T(8,128)S(1)} fusion(s32[]{:T(128)S(6)} %select_n.70, bf16[1536,512]{1,0:T(8,128)(2,1)} %copy-done.6, bf16[1536,512]{1,0:T(8,128)(2,1)} %copy-done.8, bf16[1536,512]{1,0:T(8,128)(2,1)} %copy-done.10, s32[]{:T(128)S(6)} %select_n.69), kind=kOutput, calls=%fused_computation.15 | convolution fusion | flops 405798912 | bytes 4456456 | tf_op jit(solution)/shard_map/dot_general | solution.py:89
  50.9 2.2 %collective-permute-start.8 = (f32[256,512]{1,0:T(8,128)S(1)}, f32[256,512]{1,0:T(8,128)S(1)}, u32[]{:S(2)}, u32[]{:S(2)}) collective-permute-start(f32[256,512]{1,0:T(8,128)S(1)} %fusion.10), channel_id=1, source_target_pairs={{0,2},{1,7},{2,0},{3,5},{4,6},{5,3},{6,4},{7,1},{8,10},{9,15},{10,... | collective-permute-start | bytes 1572872 | tf_op jit(solution)/shard_map/ppermute | solution.py:94
  53.1 0.0 copy-done.7
  53.1 0.0 copy-done.9
  53.2 0.0 copy-done.11
  53.2 0.9 fusion.7
  54.1 0.9 fusion.4
  55.0 0.0 copy-start
  55.0 0.0 copy-start.1
  55.0 0.0 copy-start.3
  55.0 8.7 %collective-permute-done.9 = f32[256,512]{1,0:T(8,128)S(1)} collective-permute-done((f32[256,512]{1,0:T(8,128)S(1)}, f32[256,512]{1,0:T(8,128)S(1)}, u32[]{:S(2)}, u32[]{:S(2)}) %collective-permute-start.9) | collective-permute-done | bytes 524320 | tf_op jit(solution)/shard_map/ppermute | solution.py:93
  63.8 0.1 add.115
  63.9 4.6 %collective-permute-start.10 = (f32[256,512]{1,0:T(8,128)S(1)}, f32[256,512]{1,0:T(8,128)S(1)}, u32[]{:S(2)}, u32[]{:S(2)}) collective-permute-start(f32[256,512]{1,0:T(8,128)S(1)} %add.115), channel_id=1, source_target_pairs={{0,6},{1,3},{2,4},{3,1},{4,2},{5,7},{6,0},{7,5},{8,14},{9,11},{10,... | collective-permute-start | bytes 1572872 | tf_op jit(solution)/shard_map/ppermute | solution.py:96
  68.5 7.1 %collective-permute-done.8 = f32[256,512]{1,0:T(8,128)S(1)} collective-permute-done((f32[256,512]{1,0:T(8,128)S(1)}, f32[256,512]{1,0:T(8,128)S(1)}, u32[]{:S(2)}, u32[]{:S(2)}) %collective-permute-start.8) | collective-permute-done | bytes 524320 | tf_op jit(solution)/shard_map/ppermute | solution.py:94
  75.6 6.9 %collective-permute-done.10 = f32[256,512]{1,0:T(8,128)S(1)} collective-permute-done((f32[256,512]{1,0:T(8,128)S(1)}, f32[256,512]{1,0:T(8,128)S(1)}, u32[]{:S(2)}, u32[]{:S(2)}) %collective-permute-start.10) | collective-permute-done | bytes 524320 | tf_op jit(solution)/shard_map/ppermute | solution.py:96
  82.6 0.0 copy-done
  82.6 0.0 copy-done.3
  82.6 0.4 fusion.22
  83.0 0.0 copy-start.4
  83.0 0.0 copy-start.5
  83.0 29.7 %all_to_all.10 = f32[16,16,512]{2,1,0:T(8,128)S(1)} all-to-all(f32[16,16,512]{2,1,0:T(8,128)S(1)} %bitcast.45), channel_id=1, replica_groups=mesh['replica'=16,'fsdp'=32] {'replica'}, dimensions={0} | all-to-all | bytes 1048576 | tf_op jit(solution)/shard_map/all_to_all | solution.py:119
  112.8 0.9 broadcast_in_dim.18
  113.7 4.6 %all-to-all-start.1 = ((f32[16,16,512]{2,1,0:T(8,128)}), f32[16,16,512]{2,1,0:T(8,128)S(1)}, u32[]{:S(2)}, u32[]{:S(2)}) async-start(f32[16,16,512]{2,1,0:T(8,128)} %broadcast_in_dim.18), calls=%async_computation.1 | async-start | bytes 1048576 | tf_op jit(solution)/shard_map/all_to_all | solution.py:130
  118.2 1.2 fusion.24
  119.4 0.6 add_bitcast_fusion.1
  120.0 13.2 %all-to-all-done.1 = f32[16,16,512]{2,1,0:T(8,128)S(1)} async-done(((f32[16,16,512]{2,1,0:T(8,128)}), f32[16,16,512]{2,1,0:T(8,128)S(1)}, u32[]{:S(2)}, u32[]{:S(2)}) %all-to-all-start.1) | async-done | bytes 524320 | tf_op jit(solution)/shard_map/all_to_all | solution.py:130
  133.2 0.8 copy.33
  (18 shorter events, 0.4 us)
Async XLA Ops:
  0.6 1.5 %copy-start.2 = (bf16[1,192,2048]{2,1,0:T(8,128)(2,1)S(1)}, bf16[1,192,2048]{2,1,0:T(8,128)(2,1)}, u32[]{:S(2)}) copy-start(bf16[1,192,2048]{2,1,0:T(8,128)(2,1)} %param.7) | copy-start | bytes 2359300
  2.2 13.9 %collective-permute-start = (bf16[768,512]{1,0:T(8,128)(2,1)S(1)}, bf16[768,512]{1,0:T(8,128)(2,1)S(1)}, u32[]{:S(2)}, u32[]{:S(2)}) collective-permute-start(bf16[768,512]{1,0:T(8,128)(2,1)S(1)} %pad_maximum_fusion), channel_id=1, source_target_pairs={{0,8},{1,25},{2,10},{3,27},{4,12},{5,29},{6,14},{7,31},{8,0},{9,17... | collective-permute-start | bytes 2359304 | tf_op jit(solution)/shard_map/ppermute | solution.py:70
  5.0 3.7 %collective-permute-start.4 = (bf16[384,512]{1,0:T(8,128)(2,1)S(1)}, bf16[384,512]{1,0:T(8,128)(2,1)}, u32[]{:S(2)}, u32[]{:S(2)}) collective-permute-start(bf16[384,512]{1,0:T(8,128)(2,1)S(1)} %pad_maximum_fusion.3), channel_id=1, source_target_pairs={{0,1},{1,0},{2,3},{3,2},{4,5},{5,4},{6,7},{7,6},{8,9},{9,8},{10,11... | collective-permute-start | bytes 1179656 | tf_op jit(solution)/shard_map/ppermute | solution.py:69
  8.8 15.0 %collective-permute-start.5 = (bf16[384,512]{1,0:T(8,128)(2,1)}, bf16[384,512]{1,0:T(8,128)(2,1)}, u32[]{:S(2)}, u32[]{:S(2)}) collective-permute-start(bf16[384,512]{1,0:T(8,128)(2,1)} %collective-permute-done.4), channel_id=1, source_target_pairs={{0,8},{1,25},{2,10},{3,27},{4,12},{5,29},{6,14},{7,31},{8,0},{9,17... | collective-permute-start | bytes 1179656 | tf_op jit(solution)/shard_map/ppermute | solution.py:74
  11.9 14.9 %collective-permute-start.1 = (bf16[576,512]{1,0:T(8,128)(2,1)S(1)}, bf16[576,512]{1,0:T(8,128)(2,1)}, u32[]{:S(2)}, u32[]{:S(2)}) collective-permute-start(bf16[576,512]{1,0:T(8,128)(2,1)S(1)} %pad_maximum_fusion.2), channel_id=1, source_target_pairs={{0,24},{1,9},{2,26},{3,11},{4,28},{5,13},{6,30},{7,15},{8,16},{9,1... | collective-permute-start | bytes 1769480 | tf_op jit(solution)/shard_map/ppermute | solution.py:73
  16.1 16.9 %collective-permute-start.2 = (bf16[576,512]{1,0:T(8,128)(2,1)S(1)}, bf16[576,512]{1,0:T(8,128)(2,1)S(1)}, u32[]{:S(2)}, u32[]{:S(2)}) collective-permute-start(bf16[576,512]{1,0:T(8,128)(2,1)S(1)} %slice.90), channel_id=1, source_target_pairs={{0,24},{1,9},{2,26},{3,11},{4,28},{5,13},{6,30},{7,15},{8,16},{9,1... | collective-permute-start | bytes 1769480 | tf_op jit(solution)/shard_map/ppermute | solution.py:76
  19.1 18.1 %collective-permute-start.6 = (bf16[384,512]{1,0:T(8,128)(2,1)}, bf16[384,512]{1,0:T(8,128)(2,1)S(1)}, u32[]{:S(2)}, u32[]{:S(2)}) collective-permute-start(bf16[384,512]{1,0:T(8,128)(2,1)} %collective-permute-done.4), channel_id=1, source_target_pairs={{0,24},{1,9},{2,26},{3,11},{4,28},{5,13},{6,30},{7,15},{8,16},{9,1... | collective-permute-start | bytes 1179656 | tf_op jit(solution)/shard_map/ppermute | solution.py:75
  23.8 17.7 %collective-permute-start.7 = (bf16[384,512]{1,0:T(8,128)(2,1)}, bf16[384,512]{1,0:T(8,128)(2,1)S(1)}, u32[]{:S(2)}, u32[]{:S(2)}) collective-permute-start(bf16[384,512]{1,0:T(8,128)(2,1)} %collective-permute-done.5), channel_id=1, source_target_pairs={{0,24},{1,9},{2,26},{3,11},{4,28},{5,13},{6,30},{7,15},{8,16},{9,1... | collective-permute-start | bytes 1179656 | tf_op jit(solution)/shard_map/ppermute | solution.py:77
  33.2 8.4 %collective-permute-start.3 = (bf16[768,512]{1,0:T(8,128)(2,1)S(1)}, bf16[768,512]{1,0:T(8,128)(2,1)S(1)}, u32[]{:S(2)}, u32[]{:S(2)}) collective-permute-start(bf16[768,512]{1,0:T(8,128)(2,1)S(1)} %pad_maximum_fusion.1), channel_id=1, source_target_pairs={{0,1},{1,0},{2,3},{3,2},{4,5},{5,4},{6,7},{7,6},{8,9},{9,8},{10,11... | collective-permute-start | bytes 2359304 | tf_op jit(solution)/shard_map/ppermute | solution.py:79
  41.5 1.2 copy-start.6
  41.5 1.6 %copy-start.8 = (bf16[1536,512]{1,0:T(8,128)(2,1)}, bf16[1536,512]{1,0:T(8,128)(2,1)S(1)}, u32[]{:S(2)}) copy-start(bf16[1536,512]{1,0:T(8,128)(2,1)S(1)} %get-tuple-element.49) | copy-start | bytes 4718596
  41.6 2.0 %copy-start.10 = (bf16[1536,512]{1,0:T(8,128)(2,1)}, bf16[1536,512]{1,0:T(8,128)(2,1)S(1)}, u32[]{:S(2)}) copy-start(bf16[1536,512]{1,0:T(8,128)(2,1)S(1)} %slice_dynamic-update-slice_fusion.14) | copy-start | bytes 4718596
  43.6 20.2 %collective-permute-start.9 = (f32[256,512]{1,0:T(8,128)S(1)}, f32[256,512]{1,0:T(8,128)S(1)}, u32[]{:S(2)}, u32[]{:S(2)}) collective-permute-start(f32[256,512]{1,0:T(8,128)S(1)} %fusion.1), channel_id=1, source_target_pairs={{0,2},{1,7},{2,0},{3,5},{4,6},{5,3},{6,4},{7,1},{8,10},{9,15},{10,... | collective-permute-start | bytes 1572872 | tf_op jit(solution)/shard_map/ppermute | solution.py:93
  48.1 5.0 %copy-start.7 = (bf16[1536,512]{1,0:T(8,128)(2,1)S(1)}, bf16[1536,512]{1,0:T(8,128)(2,1)}, u32[]{:S(2)}) copy-start(bf16[1536,512]{1,0:T(8,128)(2,1)} %copy-done.6) | copy-start | bytes 4718596
  48.2 5.0 %copy-start.9 = (bf16[1536,512]{1,0:T(8,128)(2,1)S(1)}, bf16[1536,512]{1,0:T(8,128)(2,1)}, u32[]{:S(2)}) copy-start(bf16[1536,512]{1,0:T(8,128)(2,1)} %copy-done.8) | copy-start | bytes 4718596
  48.2 5.0 %copy-start.11 = (bf16[1536,512]{1,0:T(8,128)(2,1)S(1)}, bf16[1536,512]{1,0:T(8,128)(2,1)}, u32[]{:S(2)}) copy-start(bf16[1536,512]{1,0:T(8,128)(2,1)} %copy-done.10) | copy-start | bytes 4718596
  50.9 24.7 %collective-permute-start.8 = (f32[256,512]{1,0:T(8,128)S(1)}, f32[256,512]{1,0:T(8,128)S(1)}, u32[]{:S(2)}, u32[]{:S(2)}) collective-permute-start(f32[256,512]{1,0:T(8,128)S(1)} %fusion.10), channel_id=1, source_target_pairs={{0,2},{1,7},{2,0},{3,5},{4,6},{5,3},{6,4},{7,1},{8,10},{9,15},{10,... | collective-permute-start | bytes 1572872 | tf_op jit(solution)/shard_map/ppermute | solution.py:94
  55.0 27.5 %copy-start = (f32[1,1,256,512]{3,2,1,0:T(8,128)S(1)}, f32[1,1,256,512]{3,2,1,0:T(8,128)}, u32[]{:S(2)}) copy-start(f32[1,1,256,512]{3,2,1,0:T(8,128)} %param.11) | copy-start | bytes 1572868
  55.0 27.5 %copy-start.1 = (f32[1,1,256,512]{3,2,1,0:T(8,128)S(1)}, f32[1,1,256,512]{3,2,1,0:T(8,128)}, u32[]{:S(2)}) copy-start(f32[1,1,256,512]{3,2,1,0:T(8,128)} %param.10) | copy-start | bytes 1572868
  55.0 27.5 %copy-start.3 = (f32[1,1,256,512]{3,2,1,0:T(8,128)S(1)}, f32[1,1,256,512]{3,2,1,0:T(8,128)}, u32[]{:S(2)}) copy-start(f32[1,1,256,512]{3,2,1,0:T(8,128)} %param.9) | copy-start | bytes 1572868
  63.9 18.7 %collective-permute-start.10 = (f32[256,512]{1,0:T(8,128)S(1)}, f32[256,512]{1,0:T(8,128)S(1)}, u32[]{:S(2)}, u32[]{:S(2)}) collective-permute-start(f32[256,512]{1,0:T(8,128)S(1)} %add.115), channel_id=1, source_target_pairs={{0,6},{1,3},{2,4},{3,1},{4,2},{5,7},{6,0},{7,5},{8,14},{9,11},{10,... | collective-permute-start | bytes 1572872 | tf_op jit(solution)/shard_map/ppermute | solution.py:96
  83.0 29.8 %copy-start.4 = (f32[1,16,512]{2,1,0:T(8,128)S(1)}, f32[1,16,512]{2,1,0:T(8,128)}, u32[]{:S(2)}) copy-start(f32[1,16,512]{2,1,0:T(8,128)} %param.12) | copy-start | bytes 98308
  83.0 29.8 %copy-start.5 = (f32[1,16,512]{2,1,0:T(8,128)S(1)}, f32[1,16,512]{2,1,0:T(8,128)}, u32[]{:S(2)}) copy-start(f32[1,16,512]{2,1,0:T(8,128)} %param.13) | copy-start | bytes 98308
  113.7 19.6 %all-to-all-start.1 = ((f32[16,16,512]{2,1,0:T(8,128)}), f32[16,16,512]{2,1,0:T(8,128)S(1)}, u32[]{:S(2)}, u32[]{:S(2)}) async-start(f32[16,16,512]{2,1,0:T(8,128)} %broadcast_in_dim.18), calls=%async_computation.1 | async-start | bytes 1048576 | tf_op jit(solution)/shard_map/all_to_all | solution.py:130

commit v7 on v6

--- a/solution.py
+++ b/solution.py
@@ -46,6 +46,10 @@
     return pairs
 
 
+def after(value, other):
+    return jnp.where(other == other, value, jnp.zeros_like(value))
+
+
 def body(acts, upstream, inner_params, first_moment, second_moment, anchor, outer_momentum):
     members = lax.axis_size("replica")
     me = lax.axis_index("fsdp")
@@ -59,8 +63,13 @@
     def a_for(dest):
         return lax.dynamic_slice(a, (0, dest * 2 * rows), (count, 2 * rows))
 
+    first = y & 1
+
     def u_for(core):
-        return [lax.dynamic_slice(u, (0, (k * 2 + core) * cols), (count, cols)) for k in range(2)]
+        return [
+            lax.dynamic_slice(u, (0, (k * 2 + core) * cols), (count, cols))
+            for k in (first, 1 - first)
+        ]
 
     def pieces(t):
         return [t[i * count : (i + 1) * count] for i in range(t.shape[0] // count)]
@@ -72,27 +81,27 @@
     )
     two = lax.ppermute(jnp.concatenate([a_for(x ^ far), *u_own], 0), "fsdp", x_pairs(1))
     one_swap = lax.ppermute(u_swap, "fsdp", x_pairs(0))
-    two_swap = lax.ppermute(u_swap, "fsdp", x_pairs(1))
+    two_swap = pieces(lax.ppermute(u_swap, "fsdp", x_pairs(1)))
     three = lax.ppermute(one[count:], "fsdp", x_pairs(1))
-    three_swap = lax.ppermute(one_swap, "fsdp", x_pairs(1))
+    three_swap = pieces(lax.ppermute(one_swap, "fsdp", x_pairs(1)))
     a_core = jnp.concatenate([a_for(x), one[:count], two[:count], three[2 * count :]], 0)
     a_other = lax.ppermute(a_core, "fsdp", core_pairs())
     other = pieces(a_other)
     a_all = jnp.concatenate([a_core, other[0], other[2], other[1], other[3]], 0)
     u_core = [u_own, pieces(one)[1:3], pieces(two)[1:], pieces(three)[:2]]
-    u_rest = [pieces(u_swap), pieces(one_swap), pieces(two_swap), pieces(three_swap)]
-    u_all = jnp.concatenate([jnp.concatenate([p[k] for p in u_core + u_rest], 0) for k in range(2)], 1)
+    u_rest = [pieces(u_swap), pieces(one_swap), two_swap, three_swap]
+    u_all = [jnp.concatenate([p[k] for p in u_core + u_rest], 0) for k in range(2)]
 
-    def part(dest):
+    def part(dest, side):
         left = lax.dynamic_slice(a_all, (0, (dest >> 1) * rows), (8 * count, rows))
-        right = lax.dynamic_slice(u_all, (0, (dest & 1) * cols), (8 * count, cols))
         return lax.dot_general(
-            left, right, (((0,), (0,)), ((), ())), preferred_element_type=jnp.float32
+            left, u_all[side], (((0,), (0,)), ((), ())), preferred_element_type=jnp.float32
         )
 
-    g_far = lax.ppermute(part(y ^ 2), "fsdp", y_pairs(0))
-    g_near = lax.ppermute(part(y ^ near), "fsdp", y_pairs(0))
-    kept_far, kept = lax.optimization_barrier((part(y ^ far), part(y)))
+    sent_far = part(y ^ 2, 0)
+    g_far = lax.ppermute(sent_far, "fsdp", y_pairs(0))
+    g_near = lax.ppermute(after(part(y ^ near, 1), sent_far), "fsdp", y_pairs(0))
+    kept_far, kept = lax.optimization_barrier((part(y ^ far, 1), part(y, 0)))
     g_two = lax.ppermute(kept_far + g_far, "fsdp", y_pairs(1))
     gradient = kept + g_near + g_two
 

time: 135 us -> 133 us (0.985)
  matrix products: 5.46 us -> 2.46 us
  waiting for transfers between devices: 49.8 us -> 52.5 us
    dot_general x4, matrix products: 5.46 us -> 2.46 us  [part(): lax.dot_general(left, u_all[side], (((0,), (0,)), ((), ())), preferred_el...]
    ppermute x4, waiting for transfers between devices: 20.1 us -> 22.9 us  [the longest x1 11.5 us: body(): g_far = lax.ppermute(sent_far, 'fsdp', y_pairs(0))]
    unnamed x33 -> x24, local copies, waits for them, and re-layouts: 4.23 us -> 4.42 us
  transfers between devices with their start and end apart: 12 -> 12, of which waited for: 10 -> 10; matrix products, arithmetic and copies ran while one was open for 8% -> 6% of each run, Pallas kernels for 0% -> 0%
where the time goes in v7:
time: 133 us
  waiting for transfers between devices  52.5 us (39%)
  starting transfers between devices  37.6 us (28%)
  blocking collectives  29.8 us (22%)
  local copies, waits for them, and re-layouts  6.74 us (5%)
  other arithmetic  2.52 us (2%)
  matrix products  2.46 us (2%)
    all_to_all x1, blocking collectives, body(): lax.all_to_all(stepped.reshape(members, slice_rows, cols), 'replica', spl...  29.8 us
    all_to_all x1, waiting for transfers between devices, body(): lax.all_to_all(jnp.broadcast_to(new_params[None], (members, slice_rows, c...  13.2 us
    ppermute x1, waiting for transfers between devices, body(): g_far = lax.ppermute(sent_far, 'fsdp', y_pairs(0))  11.5 us
    ppermute x1, waiting for transfers between devices, body(): lax.ppermute(after(part(y ^ near, 1), sent_far), 'fsdp', y_pairs(0))  7.17 us
    ppermute x1, waiting for transfers between devices, body(): g_two = lax.ppermute(kept_far + g_far, 'fsdp', y_pairs(1))  6.93 us
    ppermute x1, waiting for transfers between devices, body(): three = lax.ppermute(one[count:], 'fsdp', x_pairs(1))  5.04 us
    ppermute x1, starting transfers between devices, body(): g_two = lax.ppermute(kept_far + g_far, 'fsdp', y_pairs(1))  4.59 us
    all_to_all x1, starting transfers between devices, body(): lax.all_to_all(jnp.broadcast_to(new_params[None], (members, slice_rows, c...  4.55 us
  transfers between devices with their start and end apart: 12, of which 10 were waited for; matrix products, arithmetic and copies ran while one was open for 6% of the time, Pallas kernels for 0%

profile of v7, /device:TPU:14, one launch (start us, length us, event | category | flops | bytes accessed | tf_op | source)
XLA Modules:
  0.0 132.6 jit_solution(4196013866391936268)
XLA Ops:
  0.6 0.0 copy-start.2
  0.7 1.3 %dynamic-slice_bitcast_fusion.1 = (bf16[192,512]{1,0:T(8,128)(2,1)S(1)}, bf16[192,512]{1,0:T(8,128)(2,1)S(1)}, bf16[192,512]{1,0:T(8,128)(2,1)S(1)}, bf16[192,512]{1,0:T(8,128)(2,1)S(1)}) fusion(bf16[1,192,2048]{2,1,0:T(8,128)(2,1)} %param.8, s32[]{:T(128)S(6)} %select_n.56, s32[]{:T(128)S(6)} %select_n.51, s32[]{:T(128)S(6)} %select_n.50, s32[]{:T(128)S(6)} %select_n.57), kind=kLoop, calls=%fused_computation.46 | loop fusion | bytes 1572880 | tf_op jit(solution)/shard_map/dynamic_slice | solution.py:70
  2.0 0.1 copy-done.2
  2.2 0.1 pad_maximum_fusion
  2.2 2.7 %collective-permute-start = (bf16[768,512]{1,0:T(8,128)(2,1)S(1)}, bf16[768,512]{1,0:T(8,128)(2,1)S(1)}, u32[]{:S(2)}, u32[]{:S(2)}) collective-permute-start(bf16[768,512]{1,0:T(8,128)(2,1)S(1)} %pad_maximum_fusion), channel_id=1, source_target_pairs={{0,8},{1,25},{2,10},{3,27},{4,12},{5,29},{6,14},{7,31},{8,0},{9,17... | collective-permute-start | bytes 2359304 | tf_op jit(solution)/shard_map/ppermute | solution.py:79
  5.0 1.9 %collective-permute-start.4 = (bf16[384,512]{1,0:T(8,128)(2,1)S(1)}, bf16[384,512]{1,0:T(8,128)(2,1)}, u32[]{:S(2)}, u32[]{:S(2)}) collective-permute-start(bf16[384,512]{1,0:T(8,128)(2,1)S(1)} %pad_maximum_fusion.3), channel_id=1, source_target_pairs={{0,1},{1,0},{2,3},{3,2},{4,5},{5,4},{6,7},{7,6},{8,9},{9,8},{10,11... | collective-permute-start | bytes 1179656 | tf_op jit(solution)/shard_map/ppermute | solution.py:78
  6.9 1.8 %collective-permute-done.4 = bf16[384,512]{1,0:T(8,128)(2,1)} collective-permute-done((bf16[384,512]{1,0:T(8,128)(2,1)S(1)}, bf16[384,512]{1,0:T(8,128)(2,1)}, u32[]{:S(2)}, u32[]{:S(2)}) %collective-permute-start.4) | collective-permute-done | bytes 393248 | tf_op jit(solution)/shard_map/ppermute | solution.py:78
  8.8 3.1 %collective-permute-start.5 = (bf16[384,512]{1,0:T(8,128)(2,1)}, bf16[384,512]{1,0:T(8,128)(2,1)}, u32[]{:S(2)}, u32[]{:S(2)}) collective-permute-start(bf16[384,512]{1,0:T(8,128)(2,1)} %collective-permute-done.4), channel_id=1, source_target_pairs={{0,8},{1,25},{2,10},{3,27},{4,12},{5,29},{6,14},{7,31},{8,0},{9,17... | collective-permute-start | bytes 1179656 | tf_op jit(solution)/shard_map/ppermute | solution.py:83
  11.9 2.5 %collective-permute-start.1 = (bf16[576,512]{1,0:T(8,128)(2,1)S(1)}, bf16[576,512]{1,0:T(8,128)(2,1)}, u32[]{:S(2)}, u32[]{:S(2)}) collective-permute-start(bf16[576,512]{1,0:T(8,128)(2,1)S(1)} %pad_maximum_fusion.2), channel_id=1, source_target_pairs={{0,24},{1,9},{2,26},{3,11},{4,28},{5,13},{6,30},{7,15},{8,16},{9,1... | collective-permute-start | bytes 1769480 | tf_op jit(solution)/shard_map/ppermute | solution.py:82
  14.5 1.6 %collective-permute-done = bf16[768,512]{1,0:T(8,128)(2,1)S(1)} collective-permute-done((bf16[768,512]{1,0:T(8,128)(2,1)S(1)}, bf16[768,512]{1,0:T(8,128)(2,1)S(1)}, u32[]{:S(2)}, u32[]{:S(2)}) %collective-permute-start) | collective-permute-done | bytes 786464 | tf_op jit(solution)/shard_map/ppermute | solution.py:79
  16.1 2.9 %collective-permute-start.2 = (bf16[576,512]{1,0:T(8,128)(2,1)S(1)}, bf16[576,512]{1,0:T(8,128)(2,1)S(1)}, u32[]{:S(2)}, u32[]{:S(2)}) collective-permute-start(bf16[576,512]{1,0:T(8,128)(2,1)S(1)} %slice.90), channel_id=1, source_target_pairs={{0,24},{1,9},{2,26},{3,11},{4,28},{5,13},{6,30},{7,15},{8,16},{9,1... | collective-permute-start | bytes 1769480 | tf_op jit(solution)/shard_map/ppermute | solution.py:85
  19.1 4.1 %collective-permute-start.6 = (bf16[384,512]{1,0:T(8,128)(2,1)}, bf16[384,512]{1,0:T(8,128)(2,1)S(1)}, u32[]{:S(2)}, u32[]{:S(2)}) collective-permute-start(bf16[384,512]{1,0:T(8,128)(2,1)} %collective-permute-done.4), channel_id=1, source_target_pairs={{0,24},{1,9},{2,26},{3,11},{4,28},{5,13},{6,30},{7,15},{8,16},{9,1... | collective-permute-start | bytes 1179656 | tf_op jit(solution)/shard_map/ppermute | solution.py:84
  23.3 0.5 collective-permute-done.5
  23.8 2.4 %collective-permute-start.7 = (bf16[384,512]{1,0:T(8,128)(2,1)}, bf16[384,512]{1,0:T(8,128)(2,1)S(1)}, u32[]{:S(2)}, u32[]{:S(2)}) collective-permute-start(bf16[384,512]{1,0:T(8,128)(2,1)} %collective-permute-done.5), channel_id=1, source_target_pairs={{0,24},{1,9},{2,26},{3,11},{4,28},{5,13},{6,30},{7,15},{8,16},{9,1... | collective-permute-start | bytes 1179656 | tf_op jit(solution)/shard_map/ppermute | solution.py:86
  26.2 0.1 slice_dynamic-update-slice_fusion.6
  26.3 0.5 collective-permute-done.1
  26.8 1.2 slice_dynamic-update-slice_fusion.5
  28.0 5.0 %collective-permute-done.2 = bf16[576,512]{1,0:T(8,128)(2,1)S(1)} collective-permute-done((bf16[576,512]{1,0:T(8,128)(2,1)S(1)}, bf16[576,512]{1,0:T(8,128)(2,1)S(1)}, u32[]{:S(2)}, u32[]{:S(2)}) %collective-permute-start.2) | collective-permute-done | bytes 589856 | tf_op jit(solution)/shard_map/ppermute | solution.py:85
  33.0 0.1 slice_dynamic-update-slice_fusion.4
  33.1 0.1 pad_maximum_fusion.1
  33.2 1.9 %collective-permute-start.3 = (bf16[768,512]{1,0:T(8,128)(2,1)S(1)}, bf16[768,512]{1,0:T(8,128)(2,1)S(1)}, u32[]{:S(2)}, u32[]{:S(2)}) collective-permute-start(bf16[768,512]{1,0:T(8,128)(2,1)S(1)} %pad_maximum_fusion.1), channel_id=1, source_target_pairs={{0,1},{1,0},{2,3},{3,2},{4,5},{5,4},{6,7},{7,6},{8,9},{9,8},{10,11... | collective-permute-start | bytes 2359304 | tf_op jit(solution)/shard_map/ppermute | solution.py:88
  35.1 1.0 slice_dynamic-update-slice_fusion.3
  36.2 1.0 slice_dynamic-update-slice_fusion.2
  37.2 0.0 collective-permute-done.6
  37.3 4.2 %collective-permute-done.7 = bf16[384,512]{1,0:T(8,128)(2,1)S(1)} collective-permute-done((bf16[384,512]{1,0:T(8,128)(2,1)}, bf16[384,512]{1,0:T(8,128)(2,1)S(1)}, u32[]{:S(2)}, u32[]{:S(2)}) %collective-permute-start.7) | collective-permute-done | bytes 393248 | tf_op jit(solution)/shard_map/ppermute | solution.py:86
  41.5 0.0 collective-permute-done.3
  41.6 0.6 fusion.2
  42.2 4.5 %collective-permute-start.9 = (f32[256,512]{1,0:T(8,128)S(1)}, f32[256,512]{1,0:T(8,128)S(1)}, u32[]{:S(2)}, u32[]{:S(2)}) collective-permute-start(f32[256,512]{1,0:T(8,128)S(1)} %fusion.2), channel_id=1, source_target_pairs={{0,2},{1,7},{2,0},{3,5},{4,6},{5,3},{6,4},{7,1},{8,10},{9,15},{10,... | collective-permute-start | bytes 1572872 | tf_op jit(solution)/shard_map/ppermute | solution.py:102
  46.7 0.6 compare_select_fusion
  47.3 2.2 %collective-permute-start.8 = (f32[256,512]{1,0:T(8,128)S(1)}, f32[256,512]{1,0:T(8,128)S(1)}, u32[]{:S(2)}, u32[]{:S(2)}) collective-permute-start(f32[256,512]{1,0:T(8,128)S(1)} %compare_select_fusion), channel_id=1, source_target_pairs={{0,2},{1,7},{2,0},{3,5},{4,6},{5,3},{6,4},{7,1},{8,10},{9,15},{10,... | collective-permute-start | bytes 1572872 | tf_op jit(solution)/shard_map/ppermute | solution.py:103
  49.6 0.6 fusion.4
  50.2 0.0 copy-start
  50.2 0.0 copy-start.1
  50.2 0.0 copy-start.3
  50.2 0.6 fusion.6
  50.9 11.5 %collective-permute-done.9 = f32[256,512]{1,0:T(8,128)S(1)} collective-permute-done((f32[256,512]{1,0:T(8,128)S(1)}, f32[256,512]{1,0:T(8,128)S(1)}, u32[]{:S(2)}, u32[]{:S(2)}) %collective-permute-start.9) | collective-permute-done | bytes 524320 | tf_op jit(solution)/shard_map/ppermute | solution.py:102
  62.4 0.1 add.106
  62.5 4.6 %collective-permute-start.10 = (f32[256,512]{1,0:T(8,128)S(1)}, f32[256,512]{1,0:T(8,128)S(1)}, u32[]{:S(2)}, u32[]{:S(2)}) collective-permute-start(f32[256,512]{1,0:T(8,128)S(1)} %add.106), channel_id=1, source_target_pairs={{0,6},{1,3},{2,4},{3,1},{4,2},{5,7},{6,0},{7,5},{8,14},{9,11},{10,... | collective-permute-start | bytes 1572872 | tf_op jit(solution)/shard_map/ppermute | solution.py:105
  67.1 7.2 %collective-permute-done.8 = f32[256,512]{1,0:T(8,128)S(1)} collective-permute-done((f32[256,512]{1,0:T(8,128)S(1)}, f32[256,512]{1,0:T(8,128)S(1)}, u32[]{:S(2)}, u32[]{:S(2)}) %collective-permute-start.8) | collective-permute-done | bytes 524320 | tf_op jit(solution)/shard_map/ppermute | solution.py:103
  74.2 6.9 %collective-permute-done.10 = f32[256,512]{1,0:T(8,128)S(1)} collective-permute-done((f32[256,512]{1,0:T(8,128)S(1)}, f32[256,512]{1,0:T(8,128)S(1)}, u32[]{:S(2)}, u32[]{:S(2)}) %collective-permute-start.10) | collective-permute-done | bytes 524320 | tf_op jit(solution)/shard_map/ppermute | solution.py:105
  81.2 0.0 copy-done
  81.2 0.0 copy-done.1
  81.2 0.0 copy-done.3
  81.2 0.4 fusion.14
  81.6 0.0 copy-start.4
  81.6 0.0 copy-start.5
  81.6 29.8 %all_to_all.10 = f32[16,16,512]{2,1,0:T(8,128)S(1)} all-to-all(f32[16,16,512]{2,1,0:T(8,128)S(1)} %bitcast.49), channel_id=1, replica_groups=mesh['replica'=16,'fsdp'=32] {'replica'}, dimensions={0} | all-to-all | bytes 1048576 | tf_op jit(solution)/shard_map/all_to_all | solution.py:128
  111.4 0.0 copy-done.4
  111.4 0.0 copy-done.5
  111.4 0.9 broadcast_in_dim.22
  112.3 4.5 %all-to-all-start.1 = ((f32[16,16,512]{2,1,0:T(8,128)}), f32[16,16,512]{2,1,0:T(8,128)S(1)}, u32[]{:S(2)}, u32[]{:S(2)}) async-start(f32[16,16,512]{2,1,0:T(8,128)} %broadcast_in_dim.22), calls=%async_computation.1 | async-start | bytes 1048576 | tf_op jit(solution)/shard_map/all_to_all | solution.py:139
  116.8 1.2 fusion.16
  118.0 0.6 add_bitcast_fusion.1
  118.6 13.2 %all-to-all-done.1 = f32[16,16,512]{2,1,0:T(8,128)S(1)} async-done(((f32[16,16,512]{2,1,0:T(8,128)}), f32[16,16,512]{2,1,0:T(8,128)S(1)}, u32[]{:S(2)}, u32[]{:S(2)}) %all-to-all-start.1) | async-done | bytes 524320 | tf_op jit(solution)/shard_map/all_to_all | solution.py:139
  131.8 0.8 copy.33
  (15 shorter events, 0.4 us)
Async XLA Ops:
  0.6 1.5 %copy-start.2 = (bf16[1,192,2048]{2,1,0:T(8,128)(2,1)S(1)}, bf16[1,192,2048]{2,1,0:T(8,128)(2,1)}, u32[]{:S(2)}) copy-start(bf16[1,192,2048]{2,1,0:T(8,128)(2,1)} %param.7) | copy-start | bytes 2359300
  2.2 13.9 %collective-permute-start = (bf16[768,512]{1,0:T(8,128)(2,1)S(1)}, bf16[768,512]{1,0:T(8,128)(2,1)S(1)}, u32[]{:S(2)}, u32[]{:S(2)}) collective-permute-start(bf16[768,512]{1,0:T(8,128)(2,1)S(1)} %pad_maximum_fusion), channel_id=1, source_target_pairs={{0,8},{1,25},{2,10},{3,27},{4,12},{5,29},{6,14},{7,31},{8,0},{9,17... | collective-permute-start | bytes 2359304 | tf_op jit(solution)/shard_map/ppermute | solution.py:79
  5.0 3.7 %collective-permute-start.4 = (bf16[384,512]{1,0:T(8,128)(2,1)S(1)}, bf16[384,512]{1,0:T(8,128)(2,1)}, u32[]{:S(2)}, u32[]{:S(2)}) collective-permute-start(bf16[384,512]{1,0:T(8,128)(2,1)S(1)} %pad_maximum_fusion.3), channel_id=1, source_target_pairs={{0,1},{1,0},{2,3},{3,2},{4,5},{5,4},{6,7},{7,6},{8,9},{9,8},{10,11... | collective-permute-start | bytes 1179656 | tf_op jit(solution)/shard_map/ppermute | solution.py:78
  8.8 15.0 %collective-permute-start.5 = (bf16[384,512]{1,0:T(8,128)(2,1)}, bf16[384,512]{1,0:T(8,128)(2,1)}, u32[]{:S(2)}, u32[]{:S(2)}) collective-permute-start(bf16[384,512]{1,0:T(8,128)(2,1)} %collective-permute-done.4), channel_id=1, source_target_pairs={{0,8},{1,25},{2,10},{3,27},{4,12},{5,29},{6,14},{7,31},{8,0},{9,17... | collective-permute-start | bytes 1179656 | tf_op jit(solution)/shard_map/ppermute | solution.py:83
  11.9 14.9 %collective-permute-start.1 = (bf16[576,512]{1,0:T(8,128)(2,1)S(1)}, bf16[576,512]{1,0:T(8,128)(2,1)}, u32[]{:S(2)}, u32[]{:S(2)}) collective-permute-start(bf16[576,512]{1,0:T(8,128)(2,1)S(1)} %pad_maximum_fusion.2), channel_id=1, source_target_pairs={{0,24},{1,9},{2,26},{3,11},{4,28},{5,13},{6,30},{7,15},{8,16},{9,1... | collective-permute-start | bytes 1769480 | tf_op jit(solution)/shard_map/ppermute | solution.py:82
  16.1 16.9 %collective-permute-start.2 = (bf16[576,512]{1,0:T(8,128)(2,1)S(1)}, bf16[576,512]{1,0:T(8,128)(2,1)S(1)}, u32[]{:S(2)}, u32[]{:S(2)}) collective-permute-start(bf16[576,512]{1,0:T(8,128)(2,1)S(1)} %slice.90), channel_id=1, source_target_pairs={{0,24},{1,9},{2,26},{3,11},{4,28},{5,13},{6,30},{7,15},{8,16},{9,1... | collective-permute-start | bytes 1769480 | tf_op jit(solution)/shard_map/ppermute | solution.py:85
  19.1 18.1 %collective-permute-start.6 = (bf16[384,512]{1,0:T(8,128)(2,1)}, bf16[384,512]{1,0:T(8,128)(2,1)S(1)}, u32[]{:S(2)}, u32[]{:S(2)}) collective-permute-start(bf16[384,512]{1,0:T(8,128)(2,1)} %collective-permute-done.4), channel_id=1, source_target_pairs={{0,24},{1,9},{2,26},{3,11},{4,28},{5,13},{6,30},{7,15},{8,16},{9,1... | collective-permute-start | bytes 1179656 | tf_op jit(solution)/shard_map/ppermute | solution.py:84
  23.8 17.7 %collective-permute-start.7 = (bf16[384,512]{1,0:T(8,128)(2,1)}, bf16[384,512]{1,0:T(8,128)(2,1)S(1)}, u32[]{:S(2)}, u32[]{:S(2)}) collective-permute-start(bf16[384,512]{1,0:T(8,128)(2,1)} %collective-permute-done.5), channel_id=1, source_target_pairs={{0,24},{1,9},{2,26},{3,11},{4,28},{5,13},{6,30},{7,15},{8,16},{9,1... | collective-permute-start | bytes 1179656 | tf_op jit(solution)/shard_map/ppermute | solution.py:86
  33.2 8.3 %collective-permute-start.3 = (bf16[768,512]{1,0:T(8,128)(2,1)S(1)}, bf16[768,512]{1,0:T(8,128)(2,1)S(1)}, u32[]{:S(2)}, u32[]{:S(2)}) collective-permute-start(bf16[768,512]{1,0:T(8,128)(2,1)S(1)} %pad_maximum_fusion.1), channel_id=1, source_target_pairs={{0,1},{1,0},{2,3},{3,2},{4,5},{5,4},{6,7},{7,6},{8,9},{9,8},{10,11... | collective-permute-start | bytes 2359304 | tf_op jit(solution)/shard_map/ppermute | solution.py:88
  42.2 20.2 %collective-permute-start.9 = (f32[256,512]{1,0:T(8,128)S(1)}, f32[256,512]{1,0:T(8,128)S(1)}, u32[]{:S(2)}, u32[]{:S(2)}) collective-permute-start(f32[256,512]{1,0:T(8,128)S(1)} %fusion.2), channel_id=1, source_target_pairs={{0,2},{1,7},{2,0},{3,5},{4,6},{5,3},{6,4},{7,1},{8,10},{9,15},{10,... | collective-permute-start | bytes 1572872 | tf_op jit(solution)/shard_map/ppermute | solution.py:102
  47.3 26.9 %collective-permute-start.8 = (f32[256,512]{1,0:T(8,128)S(1)}, f32[256,512]{1,0:T(8,128)S(1)}, u32[]{:S(2)}, u32[]{:S(2)}) collective-permute-start(f32[256,512]{1,0:T(8,128)S(1)} %compare_select_fusion), channel_id=1, source_target_pairs={{0,2},{1,7},{2,0},{3,5},{4,6},{5,3},{6,4},{7,1},{8,10},{9,15},{10,... | collective-permute-start | bytes 1572872 | tf_op jit(solution)/shard_map/ppermute | solution.py:103
  50.2 31.0 %copy-start = (f32[1,1,256,512]{3,2,1,0:T(8,128)S(1)}, f32[1,1,256,512]{3,2,1,0:T(8,128)}, u32[]{:S(2)}) copy-start(f32[1,1,256,512]{3,2,1,0:T(8,128)} %param.11) | copy-start | bytes 1572868
  50.2 30.9 %copy-start.1 = (f32[1,1,256,512]{3,2,1,0:T(8,128)S(1)}, f32[1,1,256,512]{3,2,1,0:T(8,128)}, u32[]{:S(2)}) copy-start(f32[1,1,256,512]{3,2,1,0:T(8,128)} %param.10) | copy-start | bytes 1572868
  50.2 30.9 %copy-start.3 = (f32[1,1,256,512]{3,2,1,0:T(8,128)S(1)}, f32[1,1,256,512]{3,2,1,0:T(8,128)}, u32[]{:S(2)}) copy-start(f32[1,1,256,512]{3,2,1,0:T(8,128)} %param.9) | copy-start | bytes 1572868
  62.5 18.7 %collective-permute-start.10 = (f32[256,512]{1,0:T(8,128)S(1)}, f32[256,512]{1,0:T(8,128)S(1)}, u32[]{:S(2)}, u32[]{:S(2)}) collective-permute-start(f32[256,512]{1,0:T(8,128)S(1)} %add.106), channel_id=1, source_target_pairs={{0,6},{1,3},{2,4},{3,1},{4,2},{5,7},{6,0},{7,5},{8,14},{9,11},{10,... | collective-permute-start | bytes 1572872 | tf_op jit(solution)/shard_map/ppermute | solution.py:105
  81.6 29.8 %copy-start.4 = (f32[1,16,512]{2,1,0:T(8,128)S(1)}, f32[1,16,512]{2,1,0:T(8,128)}, u32[]{:S(2)}) copy-start(f32[1,16,512]{2,1,0:T(8,128)} %param.12) | copy-start | bytes 98308
  81.6 29.8 %copy-start.5 = (f32[1,16,512]{2,1,0:T(8,128)S(1)}, f32[1,16,512]{2,1,0:T(8,128)}, u32[]{:S(2)}) copy-start(f32[1,16,512]{2,1,0:T(8,128)} %param.13) | copy-start | bytes 98308
  112.3 19.5 %all-to-all-start.1 = ((f32[16,16,512]{2,1,0:T(8,128)}), f32[16,16,512]{2,1,0:T(8,128)S(1)}, u32[]{:S(2)}, u32[]{:S(2)}) async-start(f32[16,16,512]{2,1,0:T(8,128)} %broadcast_in_dim.22), calls=%async_computation.1 | async-start | bytes 1048576 | tf_op jit(solution)/shard_map/all_to_all | solution.py:139

commit v8 on v7

--- a/solution.py
+++ b/solution.py
@@ -134,10 +134,13 @@
         return momentum, anchor - outer_rate * (pseudo + outer_mu * momentum)
 
     mean = jnp.sum(parts, axis=0) / members
-    _, new_params = outer(mean, anchor[0], outer_momentum[0])
+    copies = (members, slice_rows, cols)
+    _, new_params = outer(
+        *(jnp.broadcast_to(t, copies) for t in (mean, anchor[0], outer_momentum[0]))
+    )
     new_momentum, _ = outer(*lax.optimization_barrier((mean, anchor[0], outer_momentum[0])))
     gathered = lax.all_to_all(
-        jnp.broadcast_to(new_params[None], (members, slice_rows, cols)),
+        new_params,
         "replica",
         split_axis=0,
         concat_axis=0,

time: 133 us -> 133 us (level)
  no operation moved by 1% of the time
where the time goes in v8:
time: 133 us
  waiting for transfers between devices  52.6 us (40%)
  starting transfers between devices  37.6 us (28%)
  blocking collectives  29.8 us (22%)
  local copies, waits for them, and re-layouts  6.74 us (5%)
  other arithmetic  2.51 us (2%)
  matrix products  2.46 us (2%)
    all_to_all x1, blocking collectives, body(): lax.all_to_all(stepped.reshape(members, slice_rows, cols), 'replica', spl...  29.8 us
    all_to_all x1, waiting for transfers between devices, body(): lax.all_to_all(new_params, 'replica', split_axis=0, concat_axis=0, tiled=...  13.2 us
    ppermute x1, waiting for transfers between devices, body(): g_far = lax.ppermute(sent_far, 'fsdp', y_pairs(0))  11.5 us
    ppermute x1, waiting for transfers between devices, body(): lax.ppermute(after(part(y ^ near, 1), sent_far), 'fsdp', y_pairs(0))  7.17 us
    ppermute x1, waiting for transfers between devices, body(): g_two = lax.ppermute(kept_far + g_far, 'fsdp', y_pairs(1))  6.93 us
    ppermute x1, waiting for transfers between devices, body(): three = lax.ppermute(one[count:], 'fsdp', x_pairs(1))  5.04 us
    ppermute x1, starting transfers between devices, body(): g_two = lax.ppermute(kept_far + g_far, 'fsdp', y_pairs(1))  4.59 us
    all_to_all x1, starting transfers between devices, body(): lax.all_to_all(new_params, 'replica', split_axis=0, concat_axis=0, tiled=...  4.55 us
  transfers between devices with their start and end apart: 12, of which 10 were waited for; matrix products, arithmetic and copies ran while one was open for 6% of the time, Pallas kernels for 0%

profile of v8, /device:TPU:14, one launch (start us, length us, event | category | flops | bytes accessed | tf_op | source)
XLA Modules:
  0.0 132.6 jit_solution(17185346045961270725)
XLA Ops:
  0.6 0.0 copy-start.2
  0.7 1.3 %dynamic-slice_bitcast_fusion.1 = (bf16[192,512]{1,0:T(8,128)(2,1)S(1)}, bf16[192,512]{1,0:T(8,128)(2,1)S(1)}, bf16[192,512]{1,0:T(8,128)(2,1)S(1)}, bf16[192,512]{1,0:T(8,128)(2,1)S(1)}) fusion(bf16[1,192,2048]{2,1,0:T(8,128)(2,1)} %param.8, s32[]{:T(128)S(6)} %select_n.56, s32[]{:T(128)S(6)} %select_n.51, s32[]{:T(128)S(6)} %select_n.50, s32[]{:T(128)S(6)} %select_n.57), kind=kLoop, calls=%fused_computation.46 | loop fusion | bytes 1572880 | tf_op jit(solution)/shard_map/dynamic_slice | solution.py:70
  2.0 0.1 copy-done.2
  2.2 0.1 pad_maximum_fusion
  2.2 2.7 %collective-permute-start = (bf16[768,512]{1,0:T(8,128)(2,1)S(1)}, bf16[768,512]{1,0:T(8,128)(2,1)S(1)}, u32[]{:S(2)}, u32[]{:S(2)}) collective-permute-start(bf16[768,512]{1,0:T(8,128)(2,1)S(1)} %pad_maximum_fusion), channel_id=1, source_target_pairs={{0,8},{1,25},{2,10},{3,27},{4,12},{5,29},{6,14},{7,31},{8,0},{9,17... | collective-permute-start | bytes 2359304 | tf_op jit(solution)/shard_map/ppermute | solution.py:79
  5.0 1.9 %collective-permute-start.4 = (bf16[384,512]{1,0:T(8,128)(2,1)S(1)}, bf16[384,512]{1,0:T(8,128)(2,1)}, u32[]{:S(2)}, u32[]{:S(2)}) collective-permute-start(bf16[384,512]{1,0:T(8,128)(2,1)S(1)} %pad_maximum_fusion.3), channel_id=1, source_target_pairs={{0,1},{1,0},{2,3},{3,2},{4,5},{5,4},{6,7},{7,6},{8,9},{9,8},{10,11... | collective-permute-start | bytes 1179656 | tf_op jit(solution)/shard_map/ppermute | solution.py:78
  6.9 1.8 %collective-permute-done.4 = bf16[384,512]{1,0:T(8,128)(2,1)} collective-permute-done((bf16[384,512]{1,0:T(8,128)(2,1)S(1)}, bf16[384,512]{1,0:T(8,128)(2,1)}, u32[]{:S(2)}, u32[]{:S(2)}) %collective-permute-start.4) | collective-permute-done | bytes 393248 | tf_op jit(solution)/shard_map/ppermute | solution.py:78
  8.8 3.1 %collective-permute-start.5 = (bf16[384,512]{1,0:T(8,128)(2,1)}, bf16[384,512]{1,0:T(8,128)(2,1)}, u32[]{:S(2)}, u32[]{:S(2)}) collective-permute-start(bf16[384,512]{1,0:T(8,128)(2,1)} %collective-permute-done.4), channel_id=1, source_target_pairs={{0,8},{1,25},{2,10},{3,27},{4,12},{5,29},{6,14},{7,31},{8,0},{9,17... | collective-permute-start | bytes 1179656 | tf_op jit(solution)/shard_map/ppermute | solution.py:83
  11.9 2.5 %collective-permute-start.1 = (bf16[576,512]{1,0:T(8,128)(2,1)S(1)}, bf16[576,512]{1,0:T(8,128)(2,1)}, u32[]{:S(2)}, u32[]{:S(2)}) collective-permute-start(bf16[576,512]{1,0:T(8,128)(2,1)S(1)} %pad_maximum_fusion.2), channel_id=1, source_target_pairs={{0,24},{1,9},{2,26},{3,11},{4,28},{5,13},{6,30},{7,15},{8,16},{9,1... | collective-permute-start | bytes 1769480 | tf_op jit(solution)/shard_map/ppermute | solution.py:82
  14.5 1.6 %collective-permute-done = bf16[768,512]{1,0:T(8,128)(2,1)S(1)} collective-permute-done((bf16[768,512]{1,0:T(8,128)(2,1)S(1)}, bf16[768,512]{1,0:T(8,128)(2,1)S(1)}, u32[]{:S(2)}, u32[]{:S(2)}) %collective-permute-start) | collective-permute-done | bytes 786464 | tf_op jit(solution)/shard_map/ppermute | solution.py:79
  16.1 2.9 %collective-permute-start.2 = (bf16[576,512]{1,0:T(8,128)(2,1)S(1)}, bf16[576,512]{1,0:T(8,128)(2,1)S(1)}, u32[]{:S(2)}, u32[]{:S(2)}) collective-permute-start(bf16[576,512]{1,0:T(8,128)(2,1)S(1)} %slice.90), channel_id=1, source_target_pairs={{0,24},{1,9},{2,26},{3,11},{4,28},{5,13},{6,30},{7,15},{8,16},{9,1... | collective-permute-start | bytes 1769480 | tf_op jit(solution)/shard_map/ppermute | solution.py:85
  19.1 4.1 %collective-permute-start.6 = (bf16[384,512]{1,0:T(8,128)(2,1)}, bf16[384,512]{1,0:T(8,128)(2,1)S(1)}, u32[]{:S(2)}, u32[]{:S(2)}) collective-permute-start(bf16[384,512]{1,0:T(8,128)(2,1)} %collective-permute-done.4), channel_id=1, source_target_pairs={{0,24},{1,9},{2,26},{3,11},{4,28},{5,13},{6,30},{7,15},{8,16},{9,1... | collective-permute-start | bytes 1179656 | tf_op jit(solution)/shard_map/ppermute | solution.py:84
  23.3 0.5 collective-permute-done.5
  23.8 2.4 %collective-permute-start.7 = (bf16[384,512]{1,0:T(8,128)(2,1)}, bf16[384,512]{1,0:T(8,128)(2,1)S(1)}, u32[]{:S(2)}, u32[]{:S(2)}) collective-permute-start(bf16[384,512]{1,0:T(8,128)(2,1)} %collective-permute-done.5), channel_id=1, source_target_pairs={{0,24},{1,9},{2,26},{3,11},{4,28},{5,13},{6,30},{7,15},{8,16},{9,1... | collective-permute-start | bytes 1179656 | tf_op jit(solution)/shard_map/ppermute | solution.py:86
  26.2 0.1 slice_dynamic-update-slice_fusion.6
  26.3 0.5 collective-permute-done.1
  26.8 1.2 slice_dynamic-update-slice_fusion.5
  28.0 5.0 %collective-permute-done.2 = bf16[576,512]{1,0:T(8,128)(2,1)S(1)} collective-permute-done((bf16[576,512]{1,0:T(8,128)(2,1)S(1)}, bf16[576,512]{1,0:T(8,128)(2,1)S(1)}, u32[]{:S(2)}, u32[]{:S(2)}) %collective-permute-start.2) | collective-permute-done | bytes 589856 | tf_op jit(solution)/shard_map/ppermute | solution.py:85
  33.0 0.1 slice_dynamic-update-slice_fusion.4
  33.1 0.1 pad_maximum_fusion.1
  33.2 1.9 %collective-permute-start.3 = (bf16[768,512]{1,0:T(8,128)(2,1)S(1)}, bf16[768,512]{1,0:T(8,128)(2,1)S(1)}, u32[]{:S(2)}, u32[]{:S(2)}) collective-permute-start(bf16[768,512]{1,0:T(8,128)(2,1)S(1)} %pad_maximum_fusion.1), channel_id=1, source_target_pairs={{0,1},{1,0},{2,3},{3,2},{4,5},{5,4},{6,7},{7,6},{8,9},{9,8},{10,11... | collective-permute-start | bytes 2359304 | tf_op jit(solution)/shard_map/ppermute | solution.py:88
  35.1 1.0 slice_dynamic-update-slice_fusion.3
  36.2 1.0 slice_dynamic-update-slice_fusion.2
  37.2 0.0 collective-permute-done.6
  37.3 4.2 %collective-permute-done.7 = bf16[384,512]{1,0:T(8,128)(2,1)S(1)} collective-permute-done((bf16[384,512]{1,0:T(8,128)(2,1)}, bf16[384,512]{1,0:T(8,128)(2,1)S(1)}, u32[]{:S(2)}, u32[]{:S(2)}) %collective-permute-start.7) | collective-permute-done | bytes 393248 | tf_op jit(solution)/shard_map/ppermute | solution.py:86
  41.5 0.0 collective-permute-done.3
  41.6 0.6 fusion.2
  42.2 4.5 %collective-permute-start.9 = (f32[256,512]{1,0:T(8,128)S(1)}, f32[256,512]{1,0:T(8,128)S(1)}, u32[]{:S(2)}, u32[]{:S(2)}) collective-permute-start(f32[256,512]{1,0:T(8,128)S(1)} %fusion.2), channel_id=1, source_target_pairs={{0,2},{1,7},{2,0},{3,5},{4,6},{5,3},{6,4},{7,1},{8,10},{9,15},{10,... | collective-permute-start | bytes 1572872 | tf_op jit(solution)/shard_map/ppermute | solution.py:102
  46.7 0.6 compare_select_fusion
  47.3 2.2 %collective-permute-start.8 = (f32[256,512]{1,0:T(8,128)S(1)}, f32[256,512]{1,0:T(8,128)S(1)}, u32[]{:S(2)}, u32[]{:S(2)}) collective-permute-start(f32[256,512]{1,0:T(8,128)S(1)} %compare_select_fusion), channel_id=1, source_target_pairs={{0,2},{1,7},{2,0},{3,5},{4,6},{5,3},{6,4},{7,1},{8,10},{9,15},{10,... | collective-permute-start | bytes 1572872 | tf_op jit(solution)/shard_map/ppermute | solution.py:103
  49.6 0.6 fusion.4
  50.2 0.0 copy-start
  50.2 0.0 copy-start.1
  50.2 0.0 copy-start.3
  50.2 0.6 fusion.6
  50.9 11.5 %collective-permute-done.9 = f32[256,512]{1,0:T(8,128)S(1)} collective-permute-done((f32[256,512]{1,0:T(8,128)S(1)}, f32[256,512]{1,0:T(8,128)S(1)}, u32[]{:S(2)}, u32[]{:S(2)}) %collective-permute-start.9) | collective-permute-done | bytes 524320 | tf_op jit(solution)/shard_map/ppermute | solution.py:102
  62.4 0.1 add.106
  62.5 4.6 %collective-permute-start.10 = (f32[256,512]{1,0:T(8,128)S(1)}, f32[256,512]{1,0:T(8,128)S(1)}, u32[]{:S(2)}, u32[]{:S(2)}) collective-permute-start(f32[256,512]{1,0:T(8,128)S(1)} %add.106), channel_id=1, source_target_pairs={{0,6},{1,3},{2,4},{3,1},{4,2},{5,7},{6,0},{7,5},{8,14},{9,11},{10,... | collective-permute-start | bytes 1572872 | tf_op jit(solution)/shard_map/ppermute | solution.py:105
  67.1 7.2 %collective-permute-done.8 = f32[256,512]{1,0:T(8,128)S(1)} collective-permute-done((f32[256,512]{1,0:T(8,128)S(1)}, f32[256,512]{1,0:T(8,128)S(1)}, u32[]{:S(2)}, u32[]{:S(2)}) %collective-permute-start.8) | collective-permute-done | bytes 524320 | tf_op jit(solution)/shard_map/ppermute | solution.py:103
  74.2 6.9 %collective-permute-done.10 = f32[256,512]{1,0:T(8,128)S(1)} collective-permute-done((f32[256,512]{1,0:T(8,128)S(1)}, f32[256,512]{1,0:T(8,128)S(1)}, u32[]{:S(2)}, u32[]{:S(2)}) %collective-permute-start.10) | collective-permute-done | bytes 524320 | tf_op jit(solution)/shard_map/ppermute | solution.py:105
  81.2 0.0 copy-done
  81.2 0.0 copy-done.1
  81.2 0.0 copy-done.3
  81.2 0.4 fusion.14
  81.6 0.0 copy-start.4
  81.6 0.0 copy-start.5
  81.6 29.8 %all_to_all.10 = f32[16,16,512]{2,1,0:T(8,128)S(1)} all-to-all(f32[16,16,512]{2,1,0:T(8,128)S(1)} %bitcast.45), channel_id=1, replica_groups=mesh['replica'=16,'fsdp'=32] {'replica'}, dimensions={0} | all-to-all | bytes 1048576 | tf_op jit(solution)/shard_map/all_to_all | solution.py:128
  111.4 0.0 copy-done.4
  111.4 0.0 copy-done.5
  111.4 0.9 broadcast_in_dim.18
  112.3 4.5 %all-to-all-start.1 = ((f32[16,16,512]{2,1,0:T(8,128)}), f32[16,16,512]{2,1,0:T(8,128)S(1)}, u32[]{:S(2)}, u32[]{:S(2)}) async-start(f32[16,16,512]{2,1,0:T(8,128)} %broadcast_in_dim.18), calls=%async_computation.1 | async-start | bytes 1048576 | tf_op jit(solution)/shard_map/all_to_all | solution.py:142
  116.8 1.2 fusion.16
  118.0 0.6 add_bitcast_fusion.1
  118.6 13.2 %all-to-all-done.1 = f32[16,16,512]{2,1,0:T(8,128)S(1)} async-done(((f32[16,16,512]{2,1,0:T(8,128)}), f32[16,16,512]{2,1,0:T(8,128)S(1)}, u32[]{:S(2)}, u32[]{:S(2)}) %all-to-all-start.1) | async-done | bytes 524320 | tf_op jit(solution)/shard_map/all_to_all | solution.py:142
  131.8 0.8 copy.33
  (14 shorter events, 0.4 us)
Async XLA Ops:
  0.6 1.5 %copy-start.2 = (bf16[1,192,2048]{2,1,0:T(8,128)(2,1)S(1)}, bf16[1,192,2048]{2,1,0:T(8,128)(2,1)}, u32[]{:S(2)}) copy-start(bf16[1,192,2048]{2,1,0:T(8,128)(2,1)} %param.7) | copy-start | bytes 2359300
  2.2 13.9 %collective-permute-start = (bf16[768,512]{1,0:T(8,128)(2,1)S(1)}, bf16[768,512]{1,0:T(8,128)(2,1)S(1)}, u32[]{:S(2)}, u32[]{:S(2)}) collective-permute-start(bf16[768,512]{1,0:T(8,128)(2,1)S(1)} %pad_maximum_fusion), channel_id=1, source_target_pairs={{0,8},{1,25},{2,10},{3,27},{4,12},{5,29},{6,14},{7,31},{8,0},{9,17... | collective-permute-start | bytes 2359304 | tf_op jit(solution)/shard_map/ppermute | solution.py:79
  5.0 3.7 %collective-permute-start.4 = (bf16[384,512]{1,0:T(8,128)(2,1)S(1)}, bf16[384,512]{1,0:T(8,128)(2,1)}, u32[]{:S(2)}, u32[]{:S(2)}) collective-permute-start(bf16[384,512]{1,0:T(8,128)(2,1)S(1)} %pad_maximum_fusion.3), channel_id=1, source_target_pairs={{0,1},{1,0},{2,3},{3,2},{4,5},{5,4},{6,7},{7,6},{8,9},{9,8},{10,11... | collective-permute-start | bytes 1179656 | tf_op jit(solution)/shard_map/ppermute | solution.py:78
  8.8 15.0 %collective-permute-start.5 = (bf16[384,512]{1,0:T(8,128)(2,1)}, bf16[384,512]{1,0:T(8,128)(2,1)}, u32[]{:S(2)}, u32[]{:S(2)}) collective-permute-start(bf16[384,512]{1,0:T(8,128)(2,1)} %collective-permute-done.4), channel_id=1, source_target_pairs={{0,8},{1,25},{2,10},{3,27},{4,12},{5,29},{6,14},{7,31},{8,0},{9,17... | collective-permute-start | bytes 1179656 | tf_op jit(solution)/shard_map/ppermute | solution.py:83
  11.9 14.9 %collective-permute-start.1 = (bf16[576,512]{1,0:T(8,128)(2,1)S(1)}, bf16[576,512]{1,0:T(8,128)(2,1)}, u32[]{:S(2)}, u32[]{:S(2)}) collective-permute-start(bf16[576,512]{1,0:T(8,128)(2,1)S(1)} %pad_maximum_fusion.2), channel_id=1, source_target_pairs={{0,24},{1,9},{2,26},{3,11},{4,28},{5,13},{6,30},{7,15},{8,16},{9,1... | collective-permute-start | bytes 1769480 | tf_op jit(solution)/shard_map/ppermute | solution.py:82
  16.1 16.9 %collective-permute-start.2 = (bf16[576,512]{1,0:T(8,128)(2,1)S(1)}, bf16[576,512]{1,0:T(8,128)(2,1)S(1)}, u32[]{:S(2)}, u32[]{:S(2)}) collective-permute-start(bf16[576,512]{1,0:T(8,128)(2,1)S(1)} %slice.90), channel_id=1, source_target_pairs={{0,24},{1,9},{2,26},{3,11},{4,28},{5,13},{6,30},{7,15},{8,16},{9,1... | collective-permute-start | bytes 1769480 | tf_op jit(solution)/shard_map/ppermute | solution.py:85
  19.1 18.1 %collective-permute-start.6 = (bf16[384,512]{1,0:T(8,128)(2,1)}, bf16[384,512]{1,0:T(8,128)(2,1)S(1)}, u32[]{:S(2)}, u32[]{:S(2)}) collective-permute-start(bf16[384,512]{1,0:T(8,128)(2,1)} %collective-permute-done.4), channel_id=1, source_target_pairs={{0,24},{1,9},{2,26},{3,11},{4,28},{5,13},{6,30},{7,15},{8,16},{9,1... | collective-permute-start | bytes 1179656 | tf_op jit(solution)/shard_map/ppermute | solution.py:84
  23.8 17.7 %collective-permute-start.7 = (bf16[384,512]{1,0:T(8,128)(2,1)}, bf16[384,512]{1,0:T(8,128)(2,1)S(1)}, u32[]{:S(2)}, u32[]{:S(2)}) collective-permute-start(bf16[384,512]{1,0:T(8,128)(2,1)} %collective-permute-done.5), channel_id=1, source_target_pairs={{0,24},{1,9},{2,26},{3,11},{4,28},{5,13},{6,30},{7,15},{8,16},{9,1... | collective-permute-start | bytes 1179656 | tf_op jit(solution)/shard_map/ppermute | solution.py:86
  33.2 8.3 %collective-permute-start.3 = (bf16[768,512]{1,0:T(8,128)(2,1)S(1)}, bf16[768,512]{1,0:T(8,128)(2,1)S(1)}, u32[]{:S(2)}, u32[]{:S(2)}) collective-permute-start(bf16[768,512]{1,0:T(8,128)(2,1)S(1)} %pad_maximum_fusion.1), channel_id=1, source_target_pairs={{0,1},{1,0},{2,3},{3,2},{4,5},{5,4},{6,7},{7,6},{8,9},{9,8},{10,11... | collective-permute-start | bytes 2359304 | tf_op jit(solution)/shard_map/ppermute | solution.py:88
  42.2 20.2 %collective-permute-start.9 = (f32[256,512]{1,0:T(8,128)S(1)}, f32[256,512]{1,0:T(8,128)S(1)}, u32[]{:S(2)}, u32[]{:S(2)}) collective-permute-start(f32[256,512]{1,0:T(8,128)S(1)} %fusion.2), channel_id=1, source_target_pairs={{0,2},{1,7},{2,0},{3,5},{4,6},{5,3},{6,4},{7,1},{8,10},{9,15},{10,... | collective-permute-start | bytes 1572872 | tf_op jit(solution)/shard_map/ppermute | solution.py:102
  47.3 26.9 %collective-permute-start.8 = (f32[256,512]{1,0:T(8,128)S(1)}, f32[256,512]{1,0:T(8,128)S(1)}, u32[]{:S(2)}, u32[]{:S(2)}) collective-permute-start(f32[256,512]{1,0:T(8,128)S(1)} %compare_select_fusion), channel_id=1, source_target_pairs={{0,2},{1,7},{2,0},{3,5},{4,6},{5,3},{6,4},{7,1},{8,10},{9,15},{10,... | collective-permute-start | bytes 1572872 | tf_op jit(solution)/shard_map/ppermute | solution.py:103
  50.2 31.0 %copy-start = (f32[1,1,256,512]{3,2,1,0:T(8,128)S(1)}, f32[1,1,256,512]{3,2,1,0:T(8,128)}, u32[]{:S(2)}) copy-start(f32[1,1,256,512]{3,2,1,0:T(8,128)} %param.11) | copy-start | bytes 1572868
  50.2 30.9 %copy-start.1 = (f32[1,1,256,512]{3,2,1,0:T(8,128)S(1)}, f32[1,1,256,512]{3,2,1,0:T(8,128)}, u32[]{:S(2)}) copy-start(f32[1,1,256,512]{3,2,1,0:T(8,128)} %param.10) | copy-start | bytes 1572868
  50.2 30.9 %copy-start.3 = (f32[1,1,256,512]{3,2,1,0:T(8,128)S(1)}, f32[1,1,256,512]{3,2,1,0:T(8,128)}, u32[]{:S(2)}) copy-start(f32[1,1,256,512]{3,2,1,0:T(8,128)} %param.9) | copy-start | bytes 1572868
  62.5 18.7 %collective-permute-start.10 = (f32[256,512]{1,0:T(8,128)S(1)}, f32[256,512]{1,0:T(8,128)S(1)}, u32[]{:S(2)}, u32[]{:S(2)}) collective-permute-start(f32[256,512]{1,0:T(8,128)S(1)} %add.106), channel_id=1, source_target_pairs={{0,6},{1,3},{2,4},{3,1},{4,2},{5,7},{6,0},{7,5},{8,14},{9,11},{10,... | collective-permute-start | bytes 1572872 | tf_op jit(solution)/shard_map/ppermute | solution.py:105
  81.6 29.8 %copy-start.4 = (f32[1,16,512]{2,1,0:T(8,128)S(1)}, f32[1,16,512]{2,1,0:T(8,128)}, u32[]{:S(2)}) copy-start(f32[1,16,512]{2,1,0:T(8,128)} %param.13) | copy-start | bytes 98308
  81.6 29.8 %copy-start.5 = (f32[1,16,512]{2,1,0:T(8,128)S(1)}, f32[1,16,512]{2,1,0:T(8,128)}, u32[]{:S(2)}) copy-start(f32[1,16,512]{2,1,0:T(8,128)} %param.12) | copy-start | bytes 98308
  112.3 19.5 %all-to-all-start.1 = ((f32[16,16,512]{2,1,0:T(8,128)}), f32[16,16,512]{2,1,0:T(8,128)S(1)}, u32[]{:S(2)}, u32[]{:S(2)}) async-start(f32[16,16,512]{2,1,0:T(8,128)} %broadcast_in_dim.18), calls=%async_computation.1 | async-start | bytes 1048576 | tf_op jit(solution)/shard_map/all_to_all | solution.py:142

commit v9 on v8

--- a/solution.py
+++ b/solution.py
@@ -128,17 +128,17 @@
     parts = lax.all_to_all(
         stepped.reshape(members, slice_rows, cols), "replica", split_axis=0, concat_axis=0, tiled=True
     )
-    def outer(mean, anchor, momentum):
-        pseudo = anchor - mean
+    def outer(total, anchor, momentum):
+        pseudo = anchor - total / members
         momentum = outer_mu * momentum + pseudo
         return momentum, anchor - outer_rate * (pseudo + outer_mu * momentum)
 
-    mean = jnp.sum(parts, axis=0) / members
+    total = jnp.sum(parts, axis=0)
     copies = (members, slice_rows, cols)
     _, new_params = outer(
-        *(jnp.broadcast_to(t, copies) for t in (mean, anchor[0], outer_momentum[0]))
+        *(jnp.broadcast_to(t, copies) for t in (total, anchor[0], outer_momentum[0]))
     )
-    new_momentum, _ = outer(*lax.optimization_barrier((mean, anchor[0], outer_momentum[0])))
+    new_momentum, _ = outer(*lax.optimization_barrier((total, anchor[0], outer_momentum[0])))
     gathered = lax.all_to_all(
         new_params,
         "replica",

time: 133 us -> 133 us (level)
  no operation moved by 1% of the time
where the time goes in v9:
time: 133 us
  waiting for transfers between devices  52.6 us (40%)
  starting transfers between devices  37.6 us (28%)
  blocking collectives  29.8 us (22%)
  local copies, waits for them, and re-layouts  6.74 us (5%)
  other arithmetic  2.51 us (2%)
  matrix products  2.46 us (2%)
    all_to_all x1, blocking collectives, body(): lax.all_to_all(stepped.reshape(members, slice_rows, cols), 'replica', spl...  29.8 us
    all_to_all x1, waiting for transfers between devices, body(): lax.all_to_all(new_params, 'replica', split_axis=0, concat_axis=0, tiled=...  13.2 us
    ppermute x1, waiting for transfers between devices, body(): g_far = lax.ppermute(sent_far, 'fsdp', y_pairs(0))  11.5 us
    ppermute x1, waiting for transfers between devices, body(): lax.ppermute(after(part(y ^ near, 1), sent_far), 'fsdp', y_pairs(0))  7.17 us
    ppermute x1, waiting for transfers between devices, body(): g_two = lax.ppermute(kept_far + g_far, 'fsdp', y_pairs(1))  6.93 us
    ppermute x1, waiting for transfers between devices, body(): three = lax.ppermute(one[count:], 'fsdp', x_pairs(1))  5.04 us
    ppermute x1, starting transfers between devices, body(): g_two = lax.ppermute(kept_far + g_far, 'fsdp', y_pairs(1))  4.59 us
    all_to_all x1, starting transfers between devices, body(): lax.all_to_all(new_params, 'replica', split_axis=0, concat_axis=0, tiled=...  4.55 us
  transfers between devices with their start and end apart: 12, of which 10 were waited for; matrix products, arithmetic and copies ran while one was open for 6% of the time, Pallas kernels for 0%

profile of v9, /device:TPU:14, one launch (start us, length us, event | category | flops | bytes accessed | tf_op | source)
XLA Modules:
  0.0 132.6 jit_solution(16683723798833264336)
XLA Ops:
  0.6 0.0 copy-start.2
  0.7 1.3 %dynamic-slice_bitcast_fusion.1 = (bf16[192,512]{1,0:T(8,128)(2,1)S(1)}, bf16[192,512]{1,0:T(8,128)(2,1)S(1)}, bf16[192,512]{1,0:T(8,128)(2,1)S(1)}, bf16[192,512]{1,0:T(8,128)(2,1)S(1)}) fusion(bf16[1,192,2048]{2,1,0:T(8,128)(2,1)} %param.8, s32[]{:T(128)S(6)} %select_n.56, s32[]{:T(128)S(6)} %select_n.51, s32[]{:T(128)S(6)} %select_n.50, s32[]{:T(128)S(6)} %select_n.57), kind=kLoop, calls=%fused_computation.46 | loop fusion | bytes 1572880 | tf_op jit(solution)/shard_map/dynamic_slice | solution.py:70
  2.0 0.1 copy-done.2
  2.2 0.1 pad_maximum_fusion
  2.2 2.7 %collective-permute-start = (bf16[768,512]{1,0:T(8,128)(2,1)S(1)}, bf16[768,512]{1,0:T(8,128)(2,1)S(1)}, u32[]{:S(2)}, u32[]{:S(2)}) collective-permute-start(bf16[768,512]{1,0:T(8,128)(2,1)S(1)} %pad_maximum_fusion), channel_id=1, source_target_pairs={{0,8},{1,25},{2,10},{3,27},{4,12},{5,29},{6,14},{7,31},{8,0},{9,17... | collective-permute-start | bytes 2359304 | tf_op jit(solution)/shard_map/ppermute | solution.py:79
  5.0 1.9 %collective-permute-start.4 = (bf16[384,512]{1,0:T(8,128)(2,1)S(1)}, bf16[384,512]{1,0:T(8,128)(2,1)}, u32[]{:S(2)}, u32[]{:S(2)}) collective-permute-start(bf16[384,512]{1,0:T(8,128)(2,1)S(1)} %pad_maximum_fusion.3), channel_id=1, source_target_pairs={{0,1},{1,0},{2,3},{3,2},{4,5},{5,4},{6,7},{7,6},{8,9},{9,8},{10,11... | collective-permute-start | bytes 1179656 | tf_op jit(solution)/shard_map/ppermute | solution.py:78
  6.9 1.8 %collective-permute-done.4 = bf16[384,512]{1,0:T(8,128)(2,1)} collective-permute-done((bf16[384,512]{1,0:T(8,128)(2,1)S(1)}, bf16[384,512]{1,0:T(8,128)(2,1)}, u32[]{:S(2)}, u32[]{:S(2)}) %collective-permute-start.4) | collective-permute-done | bytes 393248 | tf_op jit(solution)/shard_map/ppermute | solution.py:78
  8.8 3.1 %collective-permute-start.5 = (bf16[384,512]{1,0:T(8,128)(2,1)}, bf16[384,512]{1,0:T(8,128)(2,1)}, u32[]{:S(2)}, u32[]{:S(2)}) collective-permute-start(bf16[384,512]{1,0:T(8,128)(2,1)} %collective-permute-done.4), channel_id=1, source_target_pairs={{0,8},{1,25},{2,10},{3,27},{4,12},{5,29},{6,14},{7,31},{8,0},{9,17... | collective-permute-start | bytes 1179656 | tf_op jit(solution)/shard_map/ppermute | solution.py:83
  11.9 2.5 %collective-permute-start.1 = (bf16[576,512]{1,0:T(8,128)(2,1)S(1)}, bf16[576,512]{1,0:T(8,128)(2,1)}, u32[]{:S(2)}, u32[]{:S(2)}) collective-permute-start(bf16[576,512]{1,0:T(8,128)(2,1)S(1)} %pad_maximum_fusion.2), channel_id=1, source_target_pairs={{0,24},{1,9},{2,26},{3,11},{4,28},{5,13},{6,30},{7,15},{8,16},{9,1... | collective-permute-start | bytes 1769480 | tf_op jit(solution)/shard_map/ppermute | solution.py:82
  14.5 1.6 %collective-permute-done = bf16[768,512]{1,0:T(8,128)(2,1)S(1)} collective-permute-done((bf16[768,512]{1,0:T(8,128)(2,1)S(1)}, bf16[768,512]{1,0:T(8,128)(2,1)S(1)}, u32[]{:S(2)}, u32[]{:S(2)}) %collective-permute-start) | collective-permute-done | bytes 786464 | tf_op jit(solution)/shard_map/ppermute | solution.py:79
  16.1 2.9 %collective-permute-start.2 = (bf16[576,512]{1,0:T(8,128)(2,1)S(1)}, bf16[576,512]{1,0:T(8,128)(2,1)S(1)}, u32[]{:S(2)}, u32[]{:S(2)}) collective-permute-start(bf16[576,512]{1,0:T(8,128)(2,1)S(1)} %slice.90), channel_id=1, source_target_pairs={{0,24},{1,9},{2,26},{3,11},{4,28},{5,13},{6,30},{7,15},{8,16},{9,1... | collective-permute-start | bytes 1769480 | tf_op jit(solution)/shard_map/ppermute | solution.py:85
  19.1 4.1 %collective-permute-start.6 = (bf16[384,512]{1,0:T(8,128)(2,1)}, bf16[384,512]{1,0:T(8,128)(2,1)S(1)}, u32[]{:S(2)}, u32[]{:S(2)}) collective-permute-start(bf16[384,512]{1,0:T(8,128)(2,1)} %collective-permute-done.4), channel_id=1, source_target_pairs={{0,24},{1,9},{2,26},{3,11},{4,28},{5,13},{6,30},{7,15},{8,16},{9,1... | collective-permute-start | bytes 1179656 | tf_op jit(solution)/shard_map/ppermute | solution.py:84
  23.3 0.5 collective-permute-done.5
  23.8 2.4 %collective-permute-start.7 = (bf16[384,512]{1,0:T(8,128)(2,1)}, bf16[384,512]{1,0:T(8,128)(2,1)S(1)}, u32[]{:S(2)}, u32[]{:S(2)}) collective-permute-start(bf16[384,512]{1,0:T(8,128)(2,1)} %collective-permute-done.5), channel_id=1, source_target_pairs={{0,24},{1,9},{2,26},{3,11},{4,28},{5,13},{6,30},{7,15},{8,16},{9,1... | collective-permute-start | bytes 1179656 | tf_op jit(solution)/shard_map/ppermute | solution.py:86
  26.2 0.1 slice_dynamic-update-slice_fusion.6
  26.3 0.5 collective-permute-done.1
  26.8 1.2 slice_dynamic-update-slice_fusion.5
  28.0 5.0 %collective-permute-done.2 = bf16[576,512]{1,0:T(8,128)(2,1)S(1)} collective-permute-done((bf16[576,512]{1,0:T(8,128)(2,1)S(1)}, bf16[576,512]{1,0:T(8,128)(2,1)S(1)}, u32[]{:S(2)}, u32[]{:S(2)}) %collective-permute-start.2) | collective-permute-done | bytes 589856 | tf_op jit(solution)/shard_map/ppermute | solution.py:85
  33.0 0.1 slice_dynamic-update-slice_fusion.4
  33.1 0.1 pad_maximum_fusion.1
  33.2 1.9 %collective-permute-start.3 = (bf16[768,512]{1,0:T(8,128)(2,1)S(1)}, bf16[768,512]{1,0:T(8,128)(2,1)S(1)}, u32[]{:S(2)}, u32[]{:S(2)}) collective-permute-start(bf16[768,512]{1,0:T(8,128)(2,1)S(1)} %pad_maximum_fusion.1), channel_id=1, source_target_pairs={{0,1},{1,0},{2,3},{3,2},{4,5},{5,4},{6,7},{7,6},{8,9},{9,8},{10,11... | collective-permute-start | bytes 2359304 | tf_op jit(solution)/shard_map/ppermute | solution.py:88
  35.1 1.0 slice_dynamic-update-slice_fusion.3
  36.2 1.0 slice_dynamic-update-slice_fusion.2
  37.2 0.0 collective-permute-done.6
  37.3 4.2 %collective-permute-done.7 = bf16[384,512]{1,0:T(8,128)(2,1)S(1)} collective-permute-done((bf16[384,512]{1,0:T(8,128)(2,1)}, bf16[384,512]{1,0:T(8,128)(2,1)S(1)}, u32[]{:S(2)}, u32[]{:S(2)}) %collective-permute-start.7) | collective-permute-done | bytes 393248 | tf_op jit(solution)/shard_map/ppermute | solution.py:86
  41.5 0.0 collective-permute-done.3
  41.6 0.6 fusion.2
  42.2 4.5 %collective-permute-start.9 = (f32[256,512]{1,0:T(8,128)S(1)}, f32[256,512]{1,0:T(8,128)S(1)}, u32[]{:S(2)}, u32[]{:S(2)}) collective-permute-start(f32[256,512]{1,0:T(8,128)S(1)} %fusion.2), channel_id=1, source_target_pairs={{0,2},{1,7},{2,0},{3,5},{4,6},{5,3},{6,4},{7,1},{8,10},{9,15},{10,... | collective-permute-start | bytes 1572872 | tf_op jit(solution)/shard_map/ppermute | solution.py:102
  46.7 0.6 compare_select_fusion
  47.3 2.2 %collective-permute-start.8 = (f32[256,512]{1,0:T(8,128)S(1)}, f32[256,512]{1,0:T(8,128)S(1)}, u32[]{:S(2)}, u32[]{:S(2)}) collective-permute-start(f32[256,512]{1,0:T(8,128)S(1)} %compare_select_fusion), channel_id=1, source_target_pairs={{0,2},{1,7},{2,0},{3,5},{4,6},{5,3},{6,4},{7,1},{8,10},{9,15},{10,... | collective-permute-start | bytes 1572872 | tf_op jit(solution)/shard_map/ppermute | solution.py:103
  49.6 0.6 fusion.4
  50.2 0.0 copy-start
  50.2 0.0 copy-start.1
  50.2 0.0 copy-start.3
  50.2 0.6 fusion.6
  50.9 11.5 %collective-permute-done.9 = f32[256,512]{1,0:T(8,128)S(1)} collective-permute-done((f32[256,512]{1,0:T(8,128)S(1)}, f32[256,512]{1,0:T(8,128)S(1)}, u32[]{:S(2)}, u32[]{:S(2)}) %collective-permute-start.9) | collective-permute-done | bytes 524320 | tf_op jit(solution)/shard_map/ppermute | solution.py:102
  62.4 0.1 add.106
  62.5 4.6 %collective-permute-start.10 = (f32[256,512]{1,0:T(8,128)S(1)}, f32[256,512]{1,0:T(8,128)S(1)}, u32[]{:S(2)}, u32[]{:S(2)}) collective-permute-start(f32[256,512]{1,0:T(8,128)S(1)} %add.106), channel_id=1, source_target_pairs={{0,6},{1,3},{2,4},{3,1},{4,2},{5,7},{6,0},{7,5},{8,14},{9,11},{10,... | collective-permute-start | bytes 1572872 | tf_op jit(solution)/shard_map/ppermute | solution.py:105
  67.1 7.2 %collective-permute-done.8 = f32[256,512]{1,0:T(8,128)S(1)} collective-permute-done((f32[256,512]{1,0:T(8,128)S(1)}, f32[256,512]{1,0:T(8,128)S(1)}, u32[]{:S(2)}, u32[]{:S(2)}) %collective-permute-start.8) | collective-permute-done | bytes 524320 | tf_op jit(solution)/shard_map/ppermute | solution.py:103
  74.2 6.9 %collective-permute-done.10 = f32[256,512]{1,0:T(8,128)S(1)} collective-permute-done((f32[256,512]{1,0:T(8,128)S(1)}, f32[256,512]{1,0:T(8,128)S(1)}, u32[]{:S(2)}, u32[]{:S(2)}) %collective-permute-start.10) | collective-permute-done | bytes 524320 | tf_op jit(solution)/shard_map/ppermute | solution.py:105
  81.2 0.0 copy-done
  81.2 0.0 copy-done.1
  81.2 0.0 copy-done.3
  81.2 0.4 fusion.14
  81.6 0.0 copy-start.4
  81.6 0.0 copy-start.5
  81.6 29.8 %all_to_all.10 = f32[16,16,512]{2,1,0:T(8,128)S(1)} all-to-all(f32[16,16,512]{2,1,0:T(8,128)S(1)} %bitcast.45), channel_id=1, replica_groups=mesh['replica'=16,'fsdp'=32] {'replica'}, dimensions={0} | all-to-all | bytes 1048576 | tf_op jit(solution)/shard_map/all_to_all | solution.py:128
  111.4 0.0 copy-done.4
  111.4 0.0 copy-done.5
  111.4 0.9 broadcast_in_dim.18
  112.3 4.5 %all-to-all-start.1 = ((f32[16,16,512]{2,1,0:T(8,128)}), f32[16,16,512]{2,1,0:T(8,128)S(1)}, u32[]{:S(2)}, u32[]{:S(2)}) async-start(f32[16,16,512]{2,1,0:T(8,128)} %broadcast_in_dim.18), calls=%async_computation.1 | async-start | bytes 1048576 | tf_op jit(solution)/shard_map/all_to_all | solution.py:142
  116.8 1.2 fusion.16
  118.0 0.6 add_bitcast_fusion.1
  118.6 13.2 %all-to-all-done.1 = f32[16,16,512]{2,1,0:T(8,128)S(1)} async-done(((f32[16,16,512]{2,1,0:T(8,128)}), f32[16,16,512]{2,1,0:T(8,128)S(1)}, u32[]{:S(2)}, u32[]{:S(2)}) %all-to-all-start.1) | async-done | bytes 524320 | tf_op jit(solution)/shard_map/all_to_all | solution.py:142
  131.8 0.8 copy.33
  (14 shorter events, 0.4 us)
Async XLA Ops:
  0.6 1.5 %copy-start.2 = (bf16[1,192,2048]{2,1,0:T(8,128)(2,1)S(1)}, bf16[1,192,2048]{2,1,0:T(8,128)(2,1)}, u32[]{:S(2)}) copy-start(bf16[1,192,2048]{2,1,0:T(8,128)(2,1)} %param.7) | copy-start | bytes 2359300
  2.2 13.9 %collective-permute-start = (bf16[768,512]{1,0:T(8,128)(2,1)S(1)}, bf16[768,512]{1,0:T(8,128)(2,1)S(1)}, u32[]{:S(2)}, u32[]{:S(2)}) collective-permute-start(bf16[768,512]{1,0:T(8,128)(2,1)S(1)} %pad_maximum_fusion), channel_id=1, source_target_pairs={{0,8},{1,25},{2,10},{3,27},{4,12},{5,29},{6,14},{7,31},{8,0},{9,17... | collective-permute-start | bytes 2359304 | tf_op jit(solution)/shard_map/ppermute | solution.py:79
  5.0 3.7 %collective-permute-start.4 = (bf16[384,512]{1,0:T(8,128)(2,1)S(1)}, bf16[384,512]{1,0:T(8,128)(2,1)}, u32[]{:S(2)}, u32[]{:S(2)}) collective-permute-start(bf16[384,512]{1,0:T(8,128)(2,1)S(1)} %pad_maximum_fusion.3), channel_id=1, source_target_pairs={{0,1},{1,0},{2,3},{3,2},{4,5},{5,4},{6,7},{7,6},{8,9},{9,8},{10,11... | collective-permute-start | bytes 1179656 | tf_op jit(solution)/shard_map/ppermute | solution.py:78
  8.8 15.0 %collective-permute-start.5 = (bf16[384,512]{1,0:T(8,128)(2,1)}, bf16[384,512]{1,0:T(8,128)(2,1)}, u32[]{:S(2)}, u32[]{:S(2)}) collective-permute-start(bf16[384,512]{1,0:T(8,128)(2,1)} %collective-permute-done.4), channel_id=1, source_target_pairs={{0,8},{1,25},{2,10},{3,27},{4,12},{5,29},{6,14},{7,31},{8,0},{9,17... | collective-permute-start | bytes 1179656 | tf_op jit(solution)/shard_map/ppermute | solution.py:83
  11.9 14.9 %collective-permute-start.1 = (bf16[576,512]{1,0:T(8,128)(2,1)S(1)}, bf16[576,512]{1,0:T(8,128)(2,1)}, u32[]{:S(2)}, u32[]{:S(2)}) collective-permute-start(bf16[576,512]{1,0:T(8,128)(2,1)S(1)} %pad_maximum_fusion.2), channel_id=1, source_target_pairs={{0,24},{1,9},{2,26},{3,11},{4,28},{5,13},{6,30},{7,15},{8,16},{9,1... | collective-permute-start | bytes 1769480 | tf_op jit(solution)/shard_map/ppermute | solution.py:82
  16.1 16.9 %collective-permute-start.2 = (bf16[576,512]{1,0:T(8,128)(2,1)S(1)}, bf16[576,512]{1,0:T(8,128)(2,1)S(1)}, u32[]{:S(2)}, u32[]{:S(2)}) collective-permute-start(bf16[576,512]{1,0:T(8,128)(2,1)S(1)} %slice.90), channel_id=1, source_target_pairs={{0,24},{1,9},{2,26},{3,11},{4,28},{5,13},{6,30},{7,15},{8,16},{9,1... | collective-permute-start | bytes 1769480 | tf_op jit(solution)/shard_map/ppermute | solution.py:85
  19.1 18.1 %collective-permute-start.6 = (bf16[384,512]{1,0:T(8,128)(2,1)}, bf16[384,512]{1,0:T(8,128)(2,1)S(1)}, u32[]{:S(2)}, u32[]{:S(2)}) collective-permute-start(bf16[384,512]{1,0:T(8,128)(2,1)} %collective-permute-done.4), channel_id=1, source_target_pairs={{0,24},{1,9},{2,26},{3,11},{4,28},{5,13},{6,30},{7,15},{8,16},{9,1... | collective-permute-start | bytes 1179656 | tf_op jit(solution)/shard_map/ppermute | solution.py:84
  23.8 17.7 %collective-permute-start.7 = (bf16[384,512]{1,0:T(8,128)(2,1)}, bf16[384,512]{1,0:T(8,128)(2,1)S(1)}, u32[]{:S(2)}, u32[]{:S(2)}) collective-permute-start(bf16[384,512]{1,0:T(8,128)(2,1)} %collective-permute-done.5), channel_id=1, source_target_pairs={{0,24},{1,9},{2,26},{3,11},{4,28},{5,13},{6,30},{7,15},{8,16},{9,1... | collective-permute-start | bytes 1179656 | tf_op jit(solution)/shard_map/ppermute | solution.py:86
  33.2 8.3 %collective-permute-start.3 = (bf16[768,512]{1,0:T(8,128)(2,1)S(1)}, bf16[768,512]{1,0:T(8,128)(2,1)S(1)}, u32[]{:S(2)}, u32[]{:S(2)}) collective-permute-start(bf16[768,512]{1,0:T(8,128)(2,1)S(1)} %pad_maximum_fusion.1), channel_id=1, source_target_pairs={{0,1},{1,0},{2,3},{3,2},{4,5},{5,4},{6,7},{7,6},{8,9},{9,8},{10,11... | collective-permute-start | bytes 2359304 | tf_op jit(solution)/shard_map/ppermute | solution.py:88
  42.2 20.2 %collective-permute-start.9 = (f32[256,512]{1,0:T(8,128)S(1)}, f32[256,512]{1,0:T(8,128)S(1)}, u32[]{:S(2)}, u32[]{:S(2)}) collective-permute-start(f32[256,512]{1,0:T(8,128)S(1)} %fusion.2), channel_id=1, source_target_pairs={{0,2},{1,7},{2,0},{3,5},{4,6},{5,3},{6,4},{7,1},{8,10},{9,15},{10,... | collective-permute-start | bytes 1572872 | tf_op jit(solution)/shard_map/ppermute | solution.py:102
  47.3 26.9 %collective-permute-start.8 = (f32[256,512]{1,0:T(8,128)S(1)}, f32[256,512]{1,0:T(8,128)S(1)}, u32[]{:S(2)}, u32[]{:S(2)}) collective-permute-start(f32[256,512]{1,0:T(8,128)S(1)} %compare_select_fusion), channel_id=1, source_target_pairs={{0,2},{1,7},{2,0},{3,5},{4,6},{5,3},{6,4},{7,1},{8,10},{9,15},{10,... | collective-permute-start | bytes 1572872 | tf_op jit(solution)/shard_map/ppermute | solution.py:103
  50.2 31.0 %copy-start = (f32[1,1,256,512]{3,2,1,0:T(8,128)S(1)}, f32[1,1,256,512]{3,2,1,0:T(8,128)}, u32[]{:S(2)}) copy-start(f32[1,1,256,512]{3,2,1,0:T(8,128)} %param.11) | copy-start | bytes 1572868
  50.2 30.9 %copy-start.1 = (f32[1,1,256,512]{3,2,1,0:T(8,128)S(1)}, f32[1,1,256,512]{3,2,1,0:T(8,128)}, u32[]{:S(2)}) copy-start(f32[1,1,256,512]{3,2,1,0:T(8,128)} %param.10) | copy-start | bytes 1572868
  50.2 30.9 %copy-start.3 = (f32[1,1,256,512]{3,2,1,0:T(8,128)S(1)}, f32[1,1,256,512]{3,2,1,0:T(8,128)}, u32[]{:S(2)}) copy-start(f32[1,1,256,512]{3,2,1,0:T(8,128)} %param.9) | copy-start | bytes 1572868
  62.5 18.7 %collective-permute-start.10 = (f32[256,512]{1,0:T(8,128)S(1)}, f32[256,512]{1,0:T(8,128)S(1)}, u32[]{:S(2)}, u32[]{:S(2)}) collective-permute-start(f32[256,512]{1,0:T(8,128)S(1)} %add.106), channel_id=1, source_target_pairs={{0,6},{1,3},{2,4},{3,1},{4,2},{5,7},{6,0},{7,5},{8,14},{9,11},{10,... | collective-permute-start | bytes 1572872 | tf_op jit(solution)/shard_map/ppermute | solution.py:105
  81.6 29.8 %copy-start.4 = (f32[1,16,512]{2,1,0:T(8,128)S(1)}, f32[1,16,512]{2,1,0:T(8,128)}, u32[]{:S(2)}) copy-start(f32[1,16,512]{2,1,0:T(8,128)} %param.13) | copy-start | bytes 98308
  81.6 29.8 %copy-start.5 = (f32[1,16,512]{2,1,0:T(8,128)S(1)}, f32[1,16,512]{2,1,0:T(8,128)}, u32[]{:S(2)}) copy-start(f32[1,16,512]{2,1,0:T(8,128)} %param.12) | copy-start | bytes 98308
  112.3 19.5 %all-to-all-start.1 = ((f32[16,16,512]{2,1,0:T(8,128)}), f32[16,16,512]{2,1,0:T(8,128)S(1)}, u32[]{:S(2)}, u32[]{:S(2)}) async-start(f32[16,16,512]{2,1,0:T(8,128)} %broadcast_in_dim.18), calls=%async_computation.1 | async-start | bytes 1048576 | tf_op jit(solution)/shard_map/all_to_all | solution.py:142
